TPU v7x, 32 devices: a whole 2x2x4 slice. The times are simulated.
32 devices in a mesh: batch: 4 (over x, core), row: 4 (over z), col: 2 (over y).
Axes of the slice: x: 2, y: 2, z: 4, core: 2. Of those that a mesh axis runs over, the one named last changes fastest.
Arguments:
- image_input: bfloat16 [4, 1024, 1536], P('batch', 'row', 'col'), may hold values from -16 to 16
- text_input: bfloat16 [4, 152, 1536], P('batch', 'row', 'col'), may hold values from -16 to 16
- image_cotan: bfloat16 [4, 1024, 1536], P('batch', 'row', 'col'), may hold values from -6 to 6
- text_cotan: bfloat16 [4, 152, 1536], P('batch', 'row', 'col'), may hold values from -6 to 6
- seq_group: int32 [3], replicated, may hold values from 0 to 3, as said below
- w_attend: bfloat16 [2, 1536, 4608], P(None, 'col', 'row'), may hold values from -0.15625 to 0.15625
- w_output: bfloat16 [2, 1536, 1536], P(None, 'row', 'col'), may hold values from -4 to 4
- w_expand: bfloat16 [2, 1536, 6144], P(None, 'col', 'row'), may hold values from -0.15625 to 0.15625
- w_reduce: bfloat16 [2, 6144, 1536], P(None, 'row', 'col'), may hold values from -0.078125 to 0.078125
- m_attend: float32 [2, 1536, 4608], P(None, ('col', 'batch'), 'row'), may hold values from -9.1552734e-05 to 9.1552734e-05
- m_output: float32 [2, 1536, 1536], P(None, ('row', 'batch'), 'col'), may hold values from -9.1552734e-05 to 9.1552734e-05
- m_expand: float32 [2, 1536, 6144], P(None, ('col', 'batch'), 'row'), may hold values from -9.1552734e-05 to 9.1552734e-05
- m_reduce: float32 [2, 6144, 1536], P(None, ('row', 'batch'), 'col'), may hold values from -9.1552734e-05 to 9.1552734e-05
- v_attend: float32 [2, 1536, 4608], P(None, ('col', 'batch'), 'row'), may hold values from 8.8303176e-12 to 3.532127e-11
- v_output: float32 [2, 1536, 1536], P(None, ('row', 'batch'), 'col'), may hold values from 8.8303177e-13 to 3.532127e-12
- v_expand: float32 [2, 1536, 6144], P(None, ('col', 'batch'), 'row'), may hold values from 8.8303176e-12 to 3.532127e-11
- v_reduce: float32 [2, 6144, 1536], P(None, ('row', 'batch'), 'col'), may hold values from 8.8303176e-12 to 3.532127e-11
Outputs:
- image_output: bfloat16 [4, 1024, 1536], P('batch', 'row', 'col')
- text_output: bfloat16 [4, 152, 1536], P('batch', 'row', 'col')
- image_grad: float32 [4, 1024, 1536], P('batch', 'row', 'col')
- text_grad: float32 [4, 152, 1536], P('batch', 'row', 'col')
- g_attend: float32 [2, 1536, 4608], P(None, ('col', 'batch'), 'row')
- g_output: float32 [2, 1536, 1536], P(None, ('row', 'batch'), 'col')
- g_expand: float32 [2, 1536, 6144], P(None, ('col', 'batch'), 'row')
- g_reduce: float32 [2, 6144, 1536], P(None, ('row', 'batch'), 'col')
- mnew_attend: float32 [2, 1536, 4608], P(None, ('col', 'batch'), 'row')
- mnew_output: float32 [2, 1536, 1536], P(None, ('row', 'batch'), 'col')
- mnew_expand: float32 [2, 1536, 6144], P(None, ('col', 'batch'), 'row')
- mnew_reduce: float32 [2, 6144, 1536], P(None, ('row', 'batch'), 'col')
- vnew_attend: float32 [2, 1536, 4608], P(None, ('col', 'batch'), 'row')
- vnew_output: float32 [2, 1536, 1536], P(None, ('row', 'batch'), 'col')
- vnew_expand: float32 [2, 1536, 6144], P(None, ('col', 'batch'), 'row')
- vnew_reduce: float32 [2, 6144, 1536], P(None, ('row', 'batch'), 'col')
- step_attend: float32 [2, 1536, 4608], P(None, ('col', 'batch'), 'row')
- step_output: float32 [2, 1536, 1536], P(None, ('row', 'batch'), 'col')
- step_expand: float32 [2, 1536, 6144], P(None, ('col', 'batch'), 'row')
- step_reduce: float32 [2, 6144, 1536], P(None, ('row', 'batch'), 'col')
- grad_norm: float32 [], replicated
Inputs may be any that keep to these rules, and one draw needn't show every extreme that they name: `seq_group`: 3 different groups, each holding one sequence; the slots of other groups hold none.
All inputs are finite; a program needn't handle non-finite values.
Results may differ from a plain program's by a relative error of at most 0.013.
Values may be sent and summed in bfloat16 or wider, within the bound.
A program may use at most 256 MiB of HBM per device.

v0:
```python
from functools import partial

import jax
import jax.numpy as jnp
from jax import lax
from jax.sharding import PartitionSpec as P

D = 1536
HD = 64
STEP = 10


EPSILON = 1e-06
BETA_ONE = 0.9
BETA_TWO = 0.999
RATE = 0.02
DECAY = 0.1


def product(operand, another):
    return jnp.dot(operand, another, preferred_element_type=jnp.float32)


def product_t(operand, another):
    return lax.dot_general(
        operand, another, (((0,), (0,)), ((), ())), preferred_element_type=jnp.float32
    )


def product_nt(operand, another):
    return lax.dot_general(
        operand, another, (((1,), (1,)), ((), ())), preferred_element_type=jnp.float32
    )


def rows_in(part_one, part_two):
    return (
        lax.all_gather(part_one, "row", axis=0, tiled=True),
        lax.all_gather(part_two, "row", axis=0, tiled=True),
    )


def cols_in(part_one, part_two):
    return (
        lax.psum_scatter(part_one, "col", scatter_dimension=0, tiled=True),
        lax.psum_scatter(part_two, "col", scatter_dimension=0, tiled=True),
    )


def cols_out(part_one, part_two):
    return (
        lax.all_gather(part_one, "col", axis=0, tiled=True),
        lax.all_gather(part_two, "col", axis=0, tiled=True),
    )


def rows_out(part_one, part_two):
    return (
        lax.psum_scatter(part_one, "row", scatter_dimension=0, tiled=True),
        lax.psum_scatter(part_two, "row", scatter_dimension=0, tiled=True),
    )


def rows_back(part_one, part_two):
    return (
        lax.all_gather(part_one, "row", axis=0, tiled=True),
        lax.all_gather(part_two, "row", axis=0, tiled=True),
    )


def cols_back(part_one, part_two):
    return (
        lax.psum_scatter(part_one, "col", scatter_dimension=0, tiled=True),
        lax.psum_scatter(part_two, "col", scatter_dimension=0, tiled=True),
    )


def cols_grad(part_one, part_two):
    return (
        lax.all_gather(part_one, "col", axis=0, tiled=True),
        lax.all_gather(part_two, "col", axis=0, tiled=True),
    )


def rows_grad(part_one, part_two):
    return (
        lax.psum_scatter(part_one, "row", scatter_dimension=0, tiled=True),
        lax.psum_scatter(part_two, "row", scatter_dimension=0, tiled=True),
    )


def token_sums(part_one, part_two):
    return lax.psum((part_one, part_two), "col")


def batch_sum(part_one, part_two):
    return (
        lax.psum_scatter(part_one, "batch", scatter_dimension=1, tiled=True),
        lax.psum_scatter(part_two, "batch", scatter_dimension=1, tiled=True),
    )


def norm_local(image_x, text_x):
    joined = jnp.concatenate([image_x, text_x], 0)
    sum_one, sum_two = token_sums(jnp.sum(joined, axis=1), jnp.sum(joined * joined, axis=1))
    center = sum_one / D
    inverse = lax.rsqrt(second_moment(sum_two, center) + EPSILON)
    return ((joined - center[:, None]) * inverse[:, None], inverse)


def second_moment(sum_two, center):
    return sum_two / D - center * center


def norm_back(normed, inverse, gradient):
    sum_one, sum_two = token_sums(jnp.sum(gradient, axis=1), jnp.sum(gradient * normed, axis=1))
    return inverse[:, None] * (gradient - sum_one[:, None] / D - normed * (sum_two[:, None] / D))


def adamw(gradient, moment, square, weight, clip_factor):
    clipped = gradient * clip_factor
    moment_new = BETA_ONE * moment + (1.0 - BETA_ONE) * clipped
    square_new = BETA_TWO * square + (1.0 - BETA_TWO) * clipped * clipped
    corrected = (
        moment_new
        / (1.0 - BETA_ONE**STEP)
        / (jnp.sqrt(square_new / (1.0 - BETA_TWO**STEP)) + 1e-08)
    )
    return (moment_new, square_new, -RATE * (corrected + DECAY * weight))


def weight_shard(weight, group_index, shard_rows):
    return lax.dynamic_slice_in_dim(weight, group_index * shard_rows, shard_rows, 1).astype(
        jnp.float32
    )


def on_device(
    image_input,
    text_input,
    image_cotan,
    text_cotan,
    seq_group,
    w_attend,
    w_output,
    w_expand,
    w_reduce,
    m_attend,
    m_output,
    m_expand,
    m_reduce,
    v_attend,
    v_output,
    v_expand,
    v_reduce,
):
    image_x = image_input[0].astype(jnp.float32)
    text_x = text_input[0].astype(jnp.float32)
    image_rows = image_x.shape[0]
    local_heads = w_attend.shape[2] // (3 * HD)
    temper = HD ** (-0.5)
    normed_one, inverse_one = norm_local(image_x, text_x)
    low_one = normed_one.astype(jnp.bfloat16)
    full_image, full_text = rows_in(low_one[:image_rows], low_one[image_rows:])
    proj_image, proj_text = cols_in(
        product(full_image, w_attend[0]), product(full_text, w_attend[1])
    )
    query_rows = proj_image.shape[0]
    projected = (
        jnp.concatenate([proj_image, proj_text], 0)
        .astype(jnp.bfloat16)
        .reshape(-1, local_heads, 3, HD)
    )
    queries = projected[:, :, 0]
    key_image, key_text = (
        lax.all_gather(projected[:query_rows, :, 1:], "col", axis=0, tiled=True),
        lax.all_gather(projected[query_rows:, :, 1:], "col", axis=0, tiled=True),
    )
    key_rows = key_image.shape[0]
    keyval = jnp.concatenate([key_image, key_text], 0)
    keys_all = keyval[:, :, 0]
    values_all = keyval[:, :, 1]
    scores = (
        jnp.einsum("qhd,khd->hqk", queries, keys_all, preferred_element_type=jnp.float32) * temper
    )
    peak = jnp.max(scores, axis=2, keepdims=True)
    shifted = jnp.exp(scores - peak)
    totals = jnp.sum(shifted, axis=2, keepdims=True)
    soft_probs = (shifted / totals).astype(jnp.bfloat16)
    log_total = peak + jnp.log(totals)
    attended = jnp.einsum(
        "hqk,khd->qhd", soft_probs, values_all, preferred_element_type=jnp.float32
    )
    att_low = attended.astype(jnp.bfloat16).reshape(attended.shape[0], -1)
    gath_image, gath_text = cols_out(att_low[:query_rows], att_low[query_rows:])
    branch_image, branch_text = rows_out(
        product(gath_image, w_output[0]), product(gath_text, w_output[1])
    )
    middle = jnp.concatenate([image_x, text_x], 0) + jnp.concatenate([branch_image, branch_text], 0)
    normed_two, inverse_two = norm_local(middle[:image_rows], middle[image_rows:])
    low_two = normed_two.astype(jnp.bfloat16)
    full2_image, full2_text = rows_in(low_two[:image_rows], low_two[image_rows:])
    hidden_image, hidden_text = cols_in(
        product(full2_image, w_expand[0]), product(full2_text, w_expand[1])
    )
    hidden = jnp.concatenate([hidden_image, hidden_text], 0)
    activated = jax.nn.gelu(hidden, approximate=True).astype(jnp.bfloat16)
    act_image, act_text = cols_out(activated[:query_rows], activated[query_rows:])
    down_image, down_text = rows_out(
        product(act_image, w_reduce[0]), product(act_text, w_reduce[1])
    )
    result_rows = middle + jnp.concatenate([down_image, down_text], 0)
    image_output = result_rows[:image_rows].astype(jnp.bfloat16)[None]
    text_output = result_rows[image_rows:].astype(jnp.bfloat16)[None]
    group_index = lax.axis_index("batch")
    present = jnp.any(seq_group == group_index).astype(jnp.float32)
    grad_out = jnp.concatenate([image_cotan[0], text_cotan[0]], 0).astype(jnp.float32) * present
    low_out = grad_out.astype(jnp.bfloat16)
    dz_image, dz_text = rows_back(low_out[:image_rows], low_out[image_rows:])
    g_red = jnp.stack([product_t(act_image, dz_image), product_t(act_text, dz_text)])
    dact_image, dact_text = cols_back(
        product_nt(dz_image, w_reduce[0]), product_nt(dz_text, w_reduce[1])
    )
    gelu_pull = jax.vjp(partial(jax.nn.gelu, approximate=True), hidden)[1]
    dhidden = gelu_pull(jnp.concatenate([dact_image, dact_text], 0))[0].astype(jnp.bfloat16)
    dh_image, dh_text = cols_grad(dhidden[:query_rows], dhidden[query_rows:])
    g_exp = jnp.stack([product_t(full2_image, dh_image), product_t(full2_text, dh_text)])
    dn_image, dn_text = rows_grad(
        product_nt(dh_image, w_expand[0]), product_nt(dh_text, w_expand[1])
    )
    grad_mid = grad_out + norm_back(
        normed_two, inverse_two, jnp.concatenate([dn_image, dn_text], 0)
    )
    mlp_total = None
    low_mid = grad_mid.astype(jnp.bfloat16)
    dy_image, dy_text = rows_back(low_mid[:image_rows], low_mid[image_rows:])
    g_out = jnp.stack([product_t(gath_image, dy_image), product_t(gath_text, dy_text)])
    datt_image, datt_text = cols_back(
        product_nt(dy_image, w_output[0]), product_nt(dy_text, w_output[1])
    )
    dattend = (
        jnp.concatenate([datt_image, datt_text], 0)
        .astype(jnp.bfloat16)
        .reshape(-1, local_heads, HD)
    )
    scores_again = (
        jnp.einsum("qhd,khd->hqk", queries, keys_all, preferred_element_type=jnp.float32) * temper
    )
    soft_again = jnp.exp(scores_again - log_total)
    dprobs = jnp.einsum("qhd,khd->hqk", dattend, values_all, preferred_element_type=jnp.float32)
    row_dot = jnp.sum(soft_again * dprobs, axis=2, keepdims=True)
    dscores = (soft_again * (dprobs - row_dot)).astype(jnp.bfloat16)
    dquery = (
        jnp.einsum("hqk,khd->qhd", dscores, keys_all, preferred_element_type=jnp.float32) * temper
    )
    dkey = jnp.einsum("hqk,qhd->khd", dscores, queries, preferred_element_type=jnp.float32) * temper
    dvalue = jnp.einsum(
        "hqk,qhd->khd", soft_again.astype(jnp.bfloat16), dattend, preferred_element_type=jnp.float32
    )
    dkey_value = jnp.stack([dkey, dvalue], axis=2)
    dkv_image, dkv_text = (
        lax.psum_scatter(dkey_value[:key_rows], "col", scatter_dimension=0, tiled=True),
        lax.psum_scatter(dkey_value[key_rows:], "col", scatter_dimension=0, tiled=True),
    )
    dkv_local = jnp.concatenate([dkv_image, dkv_text], 0)
    dproject = (
        jnp.concatenate([dquery[:, :, None], dkv_local], axis=2)
        .astype(jnp.bfloat16)
        .reshape(dquery.shape[0], -1)
    )
    dp_image, dp_text = cols_grad(dproject[:query_rows], dproject[query_rows:])
    g_att = jnp.stack([product_t(full_image, dp_image), product_t(full_text, dp_text)])
    da_image, da_text = rows_grad(
        product_nt(dp_image, w_attend[0]), product_nt(dp_text, w_attend[1])
    )
    grad_in = grad_mid + norm_back(normed_one, inverse_one, jnp.concatenate([da_image, da_text], 0))
    image_grad = grad_in[:image_rows][None]
    text_grad = grad_in[image_rows:][None]
    mlp_total = batch_sum(g_exp, g_red)
    sum_exp, sum_red = mlp_total
    sum_att, sum_out = batch_sum(g_att, g_out)
    local_squares = (
        jnp.sum(sum_att * sum_att)
        + jnp.sum(sum_out * sum_out)
        + jnp.sum(sum_exp * sum_exp)
        + jnp.sum(sum_red * sum_red)
    )
    grad_norm = jnp.sqrt(lax.psum(local_squares, ("batch", "row", "col")))
    clip_factor = jnp.minimum(1.0, 1.0 / (grad_norm + 1e-06))
    attend_new = adamw(
        sum_att,
        m_attend,
        v_attend,
        weight_shard(w_attend, group_index, sum_att.shape[1]),
        clip_factor,
    )
    output_new = adamw(
        sum_out,
        m_output,
        v_output,
        weight_shard(w_output, group_index, sum_out.shape[1]),
        clip_factor,
    )
    expand_new = adamw(
        sum_exp,
        m_expand,
        v_expand,
        weight_shard(w_expand, group_index, sum_exp.shape[1]),
        clip_factor,
    )
    reduce_new = adamw(
        sum_red,
        m_reduce,
        v_reduce,
        weight_shard(w_reduce, group_index, sum_red.shape[1]),
        clip_factor,
    )
    return (
        image_output,
        text_output,
        image_grad,
        text_grad,
        sum_att,
        sum_out,
        sum_exp,
        sum_red,
        attend_new[0],
        output_new[0],
        expand_new[0],
        reduce_new[0],
        attend_new[1],
        output_new[1],
        expand_new[1],
        reduce_new[1],
        attend_new[2],
        output_new[2],
        expand_new[2],
        reduce_new[2],
        grad_norm,
    )


def solution(mesh):
    return jax.shard_map(
        on_device,
        mesh=mesh,
        in_specs=(
            P("batch", "row", "col"),
            P("batch", "row", "col"),
            P("batch", "row", "col"),
            P("batch", "row", "col"),
            P(),
            P(None, "col", "row"),
            P(None, "row", "col"),
            P(None, "col", "row"),
            P(None, "row", "col"),
            P(None, ("col", "batch"), "row"),
            P(None, ("row", "batch"), "col"),
            P(None, ("col", "batch"), "row"),
            P(None, ("row", "batch"), "col"),
            P(None, ("col", "batch"), "row"),
            P(None, ("row", "batch"), "col"),
            P(None, ("col", "batch"), "row"),
            P(None, ("row", "batch"), "col"),
        ),
        out_specs=(
            P("batch", "row", "col"),
            P("batch", "row", "col"),
            P("batch", "row", "col"),
            P("batch", "row", "col"),
            P(None, ("col", "batch"), "row"),
            P(None, ("row", "batch"), "col"),
            P(None, ("col", "batch"), "row"),
            P(None, ("row", "batch"), "col"),
            P(None, ("col", "batch"), "row"),
            P(None, ("row", "batch"), "col"),
            P(None, ("col", "batch"), "row"),
            P(None, ("row", "batch"), "col"),
            P(None, ("col", "batch"), "row"),
            P(None, ("row", "batch"), "col"),
            P(None, ("col", "batch"), "row"),
            P(None, ("row", "batch"), "col"),
            P(None, ("col", "batch"), "row"),
            P(None, ("row", "batch"), "col"),
            P(None, ("col", "batch"), "row"),
            P(None, ("row", "batch"), "col"),
            P(),
        ),
        check_vma=False,
    )
```

profile of v0, /device:TPU:0, one launch (start us, length us, event | category | flops | bytes accessed | tf_op | source)
XLA Modules:
  0.0 1409.4 jit_solution(10495120752505049246)
XLA Ops:
  8.5 5.9 all-reduce.20
  16.6 39.0 %all-gather.17.cloned.1.call-done = bf16[1024,768]{1,0:T(8,128)(2,1)} async-done(((bf16[256,768]{1,0:T(8,128)(2,1)}), bf16[1024,768]{1,0:T(8,128)(2,1)}) %all-gather.17.cloned.1.call-update) | async-done | bytes 1572880 | tf_op jit(solution)/shard_map/all_gather | solution.py:38
  55.5 6.3 fusion.59
  62.0 59.0 %reduce-scatter.31.cloned.1.call-done = f32[512,1152]{1,0:T(8,128)} async-done(((f32[1024,1152]{1,0:T(8,128)}), f32[512,1152]{1,0:T(8,128)}) %reduce-scatter.31.cloned.1.call-update) | async-done | bytes 2359312 | tf_op jit(solution)/shard_map/reduce_scatter | solution.py:45
  125.5 13.9 all-gather
  141.5 18.2 %fusion = f32[80,1152]{1,0:T(8,128)S(1)} fusion(f32[152,1152]{1,0:T(8,128)S(1)} %fusion.55), kind=kCustom, calls=%all-reduce-scatter | all-reduce-scatter fusion | flops 184321 | bytes 1069568
  164.2 7.3 all_gather.57
  172.0 10.4 fusion.120
  182.4 8.7 fusion.8
  191.1 8.1 fusion.68
  200.1 9.0 all_gather.58
  220.2 24.3 %fusion.1 = f32[40,768]{1,0:T(8,128)S(1)} fusion(f32[152,768]{1,0:T(8,128)S(1)} %fusion.87), kind=kCustom, calls=%all-reduce-scatter.1 | all-reduce-scatter fusion | flops 122881 | bytes 590336
  248.0 33.2 %reduce-scatter.33.cloned.1.call-done = f32[256,768]{1,0:T(8,128)} async-done(((f32[1024,768]{1,0:T(8,128)}), f32[256,768]{1,0:T(8,128)}) %reduce-scatter.33.cloned.1.call-update) | async-done | bytes 786448 | tf_op jit(solution)/shard_map/reduce_scatter | solution.py:59
  289.1 31.7 %all-gather.25.cloned.1.call-done = bf16[1024,768]{1,0:T(8,128)(2,1)} async-done(((bf16[256,768]{1,0:T(8,128)(2,1)}), bf16[1024,768]{1,0:T(8,128)(2,1)}) %all-gather.25.cloned.1.call-update) | async-done | bytes 1572880 | tf_op jit(solution)/shard_map/all_gather | solution.py:66
  320.9 7.4 fusion.32
  328.4 30.6 %all-gather.21.cloned.1.call-done = bf16[1024,768]{1,0:T(8,128)(2,1)} async-done(((bf16[256,768]{1,0:T(8,128)(2,1)}), bf16[1024,768]{1,0:T(8,128)(2,1)}) %all-gather.21.cloned.1.call-update) | async-done | bytes 1572880 | tf_op jit(solution)/shard_map/all_gather | solution.py:38
  358.9 7.4 fusion.42
  367.3 14.3 %all-gather.4 = bf16[4,38,768]{2,1,0:T(8,128)(2,1)S(1)} all-gather(bf16[1,38,768]{2,1,0:T(8,128)(2,1)S(1)} %slice_bitcast_fusion.6), channel_id=1, replica_groups=mesh['batch'=4,'row'=4,'col'=2] {'row'}, dimensions={0}, use_global_device_ids=true | all-gather | bytes 291840 | tf_op jit(solution)/shard_map/all_gather | solution.py:67
  384.3 13.8 all-gather.2
  401.1 46.1 %fusion.113 = (f32[80,1536]{1,0:T(8,128)}, f32[80,1536]{1,0:T(8,128)}) fusion(f32[152,1536]{1,0:T(8,128)S(1)} %fusion.38, f32[152,1536]{1,0:T(8,128)S(1)} %fusion.28), kind=kCustom, calls=%all-reduce-scatter.9 | all-reduce-scatter fusion | flops 491521 | bytes 2851328
  459.4 79.4 %reduce-scatter.35.cloned.1.call-done = f32[512,1536]{1,0:T(8,128)} async-done(((f32[1024,1536]{1,0:T(8,128)}), f32[512,1536]{1,0:T(8,128)}) %reduce-scatter.35.cloned.1.call-update) | async-done | bytes 3145744 | tf_op jit(solution)/shard_map/reduce_scatter | solution.py:45
  545.7 45.0 %all-gather.27.cloned.1.call-done = bf16[1024,1536]{1,0:T(8,128)(2,1)} async-done(((bf16[512,1536]{1,0:T(8,128)(2,1)}), bf16[1024,1536]{1,0:T(8,128)(2,1)}) %all-gather.27.cloned.1.call-update) | async-done | bytes 3145744 | tf_op jit(solution)/shard_map/all_gather | solution.py:80
  590.8 7.0 fusion.40
  597.9 8.4 all-gather.5
  609.1 25.1 %fusion.5 = f32[40,768]{1,0:T(8,128)S(1)} fusion(f32[152,768]{1,0:T(8,128)S(1)} %fusion.36), kind=kCustom, calls=%all-reduce-scatter.5 | all-reduce-scatter fusion | flops 122881 | bytes 590336
  639.1 26.9 %reduce-scatter.41.cloned.1.call-done = f32[256,768]{1,0:T(8,128)} async-done(((f32[1024,768]{1,0:T(8,128)}), f32[256,768]{1,0:T(8,128)}) %reduce-scatter.41.cloned.1.call-update) | async-done | bytes 786448 | tf_op jit(solution)/shard_map/reduce_scatter | solution.py:87
  676.6 37.6 %all-gather.29.cloned.1.call-done = bf16[1024,768]{1,0:T(8,128)(2,1)} async-done(((bf16[256,768]{1,0:T(8,128)(2,1)}), bf16[1024,768]{1,0:T(8,128)(2,1)}) %all-gather.29.cloned.1.call-update) | async-done | bytes 1572880 | tf_op jit(solution)/shard_map/all_gather | solution.py:66
  718.7 14.4 %all-gather.6 = bf16[4,38,768]{2,1,0:T(8,128)(2,1)S(1)} all-gather(bf16[1,38,768]{2,1,0:T(8,128)(2,1)S(1)} %slice_bitcast_fusion.5), channel_id=1, replica_groups=mesh['batch'=4,'row'=4,'col'=2] {'row'}, dimensions={0}, use_global_device_ids=true | all-gather | bytes 291840 | tf_op jit(solution)/shard_map/all_gather | solution.py:67
  733.4 10.5 fusion.6
  751.1 9.3 fusion.23
  760.4 11.6 multiply_reduce_fusion
  772.0 12.9 multiply_convert_fusion
  797.1 41.7 %all-reduce.24 = bf16[152,6,2,64]{0,3,1,2:T(8,128)(2,1)} all-reduce(f32[152,6,2,64]{0,3,1,2:T(8,128)} %pad_maximum_fusion.9), channel_id=17, replica_groups=mesh['batch'=4,'row'=4,'col'=2] {'col'}, use_global_device_ids=true, to_apply=%region_31.0.clone | all-reduce | flops 116736 | bytes 700416
  839.9 6.3 fusion.67
  859.6 38.4 %all-gather.23.cloned.1.call-done = bf16[1024,1536]{1,0:T(8,128)(2,1)} async-done(((bf16[512,1536]{1,0:T(8,128)(2,1)}), bf16[1024,1536]{1,0:T(8,128)(2,1)}) %all-gather.23.cloned.1.call-update) | async-done | bytes 3145744 | tf_op jit(solution)/shard_map/all_gather | solution.py:52
  898.1 6.9 fusion.34
  917.1 14.3 %all-gather.3 = bf16[2,76,1536]{2,1,0:T(8,128)(2,1)S(1)} all-gather(bf16[1,76,1536]{2,1,0:T(8,128)(2,1)S(1)} %slice_bitcast_fusion.3), channel_id=1, replica_groups=mesh['batch'=4,'row'=4,'col'=2] {'col'}, dimensions={0}, use_global_device_ids=true | all-gather | bytes 700416 | tf_op jit(solution)/shard_map/all_gather | solution.py:53
  941.5 6.1 fusion.57
  949.0 7.0 all-gather.7
  968.3 24.9 %fusion.112 = (f32[40,768]{1,0:T(8,128)S(1)}, f32[40,768]{1,0:T(8,128)S(1)}) fusion(f32[152,768]{1,0:T(8,128)S(1)} %fusion.30, f32[152,768]{1,0:T(8,128)S(1)} %fusion.53), kind=kCustom, calls=%all-reduce-scatter.8 | all-reduce-scatter fusion | flops 245761 | bytes 1180160
  1001.8 40.1 %reduce-scatter.37.cloned.1.call-done = f32[256,768]{1,0:T(8,128)} async-done(((f32[1024,768]{1,0:T(8,128)}), f32[256,768]{1,0:T(8,128)}) %reduce-scatter.37.cloned.1.call-update) | async-done | bytes 786448 | tf_op jit(solution)/shard_map/reduce_scatter | solution.py:59
  1044.5 79.9 %reduce-scatter.53.cloned.1.call-done = f32[2,192,1536]{2,1,0:T(8,128)} async-done(((f32[2,768,1536]{2,1,0:T(8,128)}), f32[2,192,1536]{2,1,0:T(8,128)}) %reduce-scatter.53.cloned.1.call-update) | async-done | bytes 2359312 | tf_op jit(solution)/shard_map/reduce_scatter | solution.py:98
  1127.3 78.8 %reduce-scatter.55.cloned.1.call-done = f32[2,384,768]{2,1,0:T(8,128)} async-done(((f32[2,1536,768]{2,1,0:T(8,128)}), f32[2,384,768]{2,1,0:T(8,128)}) %reduce-scatter.55.cloned.1.call-update) | async-done | bytes 2359312 | tf_op jit(solution)/shard_map/reduce_scatter | solution.py:99
  1208.9 59.6 %reduce-scatter.47.cloned.1.call-done = f32[256,768]{1,0:T(8,128)} async-done(((f32[1024,768]{1,0:T(8,128)}), f32[256,768]{1,0:T(8,128)}) %reduce-scatter.47.cloned.1.call-update) | async-done | bytes 786448 | tf_op jit(solution)/shard_map/reduce_scatter | solution.py:87
  1277.4 57.9 %reduce-scatter.49.cloned.1.call-done = f32[2,192,1152]{2,1,0:T(8,128)} async-done(((f32[2,768,1152]{2,1,0:T(8,128)}), f32[2,192,1152]{2,1,0:T(8,128)}) %reduce-scatter.49.cloned.1.call-update) | async-done | bytes 1769488 | tf_op jit(solution)/shard_map/reduce_scatter | solution.py:98
  1341.4 39.5 %psum.71 = f32[]{:T(128)} all-reduce(f32[]{:T(128)S(6)} %add.190), channel_id=1, replica_groups=mesh['batch'=4,'row'=4,'col'=2] {'batch','row','col'}, use_global_device_ids=true, to_apply=%region_46.0 | all-reduce | flops 1 | bytes 8 | tf_op jit(solution)/shard_map/psum | solution.py:288
  1381.6 5.8 add_multiply_fusion.2
  1387.5 5.7 add_multiply_fusion.1
  (325 shorter events, 191.3 us)
Async XLA Ops:
  7.2 48.4 %all-gather.17.cloned.1.call-start = ((), (), s32[]{:S(2)}) async-start(), calls=%async_computation.13 | async-start | bytes 1966080 | tf_op jit(solution)/shard_map/all_gather | solution.py:38
  14.4 47.5 %copy-start.56 = (f32[294]{0:T(512)}, f32[294]{0:T(512)S(1)}, u32[]{:S(2)}) copy-start(f32[294]{0:T(512)S(1)} %get-tuple-element.127) | copy-start | bytes 3532
  14.4 47.5 %copy-start.58 = (f32[294]{0:T(512)}, f32[294]{0:T(512)S(1)}, u32[]{:S(2)}) copy-start(f32[294]{0:T(512)S(1)} %get-tuple-element.128) | copy-start | bytes 3532
  15.7 46.2 %copy-start.39 = (bf16[294,768]{1,0:T(8,128)(2,1)}, bf16[294,768]{1,0:T(8,128)(2,1)S(1)}, u32[]{:S(2)}) copy-start(bf16[294,768]{1,0:T(8,128)(2,1)S(1)} %fusion.75) | copy-start | bytes 1354756
  16.5 104.4 %reduce-scatter.31.cloned.1.call-start = ((), (), s32[]{:S(2)}) async-start(), calls=%async_computation.14 | async-start | bytes 7077888 | tf_op jit(solution)/shard_map/reduce_scatter | solution.py:45
  61.9 110.1 %all-gather.19.cloned.1.call-start = ((), (), s32[]{:S(2)}) async-start(), calls=%async_computation.15 | async-start | bytes 2359296 | tf_op jit(solution)/shard_map/all_gather | solution.py:176
  123.3 48.7 %copy-start.2 = (bf16[512,1152]{0,1:T(8,128)(2,1)}, bf16[512,1152]{0,1:T(8,128)(2,1)S(1)}, u32[]{:S(2)}) copy-start(bf16[512,1152]{0,1:T(8,128)(2,1)S(1)} %copy.58) | copy-start | bytes 3538948
  124.6 37.4 %copy-start.60 = (u32[32]{0:T(128)S(1)}, u32[32]{0:T(128)}, u32[]{:S(2)}) copy-start(u32[32]{0:T(128)} %constant.25) | copy-start | bytes 388
  124.6 156.7 %reduce-scatter.33.cloned.1.call-start = ((), (), s32[]{:S(2)}) async-start(), calls=%async_computation.16 | async-start | bytes 3932160 | tf_op jit(solution)/shard_map/reduce_scatter | solution.py:59
  159.7 3.6 collective-permute-start
  211.9 33.9 %copy-start.61 = (u32[32]{0:T(128)S(1)}, u32[32]{0:T(128)}, u32[]{:S(2)}) copy-start(u32[32]{0:T(128)} %constant.112) | copy-start | bytes 388
  211.9 108.9 %all-gather.25.cloned.1.call-start = ((), (), s32[]{:S(2)}) async-start(), calls=%async_computation.21 | async-start | bytes 1966080 | tf_op jit(solution)/shard_map/all_gather | solution.py:66
  213.9 67.3 %copy-start.7 = (bf16[1,256,768]{2,1,0:T(8,128)(2,1)S(1)}, bf16[1,256,768]{2,1,0:T(8,128)(2,1)}, u32[]{:S(2)}) copy-start(bf16[1,256,768]{2,1,0:T(8,128)(2,1)} %param.17) | copy-start | bytes 1179652
  214.0 67.3 %copy-start.45 = (bf16[1,38,768]{2,1,0:T(8,128)(2,1)S(1)}, bf16[1,38,768]{2,1,0:T(8,128)(2,1)}, u32[]{:S(2)}) copy-start(bf16[1,38,768]{2,1,0:T(8,128)(2,1)} %param.18) | copy-start | bytes 175108
  214.8 144.2 %all-gather.21.cloned.1.call-start = ((), (), s32[]{:S(2)}) async-start(), calls=%async_computation.17 | async-start | bytes 1966080 | tf_op jit(solution)/shard_map/all_gather | solution.py:38
  219.9 67.9 %copy-start.48 = (bf16[152,384]{1,0:T(8,128)(2,1)}, bf16[152,384]{1,0:T(8,128)(2,1)S(1)}, u32[]{:S(2)}) copy-start(bf16[152,384]{1,0:T(8,128)(2,1)S(1)} %reshape.88) | copy-start | bytes 350212
  244.5 3.3 collective-permute-start.1
  288.6 170.8 %reduce-scatter.39.cloned.1.call-start = ((), (), s32[]{:S(2)}) async-start(), calls=%async_computation.22 | async-start | bytes 9437184 | tf_op jit(solution)/shard_map/reduce_scatter | solution.py:73
  328.3 210.5 %reduce-scatter.35.cloned.1.call-start = ((), (), s32[]{:S(2)}) async-start(), calls=%async_computation.18 | async-start | bytes 9437184 | tf_op jit(solution)/shard_map/reduce_scatter | solution.py:45
  366.4 224.4 %all-gather.27.cloned.1.call-start = ((), (), s32[]{:S(2)}) async-start(), calls=%async_computation.23 | async-start | bytes 4718592 | tf_op jit(solution)/shard_map/all_gather | solution.py:80
  448.0 5.7 collective-permute-start.4
  452.4 3.3 collective-permute-start.2
  545.7 120.3 %reduce-scatter.41.cloned.1.call-start = ((), (), s32[]{:S(2)}) async-start(), calls=%async_computation.24 | async-start | bytes 3932160 | tf_op jit(solution)/shard_map/reduce_scatter | solution.py:87
  597.8 116.4 %all-gather.29.cloned.1.call-start = ((), (), s32[]{:S(2)}) async-start(), calls=%async_computation.25 | async-start | bytes 1966080 | tf_op jit(solution)/shard_map/all_gather | solution.py:66
  606.4 32.8 %copy-start.34 = (bf16[152,1536]{1,0:T(8,128)(2,1)}, bf16[152,1536]{1,0:T(8,128)(2,1)S(1)}, u32[]{:S(2)}) copy-start(bf16[152,1536]{1,0:T(8,128)(2,1)S(1)} %reshape.96) | copy-start | bytes 1400836
  634.2 4.7 collective-permute-start.5
  639.1 33.4 %copy-start.47 = (f32[38,768]{1,0:T(8,128)}, f32[38,768]{1,0:T(8,128)S(1)}, u32[]{:S(2)}) copy-start(f32[38,768]{1,0:T(8,128)S(1)} %constant_dynamic-slice_fusion.2) | copy-start | bytes 350212
  672.5 41.7 %copy-start.14 = (bf16[2,384,768]{2,1,0:T(8,128)(2,1)S(1)}, bf16[2,384,768]{2,1,0:T(8,128)(2,1)}, u32[]{:S(2)}) copy-start(bf16[2,384,768]{2,1,0:T(8,128)(2,1)} %param.23) | copy-start | bytes 3538948
  676.5 72.4 %reduce-scatter.43.cloned.1.call-start = ((), (), s32[]{:S(2)}) async-start(), calls=%async_computation.26 | async-start | bytes 2359296 | tf_op jit(solution)/shard_map/reduce_scatter | solution.py:73
  717.7 29.0 %copy-start.55 = (f32[6,588]{1,0:T(8,128)S(1)}, f32[6,588]{1,0:T(8,128)}, u32[]{:S(2)}) copy-start(f32[6,588]{1,0:T(8,128)} %copy-done.54) | copy-start | bytes 42340
  717.8 133.2 %reduce-scatter.45.cloned.1.call-start = ((), (), s32[]{:S(2)}) async-start(), calls=%async_computation.27 | async-start | bytes 4718592 | tf_op jit(solution)/shard_map/reduce_scatter | solution.py:262
  743.9 3.9 collective-permute-start.6
  791.7 106.4 %all-gather.23.cloned.1.call-start = ((), (), s32[]{:S(2)}) async-start(), calls=%async_computation.19 | async-start | bytes 4718592 | tf_op jit(solution)/shard_map/all_gather | solution.py:52
  794.4 147.1 %all-gather.31.cloned.1.call-start = ((), (), s32[]{:S(2)}) async-start(), calls=%async_computation.28 | async-start | bytes 3538944 | tf_op jit(solution)/shard_map/all_gather | solution.py:80
  797.1 42.8 %copy-start.6 = (bf16[1024,6,2,64]{0,3,1,2:T(8,128)(2,1)S(1)}, bf16[1024,6,2,64]{0,3,1,2:T(8,128)(2,1)}, u32[]{:S(2)}) copy-start(bf16[1024,6,2,64]{0,3,1,2:T(8,128)(2,1)} %all-gather.19.cloned.1.call-done) | copy-start | bytes 4718596
  854.0 145.6 %reduce-scatter.51.cloned.1.call-start = ((), (), s32[]{:S(2)}) async-start(), calls=%async_computation.31 | async-start | bytes 2949120 | tf_op jit(solution)/shard_map/reduce_scatter | solution.py:99
  859.4 182.5 %reduce-scatter.37.cloned.1.call-start = ((), (), s32[]{:S(2)}) async-start(), calls=%async_computation.20 | async-start | bytes 3932160 | tf_op jit(solution)/shard_map/reduce_scatter | solution.py:59
  905.0 219.4 %reduce-scatter.53.cloned.1.call-start = ((), (), s32[]{:S(2)}) async-start(), calls=%async_computation.32 | async-start | bytes 11796480 | tf_op jit(solution)/shard_map/reduce_scatter | solution.py:98
  916.1 290.0 %reduce-scatter.55.cloned.1.call-start = ((), (), s32[]{:S(2)}) async-start(), calls=%async_computation.33 | async-start | bytes 11796480 | tf_op jit(solution)/shard_map/reduce_scatter | solution.py:99
  940.9 327.6 %reduce-scatter.47.cloned.1.call-start = ((), (), s32[]{:S(2)}) async-start(), calls=%async_computation.29 | async-start | bytes 3932160 | tf_op jit(solution)/shard_map/reduce_scatter | solution.py:87
  947.6 387.7 %reduce-scatter.49.cloned.1.call-start = ((), (), s32[]{:S(2)}) async-start(), calls=%async_computation.30 | async-start | bytes 8847360 | tf_op jit(solution)/shard_map/reduce_scatter | solution.py:98
  993.3 8.2 collective-permute-start.7
  997.6 4.0 collective-permute-start.3
  1044.5 224.0 %copy-start.46 = (bf16[1,38,768]{2,1,0:T(8,128)(2,1)S(1)}, bf16[1,38,768]{2,1,0:T(8,128)(2,1)}, u32[]{:S(2)}) copy-start(bf16[1,38,768]{2,1,0:T(8,128)(2,1)} %param.18) | copy-start | bytes 175108
  1044.5 224.0 %copy-start.57 = (f32[294]{0:T(512)S(1)}, f32[294]{0:T(512)}, u32[]{:S(2)}) copy-start(f32[294]{0:T(512)} %copy-done.56) | copy-start | bytes 3532
  1044.5 224.0 %copy-start.59 = (f32[294]{0:T(512)S(1)}, f32[294]{0:T(512)}, u32[]{:S(2)}) copy-start(f32[294]{0:T(512)} %copy-done.58) | copy-start | bytes 3532
  1127.3 147.7 %copy-start.19 = (f32[294,768]{1,0:T(8,128)S(1)}, f32[294,768]{1,0:T(8,128)}, u32[]{:S(2)}) copy-start(f32[294,768]{1,0:T(8,128)} %get-tuple-element.121) | copy-start | bytes 2709508
  1335.4 46.2 %copy-start.10 = (f32[2,192,1152]{2,1,0:T(8,128)S(1)}, f32[2,192,1152]{2,1,0:T(8,128)}, u32[]{:S(2)}) copy-start(f32[2,192,1152]{2,1,0:T(8,128)} %reduce-scatter.49.cloned.1.call-done) | copy-start | bytes 5308420
  (49 other events, 302.6 us)
Sparse Core Ops, SparseCore 0:
  16.6 38.8 all-gather.16
  62.0 58.8 reduce-scatter.30
  124.7 34.0 all-gather.18
  212.0 69.1 reduce-scatter.32
  283.3 37.4 all-gather.24
  322.9 35.9 all-gather.20
  361.3 96.9 reduce-scatter.38
  460.6 78.1 reduce-scatter.34
  545.8 44.9 all-gather.26
  597.9 68.0 reduce-scatter.40
  676.6 37.4 all-gather.28
  717.9 27.5 reduce-scatter.42
  791.8 59.1 reduce-scatter.44
  853.1 44.9 all-gather.22
  900.1 41.3 all-gather.30
  945.2 33.0 reduce-scatter.50
  980.4 61.4 reduce-scatter.36
  1044.9 79.4 reduce-scatter.52
  1127.6 78.4 reduce-scatter.54
  1208.2 60.2 reduce-scatter.46
  1271.6 63.6 reduce-scatter.48
where the time goes:
time: 1420 us; the launch traced here: 1410 us
  waiting for transfers between devices  746 us (53%)
  blocking collectives  358 us (25%)
  matrix products  123 us (9%)
  other arithmetic  92.2 us (6%)
  local copies, waits for them, and re-layouts  44.6 us (3%)
  between operations  22.8 us (2%)
  starting transfers between devices  22.1 us (2%)
    unnamed x7, blocking collectives  191 us
    reduce_scatter x2, waiting for transfers between devices, cols_in(): lax.psum_scatter(part_one, 'col', scatter_dimension=0, tiled=True)  138 us
    reduce_scatter x2, waiting for transfers between devices, batch_sum(): lax.psum_scatter(part_one, 'batch', scatter_dimension=1, tiled=True)  138 us
    reduce_scatter x2, waiting for transfers between devices, rows_grad(): lax.psum_scatter(part_one, 'row', scatter_dimension=0, tiled=True)  86.5 us
    reduce_scatter x2, waiting for transfers between devices, batch_sum(): lax.psum_scatter(part_two, 'batch', scatter_dimension=1, tiled=True)  78.8 us
    reduce_scatter x2, waiting for transfers between devices, rows_out(): lax.psum_scatter(part_one, 'row', scatter_dimension=0, tiled=True)  73.3 us
    all_gather x2, waiting for transfers between devices, rows_in(): lax.all_gather(part_one, 'row', axis=0, tiled=True)  69.5 us
    all_gather x2, waiting for transfers between devices, rows_back(): lax.all_gather(part_one, 'row', axis=0, tiled=True)  69.3 us
  transfers between devices with their start and end apart: 29, of which 21 were waited for; matrix products, arithmetic and copies ran while one was open for 19% of the time, Pallas kernels for 0%

commit v1 on v0

v1 whole, which is shorter than its diff:
```python
from functools import partial

import jax
import jax.numpy as jnp
from jax import lax
from jax.sharding import PartitionSpec as P

D = 1536
HD = 64
STEP = 10

EPSILON = 1e-06
BETA_ONE = 0.9
BETA_TWO = 0.999
RATE = 0.02
DECAY = 0.1

BF = jnp.bfloat16
F32 = jnp.float32


def dot(a, b):
    return lax.dot_general(a, b, (((a.ndim - 1,), (0,)), ((), ())), preferred_element_type=F32)


def dot_nt(a, b):
    return lax.dot_general(a, b, (((a.ndim - 1,), (1,)), ((), ())), preferred_element_type=F32)


def dot_tn(a, b):
    return lax.dot_general(a, b, (((0,), (0,)), ((), ())), preferred_element_type=F32)


def adamw(gradient, moment, square, weight, clip_factor):
    clipped = gradient * clip_factor
    moment_new = BETA_ONE * moment + (1.0 - BETA_ONE) * clipped
    square_new = BETA_TWO * square + (1.0 - BETA_TWO) * clipped * clipped
    corrected = (
        moment_new
        / (1.0 - BETA_ONE**STEP)
        / (jnp.sqrt(square_new / (1.0 - BETA_TWO**STEP)) + 1e-08)
    )
    return (moment_new, square_new, -RATE * (corrected + DECAY * weight))


def weight_shard(weight, group_index, shard_rows):
    return lax.dynamic_slice_in_dim(weight, group_index * shard_rows, shard_rows, 1).astype(F32)


class Layout:
    def __init__(self, n_row, img, txt):
        self.n_row = n_row
        self.img = img
        self.txt = txt
        self.txt_pad = -(-txt // 16) * 16
        self.rows = img + self.txt_pad
        self.real = img + txt

    def pack(self, image, text):
        return jnp.concatenate(
            [image, text, jnp.zeros((self.txt_pad - self.txt, image.shape[1]), image.dtype)], 0
        )

    def mm(self, full, w, f):
        full = full.reshape(self.n_row, self.rows, -1)
        one = f(full[:, : self.img], w[0])
        two = f(full[:, self.img :], w[1])
        return jnp.concatenate([one, two], 1).reshape(self.n_row * self.rows, -1)

    def grad(self, left, right):
        left = left.reshape(self.n_row, self.rows, -1)
        right = right.reshape(self.n_row, self.rows, -1)
        parts = []
        for part in (slice(0, self.img), slice(self.img, self.rows)):
            a = left[:, part].reshape(-1, left.shape[2])
            b = right[:, part].reshape(-1, right.shape[2])
            parts.append(dot_tn(a, b))
        return jnp.stack(parts)


def row_gather(x):
    return lax.all_gather(x, "row", axis=0, tiled=True)


def row_reduce(x):
    return lax.psum_scatter(x.astype(BF), "row", scatter_dimension=0, tiled=True).astype(F32)


def col_swap(x, n_col):
    return lax.ppermute(x, "col", [(i, (i + 1) % n_col) for i in range(n_col)])


def col_reduce(x, n_col):
    c = lax.axis_index("col")
    half = x.shape[1] // 2
    mine = lax.dynamic_slice_in_dim(x, c * half, half, 1)
    other = lax.dynamic_slice_in_dim(x, (1 - c) * half, half, 1).astype(BF)
    return mine + col_swap(other, n_col).astype(F32)


def col_gather(x, n_col):
    c = lax.axis_index("col")
    other = col_swap(x, n_col)
    both = jnp.where(c == 0, jnp.stack([x, other]), jnp.stack([other, x]))
    return jnp.concatenate([both[0], both[1]], 1)


def token_sums(a, b):
    return lax.psum(jnp.stack([jnp.sum(a, 1), jnp.sum(b, 1)]), "col")


def norm(x):
    sums = token_sums(x, x * x) / D
    center, square = sums[0], sums[1]
    inverse = lax.rsqrt(square - center * center + EPSILON)[:, None]
    return (x - center[:, None]) * inverse, inverse


def norm_back(normed, inverse, gradient):
    sums = token_sums(gradient, gradient * normed) / D
    return inverse * (gradient - sums[0][:, None] - normed * sums[1][:, None])


def attention_forward(qkv, heads, real, rows):
    t = qkv.shape[0]
    parts = qkv.reshape(t, heads, 3, HD)
    valid = (jnp.arange(t) % rows) < real
    s = jnp.einsum("qhd,khd->hqk", parts[:, :, 0], parts[:, :, 1], preferred_element_type=F32)
    s = jnp.where(valid[None, None], s * HD**-0.5, -1e30)
    peak = jnp.max(s, axis=2, keepdims=True)
    e = jnp.exp(s - peak)
    total = jnp.sum(e, axis=2, keepdims=True)
    p = (e / total).astype(BF)
    o = jnp.einsum("hqk,khd->qhd", p, parts[:, :, 2], preferred_element_type=F32)
    return o.astype(BF).reshape(t, heads * HD), peak + jnp.log(total)


def attention_backward(qkv, lse, do, heads, real, rows):
    t = qkv.shape[0]
    parts = qkv.reshape(t, heads, 3, HD)
    do = do.reshape(t, heads, HD)
    valid = (jnp.arange(t) % rows) < real
    q, k, v = parts[:, :, 0], parts[:, :, 1], parts[:, :, 2]
    s = jnp.einsum("qhd,khd->hqk", q, k, preferred_element_type=F32) * HD**-0.5
    p = jnp.where(valid[None, None], jnp.exp(s - lse), 0.0)
    dp = jnp.einsum("qhd,khd->hqk", do, v, preferred_element_type=F32)
    row_dot = jnp.sum(p * dp, axis=2, keepdims=True)
    ds = (p * (dp - row_dot)).astype(BF)
    dq = jnp.einsum("hqk,khd->qhd", ds, k, preferred_element_type=F32) * HD**-0.5
    dk = jnp.einsum("hqk,qhd->khd", ds, q, preferred_element_type=F32) * HD**-0.5
    dv = jnp.einsum("hqk,qhd->khd", p.astype(BF), do, preferred_element_type=F32)
    return jnp.stack([dq, dk, dv], 2).astype(BF).reshape(t, heads * 3 * HD)


def on_device(n_row, n_col, *args):
    (
        image_input,
        text_input,
        image_cotan,
        text_cotan,
        seq_group,
        w_attend,
        w_output,
        w_expand,
        w_reduce,
        m_attend,
        m_output,
        m_expand,
        m_reduce,
        v_attend,
        v_output,
        v_expand,
        v_reduce,
    ) = args
    img, txt = image_input.shape[1], text_input.shape[1]
    lay = Layout(n_row, img, txt)
    heads = w_attend.shape[2] // (3 * HD) // n_col
    group_index = lax.axis_index("batch")
    present = jnp.any(seq_group == group_index).astype(F32)

    x = lay.pack(image_input[0], text_input[0]).astype(F32)
    cot = lay.pack(image_cotan[0], text_cotan[0]).astype(F32) * present
    cb_all = row_gather(cot.astype(BF))

    normed_one, inverse_one = norm(x)
    a1_all = row_gather(normed_one.astype(BF))
    qkv = col_reduce(lay.mm(a1_all, w_attend, dot), n_col).astype(BF)
    o, lse = attention_forward(qkv, heads, lay.real, lay.rows)
    o_all = col_gather(o, n_col)
    middle = x + row_reduce(lay.mm(o_all, w_output, dot))
    normed_two, inverse_two = norm(middle)
    a2_all = row_gather(normed_two.astype(BF))
    dact = col_reduce(lay.mm(cb_all, w_reduce, dot_nt), n_col)
    hidden = col_reduce(lay.mm(a2_all, w_expand, dot), n_col)
    act, gelu_pull = jax.vjp(partial(jax.nn.gelu, approximate=True), hidden)
    dhidden = gelu_pull(dact)[0].astype(BF)
    dh_all = col_gather(dhidden, n_col)
    dn = row_reduce(lay.mm(dh_all, w_expand, dot_nt))
    g_all = col_gather(act.astype(BF), n_col)
    result = middle + row_reduce(lay.mm(g_all, w_reduce, dot))
    grad_mid = cot + norm_back(normed_two, inverse_two, dn)
    dy_all = row_gather(grad_mid.astype(BF))
    do = col_reduce(lay.mm(dy_all, w_output, dot_nt), n_col).astype(BF)

    g_red = lay.grad(g_all, cb_all)
    g_exp = lay.grad(a2_all, dh_all)
    g_out = lay.grad(o_all, dy_all)
    dqkv = attention_backward(qkv, lse, do, heads, lay.real, lay.rows)
    dqkv_all = col_gather(dqkv, n_col)
    g_att = lay.grad(a1_all, dqkv_all)
    da = row_reduce(lay.mm(dqkv_all, w_attend, dot_nt))
    grad_in = grad_mid + norm_back(normed_one, inverse_one, da)

    def batch_sum(g):
        return lax.psum_scatter(g.astype(BF), "batch", scatter_dimension=1, tiled=True).astype(F32)

    sums = [batch_sum(g) for g in (g_att, g_out, g_exp, g_red)]
    squares = sum(jnp.sum(g * g) for g in sums)
    grad_norm = jnp.sqrt(lax.psum(squares, ("batch", "row", "col")))
    clip_factor = jnp.minimum(1.0, 1.0 / (grad_norm + 1e-06))
    news = []
    for g, m, v, w in zip(
        sums,
        (m_attend, m_output, m_expand, m_reduce),
        (v_attend, v_output, v_expand, v_reduce),
        (w_attend, w_output, w_expand, w_reduce),
    ):
        news.append(adamw(g, m, v, weight_shard(w, group_index, g.shape[1]), clip_factor))
    return (
        result[:img].astype(BF)[None],
        result[img : lay.real].astype(BF)[None],
        grad_in[:img][None],
        grad_in[img : lay.real][None],
        *sums,
        *[n[0] for n in news],
        *[n[1] for n in news],
        *[n[2] for n in news],
        grad_norm,
    )


def solution(mesh):
    tokens = P("batch", "row", "col")
    wide = P(None, "col", "row")
    tall = P(None, "row", "col")
    wide_shard = P(None, ("col", "batch"), "row")
    tall_shard = P(None, ("row", "batch"), "col")
    shards = (wide_shard, tall_shard, wide_shard, tall_shard)
    return jax.shard_map(
        partial(on_device, mesh.shape["row"], mesh.shape["col"]),
        mesh=mesh,
        in_specs=(*[tokens] * 4, P(), wide, tall, wide, tall, *shards, *shards),
        out_specs=(*[tokens] * 4, *shards * 4, P()),
        check_vma=False,
    )
```

time: 1420 us -> 863 us (0.61)
  blocking collectives: 358 us -> 60.5 us
  waiting for transfers between devices: 746 us -> 505 us
  matrix products: 123 us -> 102 us
  other arithmetic: 92.2 us -> 111 us
    reduce_scatter x13 -> x8, waiting for transfers between devices: 520 us -> 166 us  [the longest x4 133 us: row_reduce(): lax.psum_scatter(x.astype(BF), 'row', scatter_dimension=0, tiled=True)]
    ppermute x0 -> x8, waiting for transfers between devices: none -> 194 us  [col_swap(): return lax.ppermute(x, 'col', [(i, (i + 1) % n_col) for i in range(n_col)])]
    unnamed x7 -> x0, blocking collectives: 191 us -> none
    all_gather x10 -> x0, blocking collectives: 107 us -> none  [the longest x2 28.7 us: rows_back(): lax.all_gather(part_two, 'row', axis=0, tiled=True)]
    all_gather x8 -> x4, waiting for transfers between devices: 222 us -> 144 us  [row_gather(): return lax.all_gather(x, 'row', axis=0, tiled=True)]
    dot_general x30, matrix products: 123 us -> 102 us  [the longest x8 20.7 us: dot_tn(): lax.dot_general(a, b, (((0,), (0,)), ((), ())), preferred_element_type=F32)]
    unnamed x8 -> x0, starting transfers between devices: 20.1 us -> none
    convert_element_type x6 -> x8, other arithmetic: 22.5 us -> 30.8 us  [the longest x1 13 us: attention_backward(): ds = (p * (dp - row_dot)).astype(BF)]
  transfers between devices with their start and end apart: 29 -> 20, of which waited for: 21 -> 16; matrix products, arithmetic and copies ran while one was open for 19% -> 17% of each run, Pallas kernels for 0% -> 0%
where the time goes in v1:
time: 863 us; the launch traced here: 858 us
  waiting for transfers between devices  505 us (59%)
  other arithmetic  111 us (13%)
  matrix products  102 us (12%)
  blocking collectives  60.5 us (7%)
  local copies, waits for them, and re-layouts  46.8 us (5%)
  between operations  20.4 us (2%)
  starting transfers between devices  12.1 us (1%)
    ppermute x8, waiting for transfers between devices, col_swap(): return lax.ppermute(x, 'col', [(i, (i + 1) % n_col) for i in range(n_col)])  194 us
    all_gather x4, waiting for transfers between devices, row_gather(): return lax.all_gather(x, 'row', axis=0, tiled=True)  144 us
    reduce_scatter x4, waiting for transfers between devices, row_reduce(): lax.psum_scatter(x.astype(BF), 'row', scatter_dimension=0, tiled=True)  133 us
    psum x1, blocking collectives, on_device(): grad_norm = jnp.sqrt(lax.psum(squares, ('batch', 'row', 'col')))  39.8 us
    reduce_scatter x4, waiting for transfers between devices, batch_sum(): lax.psum_scatter(g.astype(BF), 'batch', scatter_dimension=1, tiled=True)  32.8 us
    unnamed x114, local copies, waits for them, and re-layouts  26.2 us
    psum x4, blocking collectives, token_sums(): return lax.psum(jnp.stack([jnp.sum(a, 1), jnp.sum(b, 1)]), 'col')  20.7 us
    dot_general x8, matrix products, dot_tn(): lax.dot_general(a, b, (((0,), (0,)), ((), ())), preferred_element_type=F32)  20.7 us
  transfers between devices with their start and end apart: 20, of which 16 were waited for; matrix products, arithmetic and copies ran while one was open for 17% of the time, Pallas kernels for 0%

profile of v1, /device:TPU:0, one launch (start us, length us, event | category | flops | bytes accessed | tf_op | source)
XLA Modules:
  0.0 857.9 jit_solution(9389037330932039309)
XLA Ops:
  10.7 5.9 psum.35
  19.1 43.8 %all-gather.5.cloned.1.call-done = bf16[1216,768]{1,0:T(8,128)(2,1)} async-done(((bf16[304,768]{1,0:T(8,128)(2,1)}), bf16[1216,768]{1,0:T(8,128)(2,1)}) %all-gather.5.cloned.1.call-update) | async-done | bytes 1867792 | tf_op jit(solution)/shard_map/all_gather | solution.py:82
  65.2 3.7 fusion.63
  75.8 2.9 constant_dynamic-slice_fusion.3
  81.2 27.5 %collective-permute-done = bf16[1216,576]{0,1:T(8,128)(2,1)} collective-permute-done((bf16[1216,576]{0,1:T(8,128)(2,1)}, bf16[1216,576]{0,1:T(8,128)(2,1)}, u32[]{:S(2)}, u32[]{:S(2)}) %collective-permute-start) | collective-permute-done | bytes 1400864 | tf_op jit(solution)/shard_map/ppermute | solution.py:90
  111.2 8.2 select_reduce_fusion
  119.5 9.9 %fusion = f32[3,1216]{1,0:T(4,128)S(1)} fusion(f32[3,1216,1216]{1,2,0:T(8,128)} %get-tuple-element.73, f32[3,1216]{1,0:T(4,128)S(1)} %get-tuple-element.72, pred[1216]{0:T(1024)(128)(4,1)S(1)} %fusion.139), kind=kLoop, calls=%fused_computation.7 | loop fusion | flops 13304256 | bytes 17774272 | tf_op jit(solution)/shard_map/reduce_sum | solution.py:132
  129.4 9.3 %fusion.28 = bf16[3,64,1216]{2,1,0:T(8,128)(2,1)S(1)} fusion(f32[3,1216,1216]{1,2,0:T(8,128)} %get-tuple-element.73, f32[3,1216]{1,0:T(4,128)S(1)} %fusion, f32[3,1216]{1,0:T(4,128)S(1)} %get-tuple-element.72, pred[1216]{0:T(1024)(128)(4,1)S(1)} %fusion.139, bf16[1216,3,3,64]{0,3,2,1:T(8,128)(2,1)S(1)} %bitcast.224), kind=kOutput, calls=%fused_computation.66 | convolution fusion | flops 585781248 | bytes 18745344 | tf_op jit(solution)/shard_map/hqk,khd->qhd/dot_general | solution.py:134
  140.3 10.6 %collective-permute-done.1 = bf16[1216,192]{0,1:T(8,128)(2,1)S(1)} collective-permute-done((bf16[1216,192]{0,1:T(8,128)(2,1)S(1)}, bf16[1216,192]{0,1:T(8,128)(2,1)S(1)}, u32[]{:S(2)}, u32[]{:S(2)}) %collective-permute-start.1) | collective-permute-done | bytes 466976 | tf_op jit(solution)/shard_map/ppermute | solution.py:90
  158.4 38.5 %reduce-scatter.9.cloned.1.call-done = bf16[304,768]{1,0:T(8,128)(2,1)} async-done(((bf16[1216,768]{1,0:T(8,128)(2,1)}), bf16[304,768]{1,0:T(8,128)(2,1)}) %reduce-scatter.9.cloned.1.call-update) | async-done | bytes 466960 | tf_op jit(solution)/shard_map/reduce_scatter | solution.py:86
  198.3 4.9 psum.36
  205.5 34.7 %all-gather.9.cloned.1.call-done = bf16[1216,768]{1,0:T(8,128)(2,1)} async-done(((bf16[304,768]{1,0:T(8,128)(2,1)}), bf16[1216,768]{1,0:T(8,128)(2,1)}) %all-gather.9.cloned.1.call-update) | async-done | bytes 1867792 | tf_op jit(solution)/shard_map/all_gather | solution.py:82
  242.9 6.2 fusion.36
  249.1 3.4 pad_maximum_fusion.1
  252.6 3.1 copy-done.1
  258.7 24.3 %all-gather.7.cloned.1.call-done = bf16[1216,768]{1,0:T(8,128)(2,1)} async-done(((bf16[304,768]{1,0:T(8,128)(2,1)}), bf16[1216,768]{1,0:T(8,128)(2,1)}) %all-gather.7.cloned.1.call-update) | async-done | bytes 1867792 | tf_op jit(solution)/shard_map/all_gather | solution.py:82
  285.5 6.1 fusion.46
  291.6 3.4 pad_maximum_fusion
  295.0 3.0 copy-done.2
  300.9 41.3 %collective-permute-done.2 = bf16[1216,768]{1,0:T(8,128)(2,1)} collective-permute-done((bf16[1216,768]{1,0:T(8,128)(2,1)}, bf16[1216,768]{1,0:T(8,128)(2,1)}, u32[]{:S(2)}, u32[]{:S(2)}) %collective-permute-start.2) | collective-permute-done | bytes 1867808 | tf_op jit(solution)/shard_map/ppermute | solution.py:90
  342.2 5.8 fusion.12
  350.1 41.6 %collective-permute-done.5 = bf16[1216,768]{1,0:T(8,128)(2,1)S(1)} collective-permute-done((bf16[1216,768]{1,0:T(8,128)(2,1)S(1)}, bf16[1216,768]{1,0:T(8,128)(2,1)S(1)}, u32[]{:S(2)}, u32[]{:S(2)}) %collective-permute-start.5) | collective-permute-done | bytes 1867808 | tf_op jit(solution)/shard_map/ppermute | solution.py:90
  391.8 38.0 %collective-permute-done.3 = bf16[1216,768]{1,0:T(8,128)(2,1)S(1)} collective-permute-done((bf16[1216,768]{1,0:T(8,128)(2,1)S(1)}, bf16[1216,768]{1,0:T(8,128)(2,1)S(1)}, u32[]{:S(2)}, u32[]{:S(2)}) %collective-permute-start.3) | collective-permute-done | bytes 1867808 | tf_op jit(solution)/shard_map/ppermute | solution.py:90
  429.7 3.0 maximum_select_fusion
  433.1 3.2 slice-done
  450.2 30.4 %reduce-scatter.13.cloned.1.call-done = bf16[304,768]{1,0:T(8,128)(2,1)} async-done(((bf16[1216,768]{1,0:T(8,128)(2,1)}), bf16[304,768]{1,0:T(8,128)(2,1)}) %reduce-scatter.13.cloned.1.call-update) | async-done | bytes 466960 | tf_op jit(solution)/shard_map/reduce_scatter | solution.py:86
  482.3 4.9 psum.37
  487.2 35.2 %reduce-scatter.11.cloned.1.call-done = bf16[304,768]{1,0:T(8,128)(2,1)} async-done(((bf16[1216,768]{1,0:T(8,128)(2,1)}), bf16[304,768]{1,0:T(8,128)(2,1)}) %reduce-scatter.11.cloned.1.call-update) | async-done | bytes 466960 | tf_op jit(solution)/shard_map/reduce_scatter | solution.py:86
  522.4 3.0 fusion.157
  525.5 41.2 %all-gather.11.cloned.1.call-done = bf16[1216,768]{1,0:T(8,128)(2,1)} async-done(((bf16[304,768]{1,0:T(8,128)(2,1)}), bf16[1216,768]{1,0:T(8,128)(2,1)}) %all-gather.11.cloned.1.call-update) | async-done | bytes 1867792 | tf_op jit(solution)/shard_map/all_gather | solution.py:82
  574.6 3.2 fusion.18
  581.5 3.3 fusion.21
  584.8 4.1 fusion.17
  594.3 5.0 pad_maximum_fusion.3
  602.7 3.4 collective-permute-done.6
  607.8 13.8 %multiply_reduce_fusion = (f32[3,1216]{1,0:T(4,128)S(1)}, f32[3,1216,1216]{1,2,0:T(8,128)}) fusion(f32[3,1216,1216]{1,2,0:T(8,128)} %get-tuple-element.73, f32[3,1216]{1,0:T(4,128)S(1)} %log_add_fusion, pred[1216]{0:T(1024)(128)(4,1)S(1)} %fusion.139, bf16[1216,3,64]{0,2,1:T(8,128)(2,1)S(1)} %bitcast.264, bf16[1216,3,3,64]{0,3,2,1:T(8,128)(2,1)S(1)} %bitcast.225), kind=kOutput, calls=%fused_computation.2 | convolution fusion | flops 585544128 | bytes 36507904 | tf_op jit(solution)/shard_map/qhd,khd->hqk/dot_general | solution.py:146
  621.6 13.0 %multiply_convert_fusion = bf16[3,1216,1216]{1,2,0:T(8,128)(2,1)S(1)} fusion(f32[3,1216,1216]{1,2,0:T(8,128)} %get-tuple-element.75, f32[3,1216,1216]{1,2,0:T(8,128)} %get-tuple-element.73, f32[3,1216]{1,0:T(4,128)S(1)} %get-tuple-element.74, f32[3,1216]{1,0:T(4,128)S(1)} %log_add_fusion, pred[1216]{0:T(1024)(128)(4,1)S(1)} %fusion.139), kind=kLoop, calls=%fused_computation.1 | loop fusion | flops 22179840 | bytes 44390080 | tf_op jit(solution)/shard_map/convert_element_type | solution.py:148
  639.1 8.2 fusion.25
  649.2 32.1 %collective-permute-done.7 = bf16[1216,576]{0,1:T(8,128)(2,1)S(1)} collective-permute-done((bf16[1216,576]{0,1:T(8,128)(2,1)S(1)}, bf16[1216,576]{0,1:T(8,128)(2,1)S(1)}, u32[]{:S(2)}, u32[]{:S(2)}) %collective-permute-start.7) | collective-permute-done | bytes 1400864 | tf_op jit(solution)/shard_map/ppermute | solution.py:90
  706.6 4.7 multiply_reduce_fusion.2
  711.3 29.0 %reduce-scatter.15.cloned.1.call-done = bf16[304,768]{1,0:T(8,128)(2,1)} async-done(((bf16[1216,768]{1,0:T(8,128)(2,1)}), bf16[304,768]{1,0:T(8,128)(2,1)}) %reduce-scatter.15.cloned.1.call-update) | async-done | bytes 466960 | tf_op jit(solution)/shard_map/reduce_scatter | solution.py:86
  741.9 4.9 psum.38
  749.8 32.8 %reduce-scatter.17.cloned.1.call-done = bf16[2,192,1152]{2,1,0:T(8,128)(2,1)} async-done(((bf16[2,768,1152]{2,1,0:T(8,128)(2,1)}), bf16[2,192,1152]{2,1,0:T(8,128)(2,1)}) %reduce-scatter.17.cloned.1.call-update) | async-done | bytes 884752 | tf_op jit(solution)/shard_map/reduce_scatter | solution.py:215
  782.6 3.4 multiply_reduce_fusion.3
  789.3 39.8 %psum.39 = f32[]{:T(128)} all-reduce(f32[]{:T(128)S(6)} %add.217), channel_id=1, replica_groups=mesh['batch'=4,'row'=4,'col'=2] {'batch','row','col'}, use_global_device_ids=true, to_apply=%region_28.29 | all-reduce | flops 1 | bytes 8 | tf_op jit(solution)/shard_map/psum | solution.py:219
  829.8 6.2 add_multiply_fusion.2
  836.0 5.7 add_multiply_fusion.1
  844.4 5.4 add_multiply_fusion
  (243 shorter events, 122.4 us)
Async XLA Ops:
  7.2 55.7 %all-gather.5.cloned.1.call-start = ((), (), s32[]{:S(2)}) async-start(), calls=%async_computation.8 | async-start | bytes 2334720 | tf_op jit(solution)/shard_map/all_gather | solution.py:82
  16.6 48.6 %copy-start.40 = (f32[304]{0:T(512)}, f32[304]{0:T(512)S(1)}, u32[]{:S(2)}) copy-start(f32[304]{0:T(512)S(1)} %get-tuple-element.35) | copy-start | bytes 3652
  16.6 48.6 %copy-start.42 = (f32[304]{0:T(512)}, f32[304]{0:T(512)S(1)}, u32[]{:S(2)}) copy-start(f32[304]{0:T(512)S(1)} %add_rsqrt_fusion.1) | copy-start | bytes 3652
  19.0 177.8 %reduce-scatter.9.cloned.1.call-start = ((), (), s32[]{:S(2)}) async-start(), calls=%async_computation.9 | async-start | bytes 2334720 | tf_op jit(solution)/shard_map/reduce_scatter | solution.py:86
  74.3 34.3 %collective-permute-start = (bf16[1216,576]{0,1:T(8,128)(2,1)}, bf16[1216,576]{0,1:T(8,128)(2,1)}, u32[]{:S(2)}, u32[]{:S(2)}) collective-permute-start(bf16[1216,576]{0,1:T(8,128)(2,1)} %copy.99), channel_id=1, source_target_pairs={{0,1},{1,0},{2,3},{3,2},{4,5},{5,4},{6,7},{7,6},{8,9},{9,8},{10,11... | collective-permute-start | bytes 4202504 | tf_op jit(solution)/shard_map/ppermute | solution.py:90
  129.4 9.3 %copy-start.38 = (f32[3,1216]{1,0:T(4,128)}, f32[3,1216]{1,0:T(4,128)S(1)}, u32[]{:S(2)}) copy-start(f32[3,1216]{1,0:T(4,128)S(1)} %fusion) | copy-start | bytes 43780
  138.8 12.1 %collective-permute-start.1 = (bf16[1216,192]{0,1:T(8,128)(2,1)S(1)}, bf16[1216,192]{0,1:T(8,128)(2,1)S(1)}, u32[]{:S(2)}, u32[]{:S(2)}) collective-permute-start(bf16[1216,192]{0,1:T(8,128)(2,1)S(1)} %bitcast.277), channel_id=1, source_target_pairs={{0,1},{1,0},{2,3},{3,2},{4,5},{5,4},{6,7},{7,6},{8,9},{9,8},{10,11... | collective-permute-start | bytes 1400840 | tf_op jit(solution)/shard_map/ppermute | solution.py:90
  156.2 40.7 %copy-start = (bf16[1,256,768]{2,1,0:T(8,128)(2,1)S(1)}, bf16[1,256,768]{2,1,0:T(8,128)(2,1)}, u32[]{:S(2)}) copy-start(bf16[1,256,768]{2,1,0:T(8,128)(2,1)} %param.17) | copy-start | bytes 1179652
  156.2 40.7 %copy-start.16 = (bf16[1,38,768]{2,1,0:T(8,128)(2,1)S(1)}, bf16[1,38,768]{2,1,0:T(8,128)(2,1)}, u32[]{:S(2)}) copy-start(bf16[1,38,768]{2,1,0:T(8,128)(2,1)} %param.18) | copy-start | bytes 175108
  157.6 82.5 %all-gather.9.cloned.1.call-start = ((), (), s32[]{:S(2)}) async-start(), calls=%async_computation.12 | async-start | bytes 2334720 | tf_op jit(solution)/shard_map/all_gather | solution.py:82
  158.3 124.6 %all-gather.7.cloned.1.call-start = ((), (), s32[]{:S(2)}) async-start(), calls=%async_computation.10 | async-start | bytes 2334720 | tf_op jit(solution)/shard_map/all_gather | solution.py:82
  205.4 275.2 %reduce-scatter.13.cloned.1.call-start = ((), (), s32[]{:S(2)}) async-start(), calls=%async_computation.13 | async-start | bytes 2334720 | tf_op jit(solution)/shard_map/reduce_scatter | solution.py:86
  257.1 43.8 %collective-permute-start.4 = (bf16[1216,768]{1,0:T(8,128)(2,1)}, bf16[1216,768]{1,0:T(8,128)(2,1)}, u32[]{:S(2)}, u32[]{:S(2)}) collective-permute-start(bf16[1216,768]{1,0:T(8,128)(2,1)} %dynamic-slice_convert_fusion), channel_id=1, source_target_pairs={{0,1},{1,0},{2,3},{3,2},{4,5},{5,4},{6,7},{7,6},{8,9},{9,8},{10,11... | collective-permute-start | bytes 5603336 | tf_op jit(solution)/shard_map/ppermute | solution.py:90
  299.4 42.8 %collective-permute-start.2 = (bf16[1216,768]{1,0:T(8,128)(2,1)}, bf16[1216,768]{1,0:T(8,128)(2,1)}, u32[]{:S(2)}, u32[]{:S(2)}) collective-permute-start(bf16[1216,768]{1,0:T(8,128)(2,1)} %dynamic-slice_convert_fusion.1), channel_id=1, source_target_pairs={{0,1},{1,0},{2,3},{3,2},{4,5},{5,4},{6,7},{7,6},{8,9},{9,8},{10,11... | collective-permute-start | bytes 5603336 | tf_op jit(solution)/shard_map/ppermute | solution.py:90
  348.0 43.7 %collective-permute-start.5 = (bf16[1216,768]{1,0:T(8,128)(2,1)S(1)}, bf16[1216,768]{1,0:T(8,128)(2,1)S(1)}, u32[]{:S(2)}, u32[]{:S(2)}) collective-permute-start(bf16[1216,768]{1,0:T(8,128)(2,1)S(1)} %get-tuple-element.59), channel_id=1, source_target_pairs={{0,1},{1,0},{2,3},{3,2},{4,5},{5,4},{6,7},{7,6},{8,9},{9,8},{10,11... | collective-permute-start | bytes 5603336 | tf_op jit(solution)/shard_map/ppermute | solution.py:90
  349.6 80.1 %collective-permute-start.3 = (bf16[1216,768]{1,0:T(8,128)(2,1)S(1)}, bf16[1216,768]{1,0:T(8,128)(2,1)S(1)}, u32[]{:S(2)}, u32[]{:S(2)}) collective-permute-start(bf16[1216,768]{1,0:T(8,128)(2,1)S(1)} %get-tuple-element.60), channel_id=1, source_target_pairs={{0,1},{1,0},{2,3},{3,2},{4,5},{5,4},{6,7},{7,6},{8,9},{9,8},{10,11... | collective-permute-start | bytes 5603336 | tf_op jit(solution)/shard_map/ppermute | solution.py:90
  432.7 3.5 slice-start
  432.7 3.6 slice-start.1
  433.0 6.0 copy-start.7
  433.0 6.0 copy-start.9
  441.4 81.1 %reduce-scatter.11.cloned.1.call-start = ((), (), s32[]{:S(2)}) async-start(), calls=%async_computation.11 | async-start | bytes 2334720 | tf_op jit(solution)/shard_map/reduce_scatter | solution.py:86
  441.4 3.4 slice-start.2
  441.4 3.5 slice-start.3
  448.5 32.0 %copy-start.6 = (bf16[304,768]{1,0:T(8,128)(2,1)S(1)}, bf16[304,768]{1,0:T(8,128)(2,1)}, u32[]{:S(2)}) copy-start(bf16[304,768]{1,0:T(8,128)(2,1)} %reduce-scatter.9.cloned.1.call-done) | copy-start | bytes 1400836
  449.9 72.5 %copy-start.24 = (bf16[1,256,768]{2,1,0:T(8,128)(2,1)S(1)}, bf16[1,256,768]{2,1,0:T(8,128)(2,1)}, u32[]{:S(2)}) copy-start(bf16[1,256,768]{2,1,0:T(8,128)(2,1)} %param.19) | copy-start | bytes 1179652
  449.9 72.5 %copy-start.36 = (bf16[1,38,768]{2,1,0:T(8,128)(2,1)S(1)}, bf16[1,38,768]{2,1,0:T(8,128)(2,1)}, u32[]{:S(2)}) copy-start(bf16[1,38,768]{2,1,0:T(8,128)(2,1)} %param.20) | copy-start | bytes 175108
  449.9 116.8 %all-gather.11.cloned.1.call-start = ((), (), s32[]{:S(2)}) async-start(), calls=%async_computation.14 | async-start | bytes 2334720 | tf_op jit(solution)/shard_map/all_gather | solution.py:82
  525.5 176.7 %reduce-scatter.19.cloned.1.call-start = ((), (), s32[]{:S(2)}) async-start(), calls=%async_computation.17 | async-start | bytes 1474560 | tf_op jit(solution)/shard_map/reduce_scatter | solution.py:215
  571.8 132.1 %reduce-scatter.23.cloned.1.call-start = ((), (), s32[]{:S(2)}) async-start(), calls=%async_computation.19 | async-start | bytes 5898240 | tf_op jit(solution)/shard_map/reduce_scatter | solution.py:215
  580.4 126.2 %reduce-scatter.21.cloned.1.call-start = ((), (), s32[]{:S(2)}) async-start(), calls=%async_computation.18 | async-start | bytes 5898240 | tf_op jit(solution)/shard_map/reduce_scatter | solution.py:215
  581.5 3.3 copy-start.47
  584.8 4.1 copy-start.26
  584.8 4.1 copy-start.50
  592.9 13.3 %collective-permute-start.6 = (bf16[1216,192]{0,1:T(8,128)(2,1)}, bf16[1216,192]{0,1:T(8,128)(2,1)}, u32[]{:S(2)}, u32[]{:S(2)}) collective-permute-start(bf16[1216,192]{0,1:T(8,128)(2,1)} %copy.104), channel_id=1, source_target_pairs={{0,1},{1,0},{2,3},{3,2},{4,5},{5,4},{6,7},{7,6},{8,9},{9,8},{10,11... | collective-permute-start | bytes 1400840 | tf_op jit(solution)/shard_map/ppermute | solution.py:90
  599.4 141.0 %reduce-scatter.15.cloned.1.call-start = ((), (), s32[]{:S(2)}) async-start(), calls=%async_computation.15 | async-start | bytes 2334720 | tf_op jit(solution)/shard_map/reduce_scatter | solution.py:86
  647.6 33.6 %collective-permute-start.7 = (bf16[1216,576]{0,1:T(8,128)(2,1)S(1)}, bf16[1216,576]{0,1:T(8,128)(2,1)S(1)}, u32[]{:S(2)}, u32[]{:S(2)}) collective-permute-start(bf16[1216,576]{0,1:T(8,128)(2,1)S(1)} %bitcast.254), channel_id=1, source_target_pairs={{0,1},{1,0},{2,3},{3,2},{4,5},{5,4},{6,7},{7,6},{8,9},{9,8},{10,11... | collective-permute-start | bytes 4202504 | tf_op jit(solution)/shard_map/ppermute | solution.py:90
  693.0 89.6 %reduce-scatter.17.cloned.1.call-start = ((), (), s32[]{:S(2)}) async-start(), calls=%async_computation.16 | async-start | bytes 4423680 | tf_op jit(solution)/shard_map/reduce_scatter | solution.py:215
  703.9 137.9 %copy-start.18 = (f32[2,96,768]{2,1,0:T(8,128)}, f32[2,96,768]{2,1,0:T(8,128)S(1)}, u32[]{:S(2)}) copy-start(f32[2,96,768]{2,1,0:T(8,128)S(1)} %get-tuple-element.54) | copy-start | bytes 1769476
  706.6 137.8 %copy-start.4 = (f32[2,384,768]{2,1,0:T(8,128)}, f32[2,384,768]{2,1,0:T(8,128)S(1)}, u32[]{:S(2)}) copy-start(f32[2,384,768]{2,1,0:T(8,128)S(1)} %get-tuple-element.50) | copy-start | bytes 7077892
  706.6 33.8 %copy-start.17 = (bf16[1,38,768]{2,1,0:T(8,128)(2,1)S(1)}, bf16[1,38,768]{2,1,0:T(8,128)(2,1)}, u32[]{:S(2)}) copy-start(bf16[1,38,768]{2,1,0:T(8,128)(2,1)} %param.18) | copy-start | bytes 175108
  706.6 33.8 %copy-start.41 = (f32[304]{0:T(512)S(1)}, f32[304]{0:T(512)}, u32[]{:S(2)}) copy-start(f32[304]{0:T(512)} %copy-done.40) | copy-start | bytes 3652
  706.6 33.8 %copy-start.43 = (f32[304]{0:T(512)S(1)}, f32[304]{0:T(512)}, u32[]{:S(2)}) copy-start(f32[304]{0:T(512)} %copy-done.42) | copy-start | bytes 3652
  829.8 6.2 copy-start.5
  829.8 6.2 copy-start.19
  829.8 6.2 copy-start.20
  836.0 5.7 copy-start.27
  836.0 5.7 copy-start.28
  836.0 8.3 copy-start.22
  (27 other events, 58.7 us)
Sparse Core Ops, SparseCore 0:
  19.1 43.7 all-gather.4
  157.7 39.0 reduce-scatter.8
  199.0 41.0 all-gather.8
  242.1 40.7 all-gather.6
  441.5 39.0 reduce-scatter.12
  483.3 39.0 reduce-scatter.10
  525.6 41.0 all-gather.10
  571.9 24.5 reduce-scatter.18
  599.3 47.8 reduce-scatter.22
  649.5 47.8 reduce-scatter.20
  700.4 39.9 reduce-scatter.14
  742.9 39.5 reduce-scatter.16

commit v2 on v1

--- a/solution.py
+++ b/solution.py
@@ -1,8 +1,11 @@
+import math
 from functools import partial
 
 import jax
 import jax.numpy as jnp
 from jax import lax
+from jax.experimental import pallas as pl
+from jax.experimental.pallas import tpu as pltpu
 from jax.sharding import PartitionSpec as P
 
 D = 1536
@@ -29,6 +32,548 @@
 
 def dot_tn(a, b):
     return lax.dot_general(a, b, (((0,), (0,)), ((), ())), preferred_element_type=F32)
+
+
+MESH = pl.DeviceIdType.MESH
+VMEM = pl.BlockSpec(memory_space=pltpu.VMEM)
+
+
+def remote(src, dst, send, recv, **where):
+    return pltpu.make_async_remote_copy(
+        src_ref=src,
+        dst_ref=dst,
+        send_sem=send,
+        recv_sem=recv,
+        device_id=where,
+        device_id_type=MESH,
+    )
+
+
+def near_first(z, n, j):
+    alternate = jnp.where(j % 2 == 1, z - (j + 1) // 2, z + j // 2)
+    reach = jnp.minimum(z, n - 1 - z)
+    beyond = jnp.where(z <= n - 1 - z, j, n - 1 - j)
+    return jnp.where(j <= 2 * reach, alternate, beyond)
+
+
+def greet(n):
+    z, c = lax.axis_index("row"), lax.axis_index("col")
+    barrier = pltpu.get_barrier_semaphore()
+    pl.semaphore_signal(barrier, inc=1, device_id={"col": 1 - c}, device_id_type=MESH)
+
+    @pl.when(z > 0)
+    def _():
+        pl.semaphore_signal(barrier, inc=1, device_id={"row": z - 1}, device_id_type=MESH)
+
+    @pl.when(z < n - 1)
+    def _():
+        pl.semaphore_signal(barrier, inc=1, device_id={"row": z + 1}, device_id_type=MESH)
+
+    ends = jnp.where(z > 0, 1, 0) + jnp.where(z < n - 1, 1, 0)
+    pl.semaphore_wait(barrier, 1 + ends)
+
+
+class Gather:
+    def __init__(self, full, send, recv, n):
+        self.full, self.send, self.recv, self.n = full, send, recv, n
+        self.z = lax.axis_index("row")
+
+    def copy(self, k, step):
+        there = (self.z + step + self.n) % self.n
+        way = 0 if step > 0 else 1
+        return remote(
+            self.full.at[k], self.full.at[k], self.send.at[way, k], self.recv.at[k], row=there
+        )
+
+    def push(self, k):
+        @pl.when((k <= self.z) & (self.z < self.n - 1))
+        def _():
+            self.copy(k, 1).start()
+
+        @pl.when((k >= self.z) & (self.z > 0))
+        def _():
+            self.copy(k, -1).start()
+
+    def arrive(self, k):
+        @pl.when(k != self.z)
+        def _():
+            self.copy(k, 1).wait_recv()
+
+        self.push(k)
+
+    def arrive_after_own(self, k):
+        @pl.when(k != self.z)
+        def _():
+            self.arrive(k)
+
+    def finish(self):
+        @pl.loop(0, self.n)
+        def _(k):
+            @pl.when((k <= self.z) & (self.z < self.n - 1))
+            def _():
+                self.copy(k, 1).wait_send()
+
+            @pl.when((k >= self.z) & (self.z > 0))
+            def _():
+                self.copy(k, -1).wait_send()
+
+
+class Reduce:
+    def __init__(self, acc, out, inbox, send, recv, n):
+        self.acc, self.out, self.inbox, self.send, self.recv, self.n = acc, out, inbox, send, recv, n
+        self.z = lax.axis_index("row")
+
+    def copy(self, o):
+        way = jnp.where(o > self.z, 0, 1)
+        there = (self.z + jnp.where(o > self.z, 1, -1) + self.n) % self.n
+        return remote(
+            self.out.at[o], self.inbox.at[way, o], self.send.at[o], self.recv.at[way, o], row=there
+        )
+
+    def wait_in(self, way, o):
+        remote(
+            self.out.at[o],
+            self.inbox.at[way, o],
+            self.send.at[o],
+            self.recv.at[way, o],
+            row=(self.z + 1) % self.n,
+        ).wait_recv()
+
+    def add(self, o):
+        @pl.when((o >= self.z) & (self.z > 0))
+        def _():
+            self.wait_in(0, o)
+            self.acc[...] += self.inbox[0, o].astype(F32)
+
+        @pl.when((o <= self.z) & (self.z < self.n - 1))
+        def _():
+            self.wait_in(1, o)
+            self.acc[...] += self.inbox[1, o].astype(F32)
+
+        @pl.when(o != self.z)
+        def _():
+            self.out[o] = self.acc[...].astype(BF)
+            self.copy(o).start()
+
+    def finish(self):
+        @pl.loop(0, self.n)
+        def _(o):
+            @pl.when(o != self.z)
+            def _():
+                self.copy(o).wait_send()
+
+
+class Swap:
+    def __init__(self, out, into, send, recv):
+        self.out, self.into, self.send, self.recv = out, into, send, recv
+
+    def copy(self, k):
+        return remote(
+            self.out.at[k],
+            self.into.at[k],
+            self.send.at[k],
+            self.recv.at[k],
+            col=1 - lax.axis_index("col"),
+        )
+
+    def start(self, k):
+        self.copy(k).start()
+
+    def arrive(self, k):
+        self.copy(k).wait_recv()
+
+    def finish(self, n):
+        @pl.loop(0, n)
+        def _(k):
+            self.copy(k).wait_send()
+
+
+def sums_of(a, b):
+    lane = lax.broadcasted_iota(jnp.int32, (a.shape[0], 128), 1)
+    one, two = jnp.sum(a, axis=1, keepdims=True), jnp.sum(b, axis=1, keepdims=True)
+    return jnp.where(lane == 0, one, jnp.where(lane == 1, two, 0.0))
+
+
+def moments(stat):
+    mean = stat[0, :, 0:1] / D
+    return mean, lax.rsqrt(stat[0, :, 1:2] / D - mean * mean + EPSILON)
+
+
+def exchange(stat, stat_in, send, recv):
+    swap = Swap(stat, stat_in, send, recv)
+    swap.start(0)
+    swap.arrive(0)
+    swap.finish(1)
+    stat[0] += stat_in[0]
+
+
+def dma(*shape):
+    return pltpu.SemaphoreType.DMA(shape)
+
+
+def call(kernel, ident, outs, scratch, cost, *operands):
+    return pl.pallas_call(
+        kernel,
+        out_shape=[jax.ShapeDtypeStruct(s, t) for s, t in outs],
+        in_specs=[VMEM] * len(operands),
+        out_specs=[VMEM] * len(outs),
+        scratch_shapes=scratch,
+        compiler_params=pltpu.CompilerParams(
+            collective_id=ident, has_side_effects=True, vmem_limit_bytes=60 * 2**20
+        ),
+        cost_estimate=pl.CostEstimate(flops=cost, bytes_accessed=10**7, transcendentals=0),
+    )(*operands)
+
+
+def parts_of(lay):
+    return ((0, slice(0, lay.img)), (1, slice(lay.img, lay.rows)))
+
+
+def attend_kernel(lay, x_ref, w_ref, full_ref, qkv_ref, stat_ref, *scratch):
+    own, out, into, stat_in, g_send, g_recv, s_send, s_recv, t_send, t_recv = scratch
+    n = lay.n_row
+    z, c = lax.axis_index("row"), lax.axis_index("col")
+    half = qkv_ref.shape[2]
+    greet(n)
+    x = x_ref[...].astype(F32)
+    stat_ref[0] = sums_of(x, x * x)
+    exchange(stat_ref, stat_in, t_send, t_recv)
+    mean, inverse = moments(stat_ref)
+    full_ref[z] = ((x - mean) * inverse).astype(BF)
+    gather = Gather(full_ref, g_send, g_recv, n)
+    swap = Swap(out, into, s_send, s_recv)
+
+    @pl.loop(0, n)
+    def _(j):
+        k = near_first(z, n, j)
+        gather.arrive(k)
+        for part, rows in parts_of(lay):
+            p = dot(full_ref[k, rows], w_ref[part])
+            low, high = p[:, :half], p[:, half:]
+            own[k, rows] = jnp.where(c == 0, low, high)
+            out[k, rows] = jnp.where(c == 0, high, low).astype(BF)
+        swap.start(k)
+
+    @pl.loop(0, n)
+    def _(j):
+        k = near_first(z, n, j)
+        swap.arrive(k)
+        qkv_ref[k] = (own[k] + into[k].astype(F32)).astype(BF)
+
+    gather.finish()
+    swap.finish(n)
+
+
+def attend(lay, x, w):
+    n, r, half, d = lay.n_row, lay.rows, w.shape[2] // 2, x.shape[1]
+    return call(
+        partial(attend_kernel, lay),
+        1,
+        [((n, r, d), BF), ((n, r, half), BF), ((1, r, 128), F32)],
+        [
+            pltpu.VMEM((n, r, half), F32),
+            pltpu.VMEM((n, r, half), BF),
+            pltpu.VMEM((n, r, half), BF),
+            pltpu.VMEM((1, r, 128), F32),
+            dma(2, n),
+            dma(n),
+            dma(n),
+            dma(n),
+            dma(1),
+            dma(1),
+        ],
+        2 * n * r * w.shape[1] * w.shape[2],
+        x,
+        w,
+    )
+
+
+def split_heads(lay, qkv_ref, q_ref, k_ref, v_ref, fill):
+    n, img, txt = lay.n_row, lay.img, lay.txt_pad
+    heads = qkv_ref.shape[2] // (3 * HD)
+
+    @pl.loop(0, n)
+    def _(k):
+        first = pl.ds(pl.multiple_of(k * img, 16), img)
+        second = pl.ds(pl.multiple_of(n * img + k * txt, 16), txt)
+        for h in range(heads):
+            at = h * 3 * HD
+            rows = qkv_ref[k, :, at : at + 3 * HD]
+            q_ref[h, k] = rows[:, :HD] * jnp.asarray(HD**-0.5, BF)
+            for ref, lo in ((k_ref, HD), (v_ref, 2 * HD)):
+                value = rows[:, lo : lo + HD]
+                if ref is v_ref and fill:
+                    value = jnp.concatenate([value, jnp.ones_like(value)], 1)
+                ref[h, first] = value[:img]
+                ref[h, second] = value[img:]
+
+
+def text_bias(lay):
+    lane = lax.broadcasted_iota(jnp.int32, (1, lay.n_row * lay.txt_pad), 1)
+    return jnp.where(lane % lay.txt_pad < lay.txt, 0.0, -1e30)
+
+
+def middle_kernel(
+    lay, qkv_ref, x_ref, cot_ref, wo_ref, wr_ref, o_ref, lse_ref, cb_ref, dg_ref, mid_ref, low_ref, stat_ref, *scratch
+):
+    (
+        q_s, k_s, v_s, o_out, o_in, dg_out, dg_in, acc, r_out, inbox, stat_in,
+        g_send, g_recv, o_send, o_recv, d_send, d_recv, r_send, r_recv, t_send, t_recv,
+    ) = scratch
+    n, far = lay.n_row, lay.n_row * lay.img
+    z, c = lax.axis_index("row"), lax.axis_index("col")
+    heads, hid = q_s.shape[0], dg_ref.shape[2]
+    greet(n)
+    gather = Gather(cb_ref, g_send, g_recv, n)
+    cb_ref[z] = cot_ref[...]
+    gather.push(z)
+    swap_o = Swap(o_out, o_in, o_send, o_recv)
+    swap_d = Swap(dg_out, dg_in, d_send, d_recv)
+    reduce = Reduce(acc, r_out, inbox, r_send, r_recv, n)
+    split_heads(lay, qkv_ref, q_s, k_s, v_s, True)
+    bias = text_bias(lay)
+    lane = lax.broadcasted_iota(jnp.int32, (lay.rows, 128), 1)
+
+    def attention(k):
+        outs, lse = [], jnp.zeros((lay.rows, 128), F32)
+        for h in range(heads):
+            q = q_s[h, k]
+            s1 = dot_nt(q, k_s[h, :far])
+            s2 = dot_nt(q, k_s[h, far:]) + bias
+            peak = jnp.maximum(
+                jnp.max(s1, axis=1, keepdims=True), jnp.max(s2, axis=1, keepdims=True)
+            )
+            e1, e2 = jnp.exp(s1 - peak).astype(BF), jnp.exp(s2 - peak).astype(BF)
+            o = dot(e1, v_s[h, :far]) + dot(e2, v_s[h, far:])
+            total = o[:, HD : HD + 1]
+            outs.append((o[:, :HD] / total).astype(BF))
+            lse = jnp.where(lane == h, peak + jnp.log(total), lse)
+        lse_ref[k] = lse
+        o_out[k] = jnp.concatenate(outs, 1)
+
+    def project(k):
+        swap_o.arrive(k)
+        own, other = o_out[k], o_in[k]
+        o_ref[k] = jnp.concatenate(
+            [jnp.where(c == 0, own, other), jnp.where(c == 0, other, own)], 1
+        )
+        for part, rows in parts_of(lay):
+            acc[rows] = dot(o_ref[k, rows], wo_ref[part])
+        reduce.add(k)
+
+    @pl.loop(0, n)
+    def _(j):
+        k = near_first(z, n, n - 1 - j)
+        attention(k)
+        swap_o.start(k)
+        near = near_first(z, n, j)
+        gather.arrive_after_own(near)
+        for part, rows in parts_of(lay):
+            dg_out[near, rows] = dot_nt(
+                cb_ref[near, rows], wr_ref[part, pl.ds(pl.multiple_of((1 - c) * hid, 128), hid), :]
+            ).astype(BF)
+        swap_d.start(near)
+        for part, rows in parts_of(lay):
+            dg_ref[near, rows] = dot_nt(
+                cb_ref[near, rows], wr_ref[part, pl.ds(pl.multiple_of(c * hid, 128), hid), :]
+            )
+
+        @pl.when(j > 0)
+        def _():
+            project(near_first(z, n, n - j))
+
+    project(near_first(z, n, 0))
+    mid = x_ref[...].astype(F32) + acc[...]
+    mid_ref[...] = mid
+    stat_ref[0] = sums_of(mid, mid * mid)
+    exchange(stat_ref, stat_in, t_send, t_recv)
+    mean, inverse = moments(stat_ref)
+    low_ref[...] = ((mid - mean) * inverse).astype(BF)
+
+    @pl.loop(0, n)
+    def _(j):
+        k = near_first(z, n, j)
+        swap_d.arrive(k)
+        dg_ref[k] += dg_in[k].astype(F32)
+
+    gather.finish()
+    swap_o.finish(n)
+    swap_d.finish(n)
+    reduce.finish()
+
+
+def middle(lay, qkv, x, cot, wo, wr):
+    n, r, d = lay.n_row, lay.rows, x.shape[1]
+    heads, hid = qkv.shape[2] // (3 * HD), wr.shape[1] // 2
+    keys = n * r
+    return call(
+        partial(middle_kernel, lay),
+        2,
+        [
+            ((n, r, 2 * heads * HD), BF),
+            ((n, r, 128), F32),
+            ((n, r, d), BF),
+            ((n, r, hid), F32),
+            ((r, d), F32),
+            ((r, d), BF),
+            ((1, r, 128), F32),
+        ],
+        [
+            pltpu.VMEM((heads, n, r, HD), BF),
+            pltpu.VMEM((heads, keys, HD), BF),
+            pltpu.VMEM((heads, keys, 2 * HD), BF),
+            pltpu.VMEM((n, r, heads * HD), BF),
+            pltpu.VMEM((n, r, heads * HD), BF),
+            pltpu.VMEM((n, r, hid), BF),
+            pltpu.VMEM((n, r, hid), BF),
+            pltpu.VMEM((r, d), F32),
+            pltpu.VMEM((n, r, d), BF),
+            pltpu.VMEM((2, n, r, d), BF),
+            pltpu.VMEM((1, r, 128), F32),
+            dma(2, n),
+            dma(n),
+            dma(n),
+            dma(n),
+            dma(n),
+            dma(n),
+            dma(n),
+            dma(2, n),
+            dma(1),
+            dma(1),
+        ],
+        10**10,
+        qkv,
+        x,
+        cot,
+        wo,
+        wr,
+    )
+
+
+SLOPE = (2.0 / math.pi) ** 0.5
+CUBIC = 0.044715
+
+
+def gelu_pair(u):
+    square = u * u
+    t = jnp.tanh(SLOPE * u * (1.0 + CUBIC * square))
+    half = 0.5 * (1.0 + t)
+    slope = half + 0.5 * u * (1.0 - t * t) * (SLOPE * (1.0 + 3.0 * CUBIC * square))
+    return u * half, slope
+
+
+def hidden_kernel(
+    lay, low_ref, dg_ref, mid_ref, cot_ref, stat_ref, we_ref, full_ref, act_ref, dh_ref, dmid_ref, dy_ref, *scratch
+):
+    (
+        own, out, into, acc, r_out, inbox, stat_out, stat_in,
+        g_send, g_recv, s_send, s_recv, d_send, d_recv, r_send, r_recv, t_send, t_recv,
+    ) = scratch
+    n = lay.n_row
+    z, c = lax.axis_index("row"), lax.axis_index("col")
+    hid = dg_ref.shape[2]
+    mine = pl.ds(pl.multiple_of(c * hid, 128), hid)
+    theirs = pl.ds(pl.multiple_of((1 - c) * hid, 128), hid)
+    greet(n)
+    gather = Gather(full_ref, g_send, g_recv, n)
+    full_ref[z] = low_ref[...]
+    gather.push(z)
+    swap = Swap(out, into, s_send, s_recv)
+    reduce = Reduce(acc, r_out, inbox, r_send, r_recv, n)
+
+    def dh_copy(k):
+        half = dh_ref.at[k, :, mine]
+        return remote(half, half, d_send.at[k], d_recv.at[k], col=1 - c)
+
+    @pl.loop(0, n)
+    def _(j):
+        k = near_first(z, n, j)
+        gather.arrive_after_own(k)
+        for part, rows in parts_of(lay):
+            out[k, rows] = dot(full_ref[k, rows], we_ref[part, :, theirs]).astype(BF)
+        swap.start(k)
+        for part, rows in parts_of(lay):
+            own[k, rows] = dot(full_ref[k, rows], we_ref[part, :, mine])
+
+    def back(k):
+        half = dh_ref.at[k, :, theirs]
+        remote(half, half, d_send.at[k], d_recv.at[k], col=1 - c).wait_recv()
+        for part, rows in parts_of(lay):
+            acc[rows] = dot_nt(dh_ref[k, rows], we_ref[part])
+        reduce.add(k)
+
+    @pl.loop(0, n)
+    def _(j):
+        k = near_first(z, n, n - 1 - j)
+        swap.arrive(k)
+        act, slope = gelu_pair(own[k] + into[k].astype(F32))
+        act_ref[k] = act.astype(BF)
+        dh_ref[k, :, mine] = (dg_ref[k] * slope).astype(BF)
+        dh_copy(k).start()
+
+        @pl.when(j > 0)
+        def _():
+            back(near_first(z, n, n - j))
+
+    back(near_first(z, n, 0))
+    mean, inverse = moments(stat_ref)
+    normed = (mid_ref[...] - mean) * inverse
+    grad = acc[...]
+    stat_out[0] = sums_of(grad, grad * normed)
+    exchange(stat_out, stat_in, t_send, t_recv)
+    back_one, back_two = stat_out[0, :, 0:1] / D, stat_out[0, :, 1:2] / D
+    dmid = cot_ref[...].astype(F32) + inverse * (grad - back_one - normed * back_two)
+    dmid_ref[...] = dmid
+    dy_ref[...] = dmid.astype(BF)
+    gather.finish()
+    swap.finish(n)
+    reduce.finish()
+
+    @pl.loop(0, n)
+    def _(k):
+        dh_copy(k).wait_send()
+
+
+def hidden(lay, low, dg, mid, cot, stat, we):
+    n, r, d, hid = lay.n_row, lay.rows, low.shape[1], dg.shape[2]
+    return call(
+        partial(hidden_kernel, lay),
+        3,
+        [
+            ((n, r, d), BF),
+            ((n, r, hid), BF),
+            ((n, r, 2 * hid), BF),
+            ((r, d), F32),
+            ((r, d), BF),
+        ],
+        [
+            pltpu.VMEM((n, r, hid), F32),
+            pltpu.VMEM((n, r, hid), BF),
+            pltpu.VMEM((n, r, hid), BF),
+            pltpu.VMEM((r, d), F32),
+            pltpu.VMEM((n, r, d), BF),
+            pltpu.VMEM((2, n, r, d), BF),
+            pltpu.VMEM((1, r, 128), F32),
+            pltpu.VMEM((1, r, 128), F32),
+            dma(2, n),
+            dma(n),
+            dma(n),
+            dma(n),
+            dma(n),
+            dma(n),
+            dma(n),
+            dma(2, n),
+            dma(1),
+            dma(1),
+        ],
+        10**10,
+        low,
+        dg,
+        mid,
+        cot,
+        stat,
+        we,
+    )
 
 
 def adamw(gradient, moment, square, weight, clip_factor):
@@ -109,30 +654,9 @@
     return lax.psum(jnp.stack([jnp.sum(a, 1), jnp.sum(b, 1)]), "col")
 
 
-def norm(x):
-    sums = token_sums(x, x * x) / D
-    center, square = sums[0], sums[1]
-    inverse = lax.rsqrt(square - center * center + EPSILON)[:, None]
-    return (x - center[:, None]) * inverse, inverse
-
-
 def norm_back(normed, inverse, gradient):
     sums = token_sums(gradient, gradient * normed) / D
     return inverse * (gradient - sums[0][:, None] - normed * sums[1][:, None])
-
-
-def attention_forward(qkv, heads, real, rows):
-    t = qkv.shape[0]
-    parts = qkv.reshape(t, heads, 3, HD)
-    valid = (jnp.arange(t) % rows) < real
-    s = jnp.einsum("qhd,khd->hqk", parts[:, :, 0], parts[:, :, 1], preferred_element_type=F32)
-    s = jnp.where(valid[None, None], s * HD**-0.5, -1e30)
-    peak = jnp.max(s, axis=2, keepdims=True)
-    e = jnp.exp(s - peak)
-    total = jnp.sum(e, axis=2, keepdims=True)
-    p = (e / total).astype(BF)
-    o = jnp.einsum("hqk,khd->qhd", p, parts[:, :, 2], preferred_element_type=F32)
-    return o.astype(BF).reshape(t, heads * HD), peak + jnp.log(total)
 
 
 def attention_backward(qkv, lse, do, heads, real, rows):
@@ -178,28 +702,27 @@
     group_index = lax.axis_index("batch")
     present = jnp.any(seq_group == group_index).astype(F32)
 
-    x = lay.pack(image_input[0], text_input[0]).astype(F32)
-    cot = lay.pack(image_cotan[0], text_cotan[0]).astype(F32) * present
-    cb_all = row_gather(cot.astype(BF))
-
-    normed_one, inverse_one = norm(x)
-    a1_all = row_gather(normed_one.astype(BF))
-    qkv = col_reduce(lay.mm(a1_all, w_attend, dot), n_col).astype(BF)
-    o, lse = attention_forward(qkv, heads, lay.real, lay.rows)
-    o_all = col_gather(o, n_col)
-    middle = x + row_reduce(lay.mm(o_all, w_output, dot))
-    normed_two, inverse_two = norm(middle)
-    a2_all = row_gather(normed_two.astype(BF))
-    dact = col_reduce(lay.mm(cb_all, w_reduce, dot_nt), n_col)
-    hidden = col_reduce(lay.mm(a2_all, w_expand, dot), n_col)
-    act, gelu_pull = jax.vjp(partial(jax.nn.gelu, approximate=True), hidden)
-    dhidden = gelu_pull(dact)[0].astype(BF)
-    dh_all = col_gather(dhidden, n_col)
-    dn = row_reduce(lay.mm(dh_all, w_expand, dot_nt))
-    g_all = col_gather(act.astype(BF), n_col)
-    result = middle + row_reduce(lay.mm(g_all, w_reduce, dot))
-    grad_mid = cot + norm_back(normed_two, inverse_two, dn)
-    dy_all = row_gather(grad_mid.astype(BF))
+    low_x = lay.pack(image_input[0], text_input[0])
+    low_cot = (lay.pack(image_cotan[0], text_cotan[0]).astype(F32) * present).astype(BF)
+    x, cot = low_x.astype(F32), low_cot.astype(F32)
+    flat = n_row * lay.rows
+
+    a1_all, qkv, stat_one = attend(lay, low_x, w_attend)
+    o_all, lse, cb_all, dg, middle_x, low_two, stat_two = middle(
+        lay, qkv, low_x, low_cot, w_output, w_reduce
+    )
+    a2_all, act, dh_all, grad_mid, low_mid = hidden(
+        lay, low_two, dg, middle_x, low_cot, stat_two, w_expand
+    )
+    mean, inverse_one = moments(stat_one)
+    normed_one = (x - mean) * inverse_one
+    a1_all, qkv, o_all, cb_all, a2_all, act, dh_all = (
+        t.reshape(flat, -1) for t in (a1_all, qkv, o_all, cb_all, a2_all, act, dh_all)
+    )
+    lse = jnp.transpose(lse.reshape(flat, -1)[:, :heads])[:, :, None]
+    g_all = col_gather(act, n_col)
+    result = middle_x + row_reduce(lay.mm(g_all, w_reduce, dot))
+    dy_all = row_gather(low_mid)
     do = col_reduce(lay.mm(dy_all, w_output, dot_nt), n_col).astype(BF)
 
     g_red = lay.grad(g_all, cb_all)

time: 863 us -> 680 us (0.79)
  waiting for transfers between devices: 505 us -> 178 us
  Pallas kernels: 0 us -> 230 us
  other arithmetic: 111 us -> 74.4 us
  matrix products: 102 us -> 65.5 us
  blocking collectives: 60.5 us -> 44.5 us
    pallas_call x0 -> x3, Pallas kernels: none -> 230 us  [call(): pl.pallas_call(kernel, out_shape=[jax.ShapeDtypeStruct(s, t) for s, t in...]
    ppermute x8 -> x3, waiting for transfers between devices: 194 us -> 33.8 us  [col_swap(): return lax.ppermute(x, 'col', [(i, (i + 1) % n_col) for i in range(n_col)])]
    all_gather x4 -> x1, waiting for transfers between devices: 144 us -> 9.3 us  [row_gather(): return lax.all_gather(x, 'row', axis=0, tiled=True)]
    reduce_scatter x4 -> x2, waiting for transfers between devices: 133 us -> 7.53 us  [row_reduce(): lax.psum_scatter(x.astype(BF), 'row', scatter_dimension=0, tiled=True)]
    reduce_scatter x4, waiting for transfers between devices: 32.8 us -> 128 us  [batch_sum(): lax.psum_scatter(g.astype(BF), 'batch', scatter_dimension=1, tiled=True)]
    psum x4 -> x1, blocking collectives: 20.7 us -> 5.19 us  [token_sums(): return lax.psum(jnp.stack([jnp.sum(a, 1), jnp.sum(b, 1)]), 'col')]
    convert_element_type x5 -> x1, other arithmetic: 15.9 us -> 0.95 us  [on_device(): (lay.pack(image_cotan[0], text_cotan[0]).astype(F32) * present).astype(BF)]
    dot_general x8 -> x4, matrix products: 16.8 us -> 4.31 us  [dot_nt(): lax.dot_general(a, b, (((a.ndim - 1,), (1,)), ((), ())), preferred_elemen...]
  transfers between devices with their start and end apart: 20 -> 10, of which waited for: 16 -> 7; matrix products, arithmetic and copies ran while one was open for 17% -> 23% of each run, Pallas kernels for 0% -> 0%
where the time goes in v2:
time: 680 us; the launch traced here: 671 us
  Pallas kernels  230 us (34%)
  waiting for transfers between devices  178 us (26%)
  other arithmetic  74.4 us (11%)
  matrix products  65.5 us (10%)
  local copies, waits for them, and re-layouts  54 us (8%)
  blocking collectives  44.5 us (7%)
  between operations  20.2 us (3%)
    pallas_call x3, Pallas kernels, call(): pl.pallas_call(kernel, out_shape=[jax.ShapeDtypeStruct(s, t) for s, t in...  230 us
    reduce_scatter x4, waiting for transfers between devices, batch_sum(): lax.psum_scatter(g.astype(BF), 'batch', scatter_dimension=1, tiled=True)  128 us
    psum x1, blocking collectives, on_device(): grad_norm = jnp.sqrt(lax.psum(squares, ('batch', 'row', 'col')))  39.3 us
    ppermute x3, waiting for transfers between devices, col_swap(): return lax.ppermute(x, 'col', [(i, (i + 1) % n_col) for i in range(n_col)])  33.8 us
    unnamed x74, local copies, waits for them, and re-layouts  24.3 us
    mul x4, other arithmetic, adamw(): return (moment_new, square_new, -RATE * (corrected + DECAY * weight))  19.9 us
    dot_general x8, matrix products, dot_tn(): lax.dot_general(a, b, (((0,), (0,)), ((), ())), preferred_element_type=F32)  17.1 us
  transfers between devices with their start and end apart: 10, of which 7 were waited for; matrix products, arithmetic and copies ran while one was open for 23% of the time, Pallas kernels for 0%

profile of v2, /device:TPU:0, one launch (start us, length us, event | category | flops | bytes accessed | tf_op | source)
XLA Modules:
  0.0 671.1 jit_solution(13513607781523035905)
XLA Ops:
  9.3 1.9 maximum_maximum_fusion.x_ref
  11.2 53.0 %shard_map.328 = (bf16[4,304,768]{2,1,0:T(8,128)(2,1)}, bf16[4,304,576]{2,1,0:T(8,128)(2,1)}, f32[1,304,128]{2,1,0:T(8,128)}) custom-call(bf16[304,768]{1,0:T(8,128)(2,1)} %maximum_maximum_fusion.x_ref, bf16[2,768,1152]{2,1,0:T(8,128)(2,1)} %w_ref.1), custom_call_target="tpu_custom_call" | custom-call | flops 2151677952 | bytes 10000000 | tf_op jit(solution)/shard_map/pallas_call | solution.py:215
  65.2 71.2 %shard_map.329 = (bf16[4,304,384]{2,1,0:T(8,128)(2,1)}, f32[4,304,128]{2,1,0:T(8,128)}, bf16[4,304,768]{2,1,0:T(8,128)(2,1)}, f32[4,304,768]{2,1,0:T(8,128)}, f3...) custom-call(bf16[4,304,576]{2,1,0:T(8,128)(2,1)} %get-tuple-element.36.qkv_ref, ...), custom_call_target="tpu_custom_call" | custom-call | flops 10000000000 | bytes 10000000 | tf_op jit(solution)/shard_map/pallas_call | solution.py:215
  136.4 106.2 %shard_map.330 = (bf16[4,304,768]{2,1,0:T(8,128)(2,1)}, bf16[4,304,768]{2,1,0:T(8,128)(2,1)}, bf16[4,304,1536]{2,1,0:T(8,128)(2,1)}, f32[304,768]{1,0:T(8,128)}, bf16[304,768]{1,0:T(8,128)(2,1)}) custom-call(bf16[304,768]{1,0:T(8,128)(2,1)} %get-tuple-element.38.low_ref, f32[4,304,768]{2,1,0:T(8,128)} %get-tuple-element.39.dg_ref, ...), custom_call_target="tpu_custom_call" | custom-call | flops 10000000000 | bytes 10000000 | tf_op jit(solution)/shard_map/pallas_call | solution.py:215
  243.2 4.5 reshape.166
  247.7 9.9 %fusion.98 = (bf16[1216,3,1,64]{3,2,1,0:T(2,128)(2,1)}, bf16[1216,3,1,64]{3,2,1,0:T(2,128)(2,1)}, bf16[1216,3,1,64]{3,2,1,0:T(2,128)(2,1)S(1)}) fusion(bf16[1216,3,3,64]{3,2,1,0:T(4,128)(2,1)} %reshape.166), kind=kLoop, calls=%fused_computation.145 | loop fusion | bytes 2801664 | tf_op jit(solution)/shard_map/slice | solution.py:667
  257.6 4.7 copy.101
  262.3 3.7 copy.98
  266.0 2.7 copy.97
  269.0 5.4 maximum_select_fusion
  274.4 9.3 %all-gather.2.cloned.1.call-done = bf16[1216,768]{1,0:T(8,128)(2,1)} async-done(((bf16[304,768]{1,0:T(8,128)(2,1)}), bf16[1216,768]{1,0:T(8,128)(2,1)}) %all-gather.2.cloned.1.call-update) | async-done | bytes 1867792 | tf_op jit(solution)/shard_map/all_gather | solution.py:627
  285.1 2.5 fusion.53
  288.8 2.3 fusion.99
  292.1 5.7 fusion.39
  303.2 2.7 fusion.59
  307.3 2.9 constant_dynamic-slice_fusion.1
  310.2 2.7 copy.99
  312.9 2.0 collective-permute-done.1
  316.4 9.2 %fusion.74 = f32[3,1216,1216]{1,2,0:T(8,128)} fusion(bf16[1216,3,64]{0,2,1:T(8,128)(2,1)S(1)} %bitcast.173, bf16[1216,3,1,64]{0,3,1,2:T(8,128)(2,1)S(1)} %copy-done.15), kind=kOutput, calls=%fused_computation.112 | convolution fusion | flops 567803904 | bytes 18677760 | tf_op jit(solution)/shard_map/qhd,khd->hqk/dot_general | solution.py:670
  325.6 13.1 %multiply_reduce_fusion = (f32[3,1216]{1,0:T(4,128)S(1)}, f32[3,1216,1216]{1,2,0:T(8,128)}) fusion(f32[3,1216,1216]{1,2,0:T(8,128)} %fusion.74, f32[3,1216]{1,0:T(4,128)S(1)} %copy.72, bf16[1216,3,1,64]{0,3,1,2:T(8,128)(2,1)S(1)} %copy.97, bf16[1216,3,1,64]{0,3,1,2:T(8,128)(2,1)S(1)} %copy.98, pred[1216]{0:T(1024)(128)(4,1)S(1)} %fusion.86), kind=kOutput, calls=%fused_computation.3 | convolution fusion | flops 589980096 | bytes 36452032 | tf_op jit(solution)/shard_map/qhd,khd->hqk/dot_general | solution.py:668
  338.6 9.2 %fusion.17 = bf16[1216,3,1,64]{0,3,1,2:T(8,128)(2,1)S(1)} fusion(bf16[1216,3,64]{0,2,1:T(8,128)(2,1)S(1)} %bitcast.174, f32[3,1216,1216]{1,2,0:T(8,128)} %get-tuple-element.148), kind=kOutput, calls=%fused_computation.40 | convolution fusion | flops 572239872 | bytes 18677760 | tf_op jit(solution)/shard_map/hqk,qhd->khd/dot_general | solution.py:675
  347.8 12.8 %multiply_convert_fusion = bf16[3,1216,1216]{1,2,0:T(8,128)(2,1)S(1)} fusion(f32[3,1216,1216]{1,2,0:T(8,128)} %get-tuple-element.148, f32[3,1216,1216]{1,2,0:T(8,128)} %fusion.74, f32[3,1216]{1,0:T(4,128)S(1)} %get-tuple-element.147), kind=kLoop, calls=%fused_computation.2 | loop fusion | flops 13307904 | bytes 44374272 | tf_op jit(solution)/shard_map/convert_element_type | solution.py:672
  360.6 2.8 fusion.16
  366.7 31.8 %collective-permute-done.2 = bf16[1216,576]{0,1:T(8,128)(2,1)S(1)} collective-permute-done((bf16[1216,576]{0,1:T(8,128)(2,1)S(1)}, bf16[1216,576]{0,1:T(8,128)(2,1)S(1)}, u32[]{:S(2)}, u32[]{:S(2)}) %collective-permute-start.2) | collective-permute-done | bytes 1400864 | tf_op jit(solution)/shard_map/ppermute | solution.py:635
  400.9 2.6 copy.81
  403.5 2.6 copy.82
  410.2 2.3 fusion.36
  414.1 2.1 fusion.13
  417.0 2.9 fusion.7
  419.9 2.5 pad_maximum_fusion
  423.5 1.9 fusion.14
  425.7 3.2 fusion.10
  428.9 2.6 pad_maximum_fusion.1
  434.8 2.3 fusion.11
  437.2 2.2 pad_maximum_fusion.2
  445.4 7.5 %reduce-scatter.9.cloned.1.call-done = bf16[304,768]{1,0:T(8,128)(2,1)} async-done(((bf16[1216,768]{1,0:T(8,128)(2,1)}), bf16[304,768]{1,0:T(8,128)(2,1)}) %reduce-scatter.9.cloned.1.call-update) | async-done | bytes 466960 | tf_op jit(solution)/shard_map/reduce_scatter | solution.py:631
  454.5 5.2 psum.14
  462.2 40.4 %reduce-scatter.15.cloned.1.call-done = bf16[2,192,1536]{2,1,0:T(8,128)(2,1)} async-done(((bf16[2,768,1536]{2,1,0:T(8,128)(2,1)}), bf16[2,192,1536]{2,1,0:T(8,128)(2,1)}) %reduce-scatter.15.cloned.1.call-update) | async-done | bytes 1179664 | tf_op jit(solution)/shard_map/reduce_scatter | solution.py:738
  502.5 2.5 multiply_reduce_fusion.2
  505.0 47.8 %reduce-scatter.17.cloned.1.call-done = bf16[2,384,768]{2,1,0:T(8,128)(2,1)} async-done(((bf16[2,1536,768]{2,1,0:T(8,128)(2,1)}), bf16[2,384,768]{2,1,0:T(8,128)(2,1)}) %reduce-scatter.17.cloned.1.call-update) | async-done | bytes 1179664 | tf_op jit(solution)/shard_map/reduce_scatter | solution.py:738
  552.8 3.8 multiply_reduce_fusion.1
  556.6 39.4 %reduce-scatter.11.cloned.1.call-done = bf16[2,192,1152]{2,1,0:T(8,128)(2,1)} async-done(((bf16[2,768,1152]{2,1,0:T(8,128)(2,1)}), bf16[2,192,1152]{2,1,0:T(8,128)(2,1)}) %reduce-scatter.11.cloned.1.call-update) | async-done | bytes 884752 | tf_op jit(solution)/shard_map/reduce_scatter | solution.py:738
  596.0 3.4 multiply_reduce_fusion.3
  602.7 39.3 %psum.15 = f32[]{:T(128)} all-reduce(f32[]{:T(128)S(6)} %add.144), channel_id=1, replica_groups=mesh['batch'=4,'row'=4,'col'=2] {'batch','row','col'}, use_global_device_ids=true, to_apply=%region_15.16 | all-reduce | flops 1 | bytes 8 | tf_op jit(solution)/shard_map/psum | solution.py:742
  642.8 6.2 add_multiply_fusion.2
  649.0 5.7 add_multiply_fusion.1
  654.7 2.6 add_multiply_fusion.3
  657.3 5.4 add_multiply_fusion
  (130 shorter events, 42.6 us)
Async XLA Ops:
  7.2 276.5 %all-gather.2.cloned.1.call-start = ((), (), s32[]{:S(2)}) async-start(), calls=%async_computation.7 | async-start | bytes 2334720 | tf_op jit(solution)/shard_map/all_gather | solution.py:627
  11.2 53.0 %copy-start.25 = (bf16[1,256,768]{2,1,0:T(8,128)(2,1)S(1)}, bf16[1,256,768]{2,1,0:T(8,128)(2,1)}, u32[]{:S(2)}) copy-start(bf16[1,256,768]{2,1,0:T(8,128)(2,1)} %param.19) | copy-start | bytes 1179652
  11.2 53.0 %copy-start.28 = (bf16[1,38,768]{2,1,0:T(8,128)(2,1)S(1)}, bf16[1,38,768]{2,1,0:T(8,128)(2,1)}, u32[]{:S(2)}) copy-start(bf16[1,38,768]{2,1,0:T(8,128)(2,1)} %param.20) | copy-start | bytes 175108
  136.3 106.8 %copy-start.17 = (bf16[4,304,576]{2,1,0:T(8,128)(2,1)S(1)}, bf16[4,304,576]{2,1,0:T(8,128)(2,1)}, u32[]{:S(2)}) copy-start(bf16[4,304,576]{2,1,0:T(8,128)(2,1)} %get-tuple-element.36.qkv_ref) | copy-start | bytes 4202500
  242.6 198.0 %reduce-scatter.13.cloned.1.call-start = ((), (), s32[]{:S(2)}) async-start(), calls=%async_computation.10 | async-start | bytes 1474560 | tf_op jit(solution)/shard_map/reduce_scatter | solution.py:738
  243.1 25.9 %collective-permute-start = (bf16[1216,768]{1,0:T(8,128)(2,1)}, bf16[1216,768]{1,0:T(8,128)(2,1)}, u32[]{:S(2)}, u32[]{:S(2)}) collective-permute-start(bf16[1216,768]{1,0:T(8,128)(2,1)} %bitcast.178), channel_id=1, source_target_pairs={{0,1},{1,0},{2,3},{3,2},{4,5},{5,4},{6,7},{7,6},{8,9},{9,8},{10,11... | collective-permute-start | bytes 5603336 | tf_op jit(solution)/shard_map/ppermute | solution.py:635
  262.3 6.3 copy-start.19
  288.8 153.6 %reduce-scatter.7.cloned.1.call-start = ((), (), s32[]{:S(2)}) async-start(), calls=%async_computation.6 | async-start | bytes 2334720 | tf_op jit(solution)/shard_map/reduce_scatter | solution.py:631
  291.1 6.6 copy-start.2
  292.1 5.7 copy-start.27
  292.1 5.7 copy-start.29
  299.2 1.2 copy-start.4
  301.7 4.1 copy-start.16
  301.7 13.2 %collective-permute-start.1 = (bf16[1216,192]{0,1:T(8,128)(2,1)}, bf16[1216,192]{0,1:T(8,128)(2,1)}, u32[]{:S(2)}, u32[]{:S(2)}) collective-permute-start(bf16[1216,192]{0,1:T(8,128)(2,1)} %copy.100), channel_id=1, source_target_pairs={{0,1},{1,0},{2,3},{3,2},{4,5},{5,4},{6,7},{7,6},{8,9},{9,8},{10,11... | collective-permute-start | bytes 1400840 | tf_op jit(solution)/shard_map/ppermute | solution.py:635
  307.3 145.7 %reduce-scatter.9.cloned.1.call-start = ((), (), s32[]{:S(2)}) async-start(), calls=%async_computation.8 | async-start | bytes 2334720 | tf_op jit(solution)/shard_map/reduce_scatter | solution.py:631
  310.2 6.1 copy-start.15
  365.3 33.2 %collective-permute-start.2 = (bf16[1216,576]{0,1:T(8,128)(2,1)S(1)}, bf16[1216,576]{0,1:T(8,128)(2,1)S(1)}, u32[]{:S(2)}, u32[]{:S(2)}) collective-permute-start(bf16[1216,576]{0,1:T(8,128)(2,1)S(1)} %bitcast.171), channel_id=1, source_target_pairs={{0,1},{1,0},{2,3},{3,2},{4,5},{5,4},{6,7},{7,6},{8,9},{9,8},{10,11... | collective-permute-start | bytes 4202504 | tf_op jit(solution)/shard_map/ppermute | solution.py:635
  406.1 2.2 copy-start.26
  408.3 1.4 copy-start.5
  408.3 1.9 copy-start.7
  413.8 88.7 %reduce-scatter.15.cloned.1.call-start = ((), (), s32[]{:S(2)}) async-start(), calls=%async_computation.11 | async-start | bytes 5898240 | tf_op jit(solution)/shard_map/reduce_scatter | solution.py:738
  414.1 2.3 copy-start.30
  414.1 2.9 copy-start.33
  422.5 1.1 copy-start.23
  422.5 130.3 %reduce-scatter.17.cloned.1.call-start = ((), (), s32[]{:S(2)}) async-start(), calls=%async_computation.12 | async-start | bytes 5898240 | tf_op jit(solution)/shard_map/reduce_scatter | solution.py:738
  423.5 2.0 copy-start.3
  423.5 2.2 copy-start.32
  431.5 1.5 copy-start.31
  431.5 164.5 %reduce-scatter.11.cloned.1.call-start = ((), (), s32[]{:S(2)}) async-start(), calls=%async_computation.9 | async-start | bytes 4423680 | tf_op jit(solution)/shard_map/reduce_scatter | solution.py:738
  433.0 1.4 copy-start.6
  433.0 1.9 copy-start.8
  439.4 0.9 copy-start.20
  439.4 13.5 %copy-start.9 = (bf16[1,256,768]{2,1,0:T(8,128)(2,1)S(1)}, bf16[1,256,768]{2,1,0:T(8,128)(2,1)}, u32[]{:S(2)}) copy-start(bf16[1,256,768]{2,1,0:T(8,128)(2,1)} %param.17) | copy-start | bytes 1179652
  439.4 13.5 %copy-start.24 = (bf16[1,38,768]{2,1,0:T(8,128)(2,1)S(1)}, bf16[1,38,768]{2,1,0:T(8,128)(2,1)}, u32[]{:S(2)}) copy-start(bf16[1,38,768]{2,1,0:T(8,128)(2,1)} %param.18) | copy-start | bytes 175108
  440.5 19.2 %copy-start.18 = (f32[304,768]{1,0:T(8,128)S(1)}, f32[304,768]{1,0:T(8,128)}, u32[]{:S(2)}) copy-start(f32[304,768]{1,0:T(8,128)} %get-tuple-element.42) | copy-start | bytes 2801668
  442.4 212.3 %copy-start.10 = (f32[2,96,768]{2,1,0:T(8,128)}, f32[2,96,768]{2,1,0:T(8,128)S(1)}, u32[]{:S(2)}) copy-start(f32[2,96,768]{2,1,0:T(8,128)S(1)} %get-tuple-element.137) | copy-start | bytes 1769476
  505.0 143.9 %copy-start = (f32[2,192,1536]{2,1,0:T(8,128)}, f32[2,192,1536]{2,1,0:T(8,128)S(1)}, u32[]{:S(2)}) copy-start(f32[2,192,1536]{2,1,0:T(8,128)S(1)} %get-tuple-element.135) | copy-start | bytes 7077892
  642.7 6.2 copy-start.11
  642.7 6.2 copy-start.12
  649.0 5.8 copy-start.21
  649.0 5.8 copy-start.22
  649.0 8.4 %copy-start.13 = (f32[2,384,768]{2,1,0:T(8,128)S(1)}, f32[2,384,768]{2,1,0:T(8,128)}, u32[]{:S(2)}) copy-start(f32[2,384,768]{2,1,0:T(8,128)} %param.33) | copy-start | bytes 7077892
  649.0 8.3 %copy-start.14 = (f32[2,384,768]{2,1,0:T(8,128)S(1)}, f32[2,384,768]{2,1,0:T(8,128)}, u32[]{:S(2)}) copy-start(f32[2,384,768]{2,1,0:T(8,128)} %param.29) | copy-start | bytes 7077892
  654.7 2.6 copy-start.1
Sparse Core Ops, SparseCore 0:
  242.7 40.9 all-gather.1
  288.9 24.5 reduce-scatter.12
  316.5 39.9 reduce-scatter.6
  413.9 38.9 reduce-scatter.8
  455.5 46.9 reduce-scatter.14
  504.9 47.8 reduce-scatter.16
  555.5 40.4 reduce-scatter.10

commit v3 on v2

--- a/solution.py
+++ b/solution.py
@@ -11,6 +11,7 @@
 D = 1536
 HD = 64
 STEP = 10
+STRIPE = 512
 
 EPSILON = 1e-06
 BETA_ONE = 0.9
@@ -56,7 +57,7 @@
     return jnp.where(j <= 2 * reach, alternate, beyond)
 
 
-def greet(n):
+def greet(n, fused=False):
     z, c = lax.axis_index("row"), lax.axis_index("col")
     barrier = pltpu.get_barrier_semaphore()
     pl.semaphore_signal(barrier, inc=1, device_id={"col": 1 - c}, device_id_type=MESH)
@@ -69,8 +70,12 @@
     def _():
         pl.semaphore_signal(barrier, inc=1, device_id={"row": z + 1}, device_id_type=MESH)
 
+    if fused:
+        b = lax.axis_index("batch")
+        for other in (b + 1 - 2 * (b % 2), (b + 2) % 4):
+            pl.semaphore_signal(barrier, inc=1, device_id={"batch": other}, device_id_type=MESH)
     ends = jnp.where(z > 0, 1, 0) + jnp.where(z < n - 1, 1, 0)
-    pl.semaphore_wait(barrier, 1 + ends)
+    pl.semaphore_wait(barrier, ends + (3 if fused else 1))
 
 
 class Gather:
@@ -124,31 +129,30 @@
         self.z = lax.axis_index("row")
 
     def copy(self, o):
-        way = jnp.where(o > self.z, 0, 1)
+        slot = jnp.where(o > self.z, o + 1, o)
         there = (self.z + jnp.where(o > self.z, 1, -1) + self.n) % self.n
         return remote(
-            self.out.at[o], self.inbox.at[way, o], self.send.at[o], self.recv.at[way, o], row=there
+            self.out.at[o], self.inbox.at[slot], self.send.at[o], self.recv.at[slot], row=there
         )
 
-    def wait_in(self, way, o):
+    def take(self, slot):
         remote(
-            self.out.at[o],
-            self.inbox.at[way, o],
-            self.send.at[o],
-            self.recv.at[way, o],
+            self.out.at[0],
+            self.inbox.at[slot],
+            self.send.at[0],
+            self.recv.at[slot],
             row=(self.z + 1) % self.n,
         ).wait_recv()
+        self.acc[...] += self.inbox[slot].astype(F32)
 
     def add(self, o):
         @pl.when((o >= self.z) & (self.z > 0))
         def _():
-            self.wait_in(0, o)
-            self.acc[...] += self.inbox[0, o].astype(F32)
+            self.take(o + 1)
 
         @pl.when((o <= self.z) & (self.z < self.n - 1))
         def _():
-            self.wait_in(1, o)
-            self.acc[...] += self.inbox[1, o].astype(F32)
+            self.take(o)
 
         @pl.when(o != self.z)
         def _():
@@ -428,7 +432,7 @@
             pltpu.VMEM((n, r, hid), BF),
             pltpu.VMEM((r, d), F32),
             pltpu.VMEM((n, r, d), BF),
-            pltpu.VMEM((2, n, r, d), BF),
+            pltpu.VMEM((n + 1, r, d), BF),
             pltpu.VMEM((1, r, 128), F32),
             dma(2, n),
             dma(n),
@@ -437,7 +441,7 @@
             dma(n),
             dma(n),
             dma(n),
-            dma(2, n),
+            dma(n + 1),
             dma(1),
             dma(1),
         ],
@@ -552,7 +556,7 @@
             pltpu.VMEM((n, r, hid), BF),
             pltpu.VMEM((r, d), F32),
             pltpu.VMEM((n, r, d), BF),
-            pltpu.VMEM((2, n, r, d), BF),
+            pltpu.VMEM((n + 1, r, d), BF),
             pltpu.VMEM((1, r, 128), F32),
             pltpu.VMEM((1, r, 128), F32),
             dma(2, n),
@@ -562,7 +566,7 @@
             dma(n),
             dma(n),
             dma(n),
-            dma(2, n),
+            dma(n + 1),
             dma(1),
             dma(1),
         ],
@@ -576,6 +580,429 @@
     )
 
 
+class BatchSum:
+    def __init__(self, local, first, out, second, sems):
+        self.local, self.first, self.out, self.second = local, first, out, second
+        self.f_send, self.f_recv, self.s_send, self.s_recv = sems
+        b = lax.axis_index("batch")
+        self.x, self.core = b // 2, b % 2
+        self.to_core, self.to_x = 2 * self.x + 1 - self.core, 2 * (1 - self.x) + self.core
+        self.s = out.shape[1]
+
+    def rows(self, block):
+        return pl.ds(pl.multiple_of(block * self.s, 16), self.s)
+
+    def core_copy(self, q):
+        block = 2 * q + 1 - self.core
+        return remote(
+            self.local.at[:, self.rows(block), :],
+            self.first.at[q],
+            self.f_send.at[q],
+            self.f_recv.at[q],
+            batch=self.to_core,
+        )
+
+    def x_copy(self):
+        return remote(self.out, self.second, self.s_send.at[0], self.s_recv.at[0], batch=self.to_x)
+
+    def start(self):
+        self.core_copy(1 - self.x).start()
+        self.core_copy(self.x).start()
+
+    def block(self, q):
+        self.core_copy(q).wait_recv()
+        mine = self.local[:, self.rows(2 * q + self.core), :].astype(F32)
+        return mine + self.first[q].astype(F32)
+
+    def pass_on(self):
+        self.out[...] = self.block(1 - self.x).astype(BF)
+        self.x_copy().start()
+
+    def total(self):
+        near = self.block(self.x)
+        self.x_copy().wait_recv()
+        return near + self.second[...].astype(F32)
+
+    def finish(self):
+        self.core_copy(0).wait_send()
+        self.core_copy(1).wait_send()
+        self.x_copy().wait_send()
+
+
+def batch_scratch(rows, cols):
+    s = rows // 4
+    return [
+        pltpu.VMEM((2, rows, cols), BF),
+        pltpu.VMEM((2, 2, s, cols), BF),
+        pltpu.VMEM((2, s, cols), BF),
+        pltpu.VMEM((2, s, cols), BF),
+        dma(2),
+        dma(2),
+        dma(1),
+        dma(1),
+    ]
+
+
+def batch_of(scratch):
+    return BatchSum(*scratch[:4], scratch[4:])
+
+
+def transpose_rows(lay, left, turned):
+    n, img, far = lay.n_row, lay.img, lay.n_row * lay.img
+    for k in range(n):
+        turned[:, k * img : (k + 1) * img] = left[k, :img, :].T
+    turned[:, far:] = jnp.concatenate([left[k, img:, :] for k in range(n)], 0).T
+
+
+def weight_gradient(lay, turned, right, local, part, cols):
+    n, img, far = lay.n_row, lay.img, lay.n_row * lay.img
+    if part == 0:
+        total = dot(turned[:, :img], right[0, :img, cols])
+        for k in range(1, n):
+            total += dot(turned[:, k * img : (k + 1) * img], right[k, :img, cols])
+    else:
+        text = jnp.concatenate([right[k, img:, cols] for k in range(n)], 0)
+        total = dot(turned[:, far:], text)
+    local[part, :, cols] = total.astype(BF)
+
+
+def pull_kernel(
+    lay, fused, low_ref, qkv_ref, lse_ref, wo_ref, act_ref, wr_ref, mid_ref, a2_ref, dh_ref, full_ref, dqkv_ref, g_ref, res_ref, exp_ref, *scratch
+):
+    (
+        q_s, k_s, v_s, do_own, do_out, do_in, do_s, dq_s, dk_s, dv_s, acc, r_out, inbox, turned,
+        g_send, g_recv, s_send, s_recv, a_send, a_recv, r_send, r_recv,
+    ) = scratch[:22]
+    n, img, txt, far = lay.n_row, lay.img, lay.txt_pad, lay.n_row * lay.img
+    z, c = lax.axis_index("row"), lax.axis_index("col")
+    heads, half, hid = q_s.shape[0], do_own.shape[2], act_ref.shape[2]
+    mine = pl.ds(pl.multiple_of(c * half, 16), half)
+    theirs = pl.ds(pl.multiple_of((1 - c) * half, 16), half)
+    my_act = pl.ds(pl.multiple_of(c * hid, 128), hid)
+    their_act = pl.ds(pl.multiple_of((1 - c) * hid, 128), hid)
+    greet(n, fused)
+    gather = Gather(full_ref, g_send, g_recv, n)
+    full_ref[z] = low_ref[...]
+    gather.push(z)
+    swap = Swap(do_out, do_in, s_send, s_recv)
+    reduce = Reduce(acc, r_out, inbox, r_send, r_recv, n)
+    local = exp_ref
+    if fused:
+        batch = batch_of(scratch[22:])
+        local = batch.local
+    split_heads(lay, qkv_ref, q_s, k_s, v_s, False)
+    bias = text_bias(lay)
+    dk_s[...] = jnp.zeros_like(dk_s)
+    dv_s[...] = jnp.zeros_like(dv_s)
+    lag = jnp.minimum(z, n - 1 - z)
+
+    def act_copy(k, where):
+        return remote(act_ref.at[k], g_ref.at[k, :, where], a_send.at[k], a_recv.at[k], col=1 - c)
+
+    def arrive(k):
+        gather.arrive_after_own(k)
+        for part, rows in parts_of(lay):
+            do_out[k, rows] = dot_nt(full_ref[k, rows], wo_ref[part, theirs, :]).astype(BF)
+        swap.start(k)
+        for part, rows in parts_of(lay):
+            do_own[k, rows] = dot_nt(full_ref[k, rows], wo_ref[part, mine, :])
+
+    def expand_gradient():
+        transpose_rows(lay, a2_ref, turned)
+
+        @pl.loop(0, 2 * hid // STRIPE)
+        def _(i):
+            cols = pl.ds(pl.multiple_of(i * STRIPE, 128), STRIPE)
+            for part in range(2):
+                weight_gradient(lay, turned, dh_ref, local, part, cols)
+
+    def attention(k):
+        swap.arrive(k)
+        do_s[...] = (do_own[k] + do_in[k].astype(F32)).astype(BF)
+        for h in range(heads):
+            q, do = q_s[h, k], do_s[:, h * HD : (h + 1) * HD]
+            lse = lse_ref[k, :, h : h + 1]
+            p1 = jnp.exp(dot_nt(q, k_s[h, :far]) - lse)
+            p2 = jnp.exp(dot_nt(q, k_s[h, far:]) + bias - lse)
+            dp1 = dot_nt(do, v_s[h, :far])
+            dp2 = dot_nt(do, v_s[h, far:])
+            row = jnp.sum(p1 * dp1, axis=1, keepdims=True) + jnp.sum(
+                p2 * dp2, axis=1, keepdims=True
+            )
+            ds1 = (p1 * (dp1 - row)).astype(BF)
+            ds2 = (p2 * (dp2 - row)).astype(BF)
+            dq_s[h, k] = dot(ds1, k_s[h, :far]) + dot(ds2, k_s[h, far:])
+            dk_s[h, :, :far] += dot_tn(q, ds1)
+            dk_s[h, :, far:] += dot_tn(q, ds2)
+            dv_s[h, :, :far] += dot_tn(do, p1.astype(BF))
+            dv_s[h, :, far:] += dot_tn(do, p2.astype(BF))
+
+    def down(k):
+        act_copy(k, their_act).wait_recv()
+        g_ref[k, :, my_act] = act_ref[k]
+        for part, rows in parts_of(lay):
+            acc[rows] = dot(g_ref[k, rows], wr_ref[part])
+        reduce.add(k)
+
+    @pl.loop(0, n + 1 + (n - 1) // 2)
+    def _(j):
+        @pl.when(j < n)
+        def _():
+            arrive(near_first(z, n, j))
+            act_copy(near_first(z, n, n - 1 - j), my_act).start()
+
+        @pl.when(j == 0)
+        def _():
+            expand_gradient()
+            if fused:
+                batch.start()
+
+        if fused:
+
+            @pl.when(j == 1)
+            def _():
+                batch.pass_on()
+
+        @pl.when((j > 0) & (j <= n))
+        def _():
+            attention(near_first(z, n, j - 1))
+
+        i = j - 1 - lag
+
+        @pl.when((i >= 0) & (i < n))
+        def _():
+            down(near_first(z, n, n - 1 - i))
+
+    res_ref[...] = (mid_ref[...] + acc[...]).astype(BF)
+    for k in range(n):
+        for h in range(heads):
+            at = h * 3 * HD
+            for rows, first, count in (
+                (slice(0, img), k * img, img),
+                (slice(img, lay.rows), far + k * txt, txt),
+            ):
+                dk = dk_s[h, :, first : first + count].T
+                dv = dv_s[h, :, first : first + count].T
+                dq = dq_s[h, k, rows] * HD**-0.5
+                dqkv_ref[k, rows, at : at + 3 * HD] = jnp.concatenate([dq, dk, dv], 1).astype(BF)
+    if fused:
+        exp_ref[...] = batch.total()
+        batch.finish()
+    gather.finish()
+    swap.finish(n)
+    reduce.finish()
+
+    @pl.loop(0, n)
+    def _(k):
+        act_copy(k, my_act).wait_send()
+
+
+def pull(lay, fused, low, qkv, lse, wo, act, wr, mid, a2, dh):
+    n, r, d, hid = lay.n_row, lay.rows, low.shape[1], act.shape[2]
+    heads = qkv.shape[2] // (3 * HD)
+    keys = n * r
+    return call(
+        partial(pull_kernel, lay, fused),
+        4,
+        [
+            ((n, r, d), BF),
+            ((n, r, 3 * heads * HD), BF),
+            ((n, r, 2 * hid), BF),
+            ((r, d), BF),
+            ((2, d // 4, 2 * hid), F32) if fused else ((2, d, 2 * hid), BF),
+        ],
+        [
+            pltpu.VMEM((heads, n, r, HD), BF),
+            pltpu.VMEM((heads, keys, HD), BF),
+            pltpu.VMEM((heads, keys, HD), BF),
+            pltpu.VMEM((n, r, heads * HD), F32),
+            pltpu.VMEM((n, r, heads * HD), BF),
+            pltpu.VMEM((n, r, heads * HD), BF),
+            pltpu.VMEM((r, heads * HD), BF),
+            pltpu.VMEM((heads, n, r, HD), F32),
+            pltpu.VMEM((heads, HD, keys), F32),
+            pltpu.VMEM((heads, HD, keys), F32),
+            pltpu.VMEM((r, d), F32),
+            pltpu.VMEM((n, r, d), BF),
+            pltpu.VMEM((n + 1, r, d), BF),
+            pltpu.VMEM((d, keys), BF),
+            dma(2, n),
+            dma(n),
+            dma(n),
+            dma(n),
+            dma(n),
+            dma(n),
+            dma(n),
+            dma(n + 1),
+            *(batch_scratch(d, 2 * hid) if fused else []),
+        ],
+        10**10,
+        low,
+        qkv,
+        lse,
+        wo,
+        act,
+        wr,
+        mid,
+        a2,
+        dh,
+    )
+
+
+def input_kernel(
+    lay, fused, dqkv_ref, x_ref, dmid_ref, stat_ref, wa_ref, a1_ref, o_ref, dy_ref, g_ref, cb_ref, dx_ref, att_ref, out_ref, red_ref, *scratch
+):
+    (
+        full, into, acc, r_out, inbox, stat_out, stat_in, turned, turned_g,
+        s_send, s_recv, r_send, r_recv, t_send, t_recv,
+    ) = scratch[:15]
+    n = lay.n_row
+    z, c = lax.axis_index("row"), lax.axis_index("col")
+    half, d = dqkv_ref.shape[2], x_ref.shape[1]
+    greet(n, fused)
+    swap = Swap(dqkv_ref, into, s_send, s_recv)
+    reduce = Reduce(acc, r_out, inbox, r_send, r_recv, n)
+    own, other, red, out = (scratch[15 + 8 * i : 23 + 8 * i] for i in range(4)) if fused else (
+        scratch[15:16], scratch[16:17], (red_ref,), (out_ref,)
+    )
+    sums = [batch_of(s) for s in (own, other, red, out)] if fused else []
+
+    @pl.loop(0, n)
+    def _(j):
+        swap.start(near_first(z, n, n - 1 - j))
+
+    def gradient(turned, right, local, stripe):
+        if stripe == right.shape[2]:
+            for part in range(2):
+                weight_gradient(lay, turned, right, local, part, slice(0, stripe))
+            return
+
+        @pl.loop(0, right.shape[2] // stripe)
+        def _(i):
+            cols = pl.ds(pl.multiple_of(i * stripe, 128), stripe)
+            for part in range(2):
+                weight_gradient(lay, turned, right, local, part, cols)
+
+    transpose_rows(lay, a1_ref, turned)
+    gradient(turned, dqkv_ref, own[0], half)
+    if fused:
+        sums[0].start()
+    transpose_rows(lay, g_ref, turned_g)
+    gradient(turned_g, cb_ref, red[0], STRIPE // 2)
+    if fused:
+        sums[2].start()
+        sums[0].pass_on()
+    lag = jnp.minimum(z, n - 1 - z)
+
+    @pl.loop(0, n + (n - 1) // 2)
+    def _(j):
+        i = j - lag
+
+        @pl.when((i >= 0) & (i < n))
+        def _():
+            k = near_first(z, n, n - 1 - i)
+            swap.arrive(k)
+            mine, theirs = dqkv_ref[k], into[k]
+            full[...] = jnp.concatenate(
+                [jnp.where(c == 0, mine, theirs), jnp.where(c == 0, theirs, mine)], 1
+            )
+            for part, rows in parts_of(lay):
+                acc[rows] = dot_nt(full[rows], wa_ref[part])
+            reduce.add(k)
+
+        if fused:
+
+            @pl.when(j == 0)
+            def _():
+                sums[2].pass_on()
+
+        @pl.when(j == 2)
+        def _():
+            turned_o = turned_g.at[: o_ref.shape[2]]
+            transpose_rows(lay, o_ref, turned_o)
+            gradient(turned_o, dy_ref, out[0], d)
+            if fused:
+                sums[3].start()
+
+    gradient(turned, into, other[0], half)
+    if fused:
+        sums[1].start()
+        sums[3].pass_on()
+    mean, inverse = moments(stat_ref)
+    normed = (x_ref[...].astype(F32) - mean) * inverse
+    grad = acc[...]
+    stat_out[0] = sums_of(grad, grad * normed)
+    exchange(stat_out, stat_in, t_send, t_recv)
+    back_one, back_two = stat_out[0, :, 0:1] / D, stat_out[0, :, 1:2] / D
+    dx_ref[...] = dmid_ref[...] + inverse * (grad - back_one - normed * back_two)
+    if fused:
+        sums[1].pass_on()
+        red_ref[...] = sums[2].total()
+        out_ref[...] = sums[3].total()
+        mine, theirs = sums[0].total(), sums[1].total()
+    else:
+        mine, theirs = own[0][...], other[0][...]
+    att_ref[...] = jnp.concatenate(
+        [jnp.where(c == 0, mine, theirs), jnp.where(c == 0, theirs, mine)], 2
+    )
+    for total in sums:
+        total.finish()
+    swap.finish(n)
+    reduce.finish()
+
+
+def inputs_back(lay, fused, dqkv, x, dmid, stat, wa, a1, o, dy, g, cb):
+    n, r, d, half = lay.n_row, lay.rows, x.shape[1], dqkv.shape[2]
+    keys = n * r
+    shapes = [(d, 2 * half), (o.shape[2], d), (g.shape[2], d)]
+    return call(
+        partial(input_kernel, lay, fused),
+        5,
+        [
+            ((r, d), F32),
+            *[((2, s[0] // 4, s[1]), F32) if fused else ((2, *s), BF) for s in shapes],
+        ],
+        [
+            pltpu.VMEM((r, 2 * half), BF),
+            pltpu.VMEM((n, r, half), BF),
+            pltpu.VMEM((r, d), F32),
+            pltpu.VMEM((n, r, d), BF),
+            pltpu.VMEM((n + 1, r, d), BF),
+            pltpu.VMEM((1, r, 128), F32),
+            pltpu.VMEM((1, r, 128), F32),
+            pltpu.VMEM((d, keys), BF),
+            pltpu.VMEM((g.shape[2], keys), BF),
+            dma(n),
+            dma(n),
+            dma(n),
+            dma(n + 1),
+            dma(1),
+            dma(1),
+            *(
+                [
+                    *batch_scratch(d, half),
+                    *batch_scratch(d, half),
+                    *batch_scratch(g.shape[2], d),
+                    *batch_scratch(o.shape[2], d),
+                ]
+                if fused
+                else [pltpu.VMEM((2, d, half), BF)] * 2
+            ),
+        ],
+        10**10,
+        dqkv,
+        x,
+        dmid,
+        stat,
+        wa,
+        a1,
+        o,
+        dy,
+        g,
+        cb,
+    )
+
+
 def adamw(gradient, moment, square, weight, clip_factor):
     clipped = gradient * clip_factor
     moment_new = BETA_ONE * moment + (1.0 - BETA_ONE) * clipped
@@ -606,77 +1033,8 @@
             [image, text, jnp.zeros((self.txt_pad - self.txt, image.shape[1]), image.dtype)], 0
         )
 
-    def mm(self, full, w, f):
-        full = full.reshape(self.n_row, self.rows, -1)
-        one = f(full[:, : self.img], w[0])
-        two = f(full[:, self.img :], w[1])
-        return jnp.concatenate([one, two], 1).reshape(self.n_row * self.rows, -1)
-
-    def grad(self, left, right):
-        left = left.reshape(self.n_row, self.rows, -1)
-        right = right.reshape(self.n_row, self.rows, -1)
-        parts = []
-        for part in (slice(0, self.img), slice(self.img, self.rows)):
-            a = left[:, part].reshape(-1, left.shape[2])
-            b = right[:, part].reshape(-1, right.shape[2])
-            parts.append(dot_tn(a, b))
-        return jnp.stack(parts)
-
-
-def row_gather(x):
-    return lax.all_gather(x, "row", axis=0, tiled=True)
-
-
-def row_reduce(x):
-    return lax.psum_scatter(x.astype(BF), "row", scatter_dimension=0, tiled=True).astype(F32)
-
-
-def col_swap(x, n_col):
-    return lax.ppermute(x, "col", [(i, (i + 1) % n_col) for i in range(n_col)])
-
-
-def col_reduce(x, n_col):
-    c = lax.axis_index("col")
-    half = x.shape[1] // 2
-    mine = lax.dynamic_slice_in_dim(x, c * half, half, 1)
-    other = lax.dynamic_slice_in_dim(x, (1 - c) * half, half, 1).astype(BF)
-    return mine + col_swap(other, n_col).astype(F32)
-
-
-def col_gather(x, n_col):
-    c = lax.axis_index("col")
-    other = col_swap(x, n_col)
-    both = jnp.where(c == 0, jnp.stack([x, other]), jnp.stack([other, x]))
-    return jnp.concatenate([both[0], both[1]], 1)
-
-
-def token_sums(a, b):
-    return lax.psum(jnp.stack([jnp.sum(a, 1), jnp.sum(b, 1)]), "col")
-
-
-def norm_back(normed, inverse, gradient):
-    sums = token_sums(gradient, gradient * normed) / D
-    return inverse * (gradient - sums[0][:, None] - normed * sums[1][:, None])
-
-
-def attention_backward(qkv, lse, do, heads, real, rows):
-    t = qkv.shape[0]
-    parts = qkv.reshape(t, heads, 3, HD)
-    do = do.reshape(t, heads, HD)
-    valid = (jnp.arange(t) % rows) < real
-    q, k, v = parts[:, :, 0], parts[:, :, 1], parts[:, :, 2]
-    s = jnp.einsum("qhd,khd->hqk", q, k, preferred_element_type=F32) * HD**-0.5
-    p = jnp.where(valid[None, None], jnp.exp(s - lse), 0.0)
-    dp = jnp.einsum("qhd,khd->hqk", do, v, preferred_element_type=F32)
-    row_dot = jnp.sum(p * dp, axis=2, keepdims=True)
-    ds = (p * (dp - row_dot)).astype(BF)
-    dq = jnp.einsum("hqk,khd->qhd", ds, k, preferred_element_type=F32) * HD**-0.5
-    dk = jnp.einsum("hqk,qhd->khd", ds, q, preferred_element_type=F32) * HD**-0.5
-    dv = jnp.einsum("hqk,qhd->khd", p.astype(BF), do, preferred_element_type=F32)
-    return jnp.stack([dq, dk, dv], 2).astype(BF).reshape(t, heads * 3 * HD)
-
-
-def on_device(n_row, n_col, *args):
+
+def on_device(n_batch, n_row, *args):
     (
         image_input,
         text_input,
@@ -698,14 +1056,12 @@
     ) = args
     img, txt = image_input.shape[1], text_input.shape[1]
     lay = Layout(n_row, img, txt)
-    heads = w_attend.shape[2] // (3 * HD) // n_col
     group_index = lax.axis_index("batch")
     present = jnp.any(seq_group == group_index).astype(F32)
 
     low_x = lay.pack(image_input[0], text_input[0])
     low_cot = (lay.pack(image_cotan[0], text_cotan[0]).astype(F32) * present).astype(BF)
-    x, cot = low_x.astype(F32), low_cot.astype(F32)
-    flat = n_row * lay.rows
+    fused = n_batch == 4
 
     a1_all, qkv, stat_one = attend(lay, low_x, w_attend)
     o_all, lse, cb_all, dg, middle_x, low_two, stat_two = middle(
@@ -714,32 +1070,19 @@
     a2_all, act, dh_all, grad_mid, low_mid = hidden(
         lay, low_two, dg, middle_x, low_cot, stat_two, w_expand
     )
-    mean, inverse_one = moments(stat_one)
-    normed_one = (x - mean) * inverse_one
-    a1_all, qkv, o_all, cb_all, a2_all, act, dh_all = (
-        t.reshape(flat, -1) for t in (a1_all, qkv, o_all, cb_all, a2_all, act, dh_all)
-    )
-    lse = jnp.transpose(lse.reshape(flat, -1)[:, :heads])[:, :, None]
-    g_all = col_gather(act, n_col)
-    result = middle_x + row_reduce(lay.mm(g_all, w_reduce, dot))
-    dy_all = row_gather(low_mid)
-    do = col_reduce(lay.mm(dy_all, w_output, dot_nt), n_col).astype(BF)
-
-    g_red = lay.grad(g_all, cb_all)
-    g_exp = lay.grad(a2_all, dh_all)
-    g_out = lay.grad(o_all, dy_all)
-    dqkv = attention_backward(qkv, lse, do, heads, lay.real, lay.rows)
-    dqkv_all = col_gather(dqkv, n_col)
-    g_att = lay.grad(a1_all, dqkv_all)
-    da = row_reduce(lay.mm(dqkv_all, w_attend, dot_nt))
-    grad_in = grad_mid + norm_back(normed_one, inverse_one, da)
-
-    def batch_sum(g):
-        return lax.psum_scatter(g.astype(BF), "batch", scatter_dimension=1, tiled=True).astype(F32)
-
-    sums = [batch_sum(g) for g in (g_att, g_out, g_exp, g_red)]
+    dy_all, dqkv, g_all, result, g_exp = pull(
+        lay, fused, low_mid, qkv, lse, w_output, act, w_reduce, middle_x, a2_all, dh_all
+    )
+    grad_in, g_att, g_out, g_red = inputs_back(
+        lay, fused, dqkv, low_x, grad_mid, stat_one, w_attend, a1_all, o_all, dy_all, g_all, cb_all
+    )
+    sums = [g_att, g_out, g_exp, g_red]
+    if not fused:
+        sums = [
+            lax.psum_scatter(g, "batch", scatter_dimension=1, tiled=True).astype(F32) for g in sums
+        ]
     squares = sum(jnp.sum(g * g) for g in sums)
-    grad_norm = jnp.sqrt(lax.psum(squares, ("batch", "row", "col")))
+    grad_norm = jnp.sqrt(lax.psum(lax.psum(lax.psum(squares, "batch"), "row"), "col"))
     clip_factor = jnp.minimum(1.0, 1.0 / (grad_norm + 1e-06))
     news = []
     for g, m, v, w in zip(
@@ -750,8 +1093,8 @@
     ):
         news.append(adamw(g, m, v, weight_shard(w, group_index, g.shape[1]), clip_factor))
     return (
-        result[:img].astype(BF)[None],
-        result[img : lay.real].astype(BF)[None],
+        result[:img][None],
+        result[img : lay.real][None],
         grad_in[:img][None],
         grad_in[img : lay.real][None],
         *sums,
@@ -770,7 +1113,7 @@
     tall_shard = P(None, ("row", "batch"), "col")
     shards = (wide_shard, tall_shard, wide_shard, tall_shard)
     return jax.shard_map(
-        partial(on_device, mesh.shape["row"], mesh.shape["col"]),
+        partial(on_device, mesh.shape["batch"], mesh.shape["row"]),
         mesh=mesh,
         in_specs=(*[tokens] * 4, P(), wide, tall, wide, tall, *shards, *shards),
         out_specs=(*[tokens] * 4, *shards * 4, P()),

time: 680 us -> 456 us (0.67)
  waiting for transfers between devices: 178 us -> 0 us
  Pallas kernels: 230 us -> 378 us
  matrix products: 65.5 us -> 0 us
  local copies, waits for them, and re-layouts: 54 us -> 10 us
  other arithmetic: 74.4 us -> 31.4 us
  blocking collectives: 44.5 us -> 21 us
  between operations: 20.2 us -> 6.37 us
    pallas_call x3 -> x5, Pallas kernels: 230 us -> 378 us  [call(): pl.pallas_call(kernel, out_shape=[jax.ShapeDtypeStruct(s, t) for s, t in...]
    reduce_scatter x6 -> x0, waiting for transfers between devices: 135 us -> none  [the longest x4 128 us: batch_sum(): lax.psum_scatter(g.astype(BF), 'batch', scatter_dimension=1, tiled=True)]
    dot_general x19 -> x0, matrix products: 65.5 us -> none  [the longest x8 17.1 us: dot_tn(): lax.dot_general(a, b, (((0,), (0,)), ((), ())), preferred_element_type=F32)]
    ppermute x3 -> x0, waiting for transfers between devices: 33.8 us -> none  [col_swap(): return lax.ppermute(x, 'col', [(i, (i + 1) % n_col) for i in range(n_col)])]
    psum x2 -> x3, blocking collectives: 44.5 us -> 21 us  [the longest x1 8.97 us: on_device(): lax.psum(lax.psum(squares, 'batch'), 'row')]
    slice x6 -> x0, local copies, waits for them, and re-layouts: 19.2 us -> none  [the longest x1 9.9 us: attention_backward(): q, k, v = (parts[:, :, 0], parts[:, :, 1], parts[:, :, 2])]
    unnamed x74 -> x31, local copies, waits for them, and re-layouts: 24.3 us -> 5.66 us
    convert_element_type x3 -> x0, other arithmetic: 14.4 us -> none  [the longest x1 12.8 us: attention_backward(): ds = (p * (dp - row_dot)).astype(BF)]
  transfers between devices with their start and end apart: 10 -> 0, of which waited for: 7 -> 0; matrix products, arithmetic and copies ran while one was open for 23% -> 0% of each run, Pallas kernels for 0% -> 0%
where the time goes in v3:
time: 456 us; the launch traced here: 447 us
  Pallas kernels  378 us (83%)
  other arithmetic  31.4 us (7%)
  blocking collectives  21 us (5%)
  local copies, waits for them, and re-layouts  10 us (2%)
  between operations  6.37 us (1%)
    pallas_call x5, Pallas kernels, call(): pl.pallas_call(kernel, out_shape=[jax.ShapeDtypeStruct(s, t) for s, t in...  378 us
    mul x4, other arithmetic, adamw(): return (moment_new, square_new, -RATE * (corrected + DECAY * weight))  18.4 us

profile of v3, /device:TPU:0, one launch (start us, length us, event | category | flops | bytes accessed | tf_op | source)
XLA Modules:
  0.0 447.2 jit_solution(12219033347421001747)
XLA Ops:
  0.7 1.3 compare_reduce_fusion
  2.6 0.1 pad.5.clone
  2.7 2.0 multiply_convert_fusion.cot_ref
  4.7 1.9 maximum_maximum_fusion.x_ref
  6.6 52.9 %shard_map.328 = (bf16[4,304,768]{2,1,0:T(8,128)(2,1)}, bf16[4,304,576]{2,1,0:T(8,128)(2,1)}, f32[1,304,128]{2,1,0:T(8,128)}) custom-call(bf16[304,768]{1,0:T(8,128)(2,1)} %maximum_maximum_fusion.x_ref, bf16[2,768,1152]{2,1,0:T(8,128)(2,1)} %wa_ref.1), custom_call_target="tpu_custom_call" | custom-call | flops 2151677952 | bytes 10000000 | tf_op jit(solution)/shard_map/pallas_call | solution.py:219
  59.5 71.2 %shard_map.329 = (bf16[4,304,384]{2,1,0:T(8,128)(2,1)}, f32[4,304,128]{2,1,0:T(8,128)}, bf16[4,304,768]{2,1,0:T(8,128)(2,1)}, f32[4,304,768]{2,1,0:T(8,128)}, f3...) custom-call(bf16[4,304,576]{2,1,0:T(8,128)(2,1)} %get-tuple-element.45.qkv_ref, ...), custom_call_target="tpu_custom_call" | custom-call | flops 10000000000 | bytes 10000000 | tf_op jit(solution)/shard_map/pallas_call | solution.py:219
  130.7 104.4 %shard_map.330 = (bf16[4,304,768]{2,1,0:T(8,128)(2,1)}, bf16[4,304,768]{2,1,0:T(8,128)(2,1)}, bf16[4,304,1536]{2,1,0:T(8,128)(2,1)}, f32[304,768]{1,0:T(8,128)}, bf16[304,768]{1,0:T(8,128)(2,1)}) custom-call(bf16[304,768]{1,0:T(8,128)(2,1)} %get-tuple-element.46.low_ref, f32[4,304,768]{2,1,0:T(8,128)} %get-tuple-element.47.dg_ref, ...), custom_call_target="tpu_custom_call" | custom-call | flops 10000000000 | bytes 10000000 | tf_op jit(solution)/shard_map/pallas_call | solution.py:219
  235.2 75.2 %shard_map.331 = (bf16[4,304,768]{2,1,0:T(8,128)(2,1)}, bf16[4,304,576]{2,1,0:T(8,128)(2,1)}, bf16[4,304,1536]{2,1,0:T(8,128)(2,1)}, bf16[304,768]{1,0:T(8,128)(2,1)}, f32[2,192,1536]{2,1,0:T(8,128)}) custom-call(bf16[304,768]{1,0:T(8,128)(2,1)} %get-tuple-element.50.low_ref, bf16[4,304,576]{2,1,0:T(8,128)(2,1)} %get-tuple-element.45.qkv_ref, ...), custom_call_target="tpu_custom_call" | custom-call | flops 10000000000 | bytes 10000000 | tf_op jit(solution)/shard_map/pallas_call | solution.py:219
  310.4 2.9 multiply_reduce_fusion.1
  313.3 74.7 %shard_map.332 = (f32[304,768]{1,0:T(8,128)}, f32[2,192,1152]{2,1,0:T(8,128)}, f32[2,96,768]{2,1,0:T(8,128)}, f32[2,384,768]{2,1,0:T(8,128)}) custom-call(bf16[4,304,576]{2,1,0:T(8,128)(2,1)} %get-tuple-element.56.dqkv_ref, bf16[304,768]{1,0:T(8,128)(2,1)} %maximum_maximum_fusion.x_ref, f32[304,768]{1,0:T(8,128)} %get-tuple-element.57.dmid_ref, ...), custom_call_target="tpu_custom_call" | custom-call | flops 10000000000 | bytes 10000000 | tf_op jit(solution)/shard_map/pallas_call | solution.py:219
  388.0 0.0 copy-start.3
  388.0 0.0 copy-start.2
  388.0 0.0 copy-start.10
  388.0 3.0 multiply_reduce_fusion
  391.0 0.0 copy-done.3
  391.0 0.7 multiply_reduce_fusion.3
  391.8 0.0 copy-done.2
  391.8 1.1 multiply_reduce_fusion.2
  395.4 6.3 %psum.21 = f32[]{:T(128)} all-reduce(f32[]{:T(128)S(6)} %add.90), channel_id=1, replica_groups=mesh['batch'=4,'row'=4,'col'=2] {'batch'}, use_global_device_ids=true, to_apply=%region_5.0 | all-reduce | flops 1 | bytes 8 | tf_op jit(solution)/shard_map/psum | solution.py:1085
  401.7 9.0 %psum.22 = f32[]{:T(128)} all-reduce(f32[]{:T(128)} %psum.21), channel_id=1, replica_groups=mesh['batch'=4,'row'=4,'col'=2] {'row'}, use_global_device_ids=true, to_apply=%region_6.0 | all-reduce | flops 1 | bytes 8 | tf_op jit(solution)/shard_map/psum | solution.py:1085
  410.7 5.8 %psum.23 = f32[]{:T(128)} all-reduce(f32[]{:T(128)} %psum.22), channel_id=1, replica_groups=mesh['batch'=4,'row'=4,'col'=2] {'col'}, use_global_device_ids=true, to_apply=%region_7.0 | all-reduce | flops 1 | bytes 8 | tf_op jit(solution)/shard_map/psum | solution.py:1085
  417.2 0.0 copy-start.11
  417.2 0.0 copy-start.12
  417.2 1.6 slice_bitcast_fusion.3
  418.8 1.8 slice_bitcast_fusion.1
  420.6 0.0 copy-done.10
  420.6 0.9 slice_bitcast_fusion
  421.5 0.8 copy.38
  422.3 0.0 copy-done.11
  422.3 0.0 copy-done.12
  422.3 2.8 add_multiply_fusion.3
  425.1 0.0 copy-done.8
  425.1 0.0 copy-done.9
  425.1 0.0 copy-start.4
  425.1 0.0 copy-start.5
  425.1 4.6 %add_multiply_fusion.2 = (f32[2,192,1152]{2,1,0:T(8,128)}, f32[2,192,1152]{2,1,0:T(8,128)}, f32[2,192,1152]{2,1,0:T(8,128)}) fusion(bf16[2,768,1152]{2,1,0:T(8,128)(2,1)} %wa_ref.1, s32[]{:T(128)S(6)} %select_n.10, f32[2,192,1152]{2,1,0:T(8,128)S(1)} %copy-done.2, f32[]{:T(128)S(6)} %min.3, f32[2,192,1152]{2,1,0:T(8,128)S(1)} %copy-done.8, ...), kind=kLoop, calls=%fused_computation.12 | loop fusion | flops 7077888 | bytes 11501576 | tf_op jit(solution)/shard_map/mul | solution.py:1015
  429.7 0.0 copy-done
  429.7 0.0 copy-done.4
  429.7 0.0 copy-done.5
  429.7 0.0 copy-start.6
  429.7 0.0 copy-start.7
  429.7 5.7 %add_multiply_fusion.1 = (f32[2,192,1536]{2,1,0:T(8,128)}, f32[2,192,1536]{2,1,0:T(8,128)}, f32[2,192,1536]{2,1,0:T(8,128)}) fusion(bf16[2,768,1536]{2,1,0:T(8,128)(2,1)} %we_ref.1, s32[]{:T(128)S(6)} %select_n.10, f32[2,192,1536]{2,1,0:T(8,128)S(1)} %copy-done, f32[]{:T(128)S(6)} %min.3, f32[2,192,1536]{2,1,0:T(8,128)S(1)} %copy-done.4, ...), kind=kLoop, calls=%fused_computation.6 | loop fusion | flops 9437184 | bytes 15335432 | tf_op jit(solution)/shard_map/mul | solution.py:1015
  435.4 0.0 copy-done.6
  435.4 5.4 %add_multiply_fusion = (f32[2,384,768]{2,1,0:T(8,128)}, f32[2,384,768]{2,1,0:T(8,128)}, f32[2,384,768]{2,1,0:T(8,128)}) fusion(bf16[2,1536,768]{2,1,0:T(8,128)(2,1)} %wr_ref.3, s32[]{:T(128)S(6)} %select_n.12, f32[2,384,768]{2,1,0:T(8,128)S(1)} %copy-done.1, f32[]{:T(128)S(6)} %min.3, f32[2,384,768]{2,1,0:T(8,128)S(1)} %copy-done.6, ...), kind=kLoop, calls=%fused_computation.5 | loop fusion | flops 9437184 | bytes 15335432 | tf_op jit(solution)/shard_map/mul | solution.py:1015
  440.8 1.2 copy.43
  442.0 0.8 copy.44
  442.8 1.4 copy.45
  444.2 1.4 copy.46
  (8 shorter events, 0.0 us)
Async XLA Ops:
  388.0 3.1 copy-start.3
  388.0 3.8 copy-start.2
  388.0 32.6 %copy-start.10 = (f32[304,768]{1,0:T(8,128)S(1)}, f32[304,768]{1,0:T(8,128)}, u32[]{:S(2)}) copy-start(f32[304,768]{1,0:T(8,128)} %get-tuple-element.64) | copy-start | bytes 2801668
  417.2 5.1 %copy-start.11 = (f32[2,96,768]{2,1,0:T(8,128)S(1)}, f32[2,96,768]{2,1,0:T(8,128)}, u32[]{:S(2)}) copy-start(f32[2,96,768]{2,1,0:T(8,128)} %param.31) | copy-start | bytes 1769476
  417.2 5.1 %copy-start.12 = (f32[2,96,768]{2,1,0:T(8,128)S(1)}, f32[2,96,768]{2,1,0:T(8,128)}, u32[]{:S(2)}) copy-start(f32[2,96,768]{2,1,0:T(8,128)} %param.27) | copy-start | bytes 1769476
  421.5 3.6 copy-start.8
  421.5 3.6 copy-start.9
  425.1 4.6 %copy-start = (f32[2,192,1536]{2,1,0:T(8,128)S(1)}, f32[2,192,1536]{2,1,0:T(8,128)}, u32[]{:S(2)}) copy-start(f32[2,192,1536]{2,1,0:T(8,128)} %get-tuple-element.129) | copy-start | bytes 7077892
  425.1 4.6 %copy-start.4 = (f32[2,192,1536]{2,1,0:T(8,128)S(1)}, f32[2,192,1536]{2,1,0:T(8,128)}, u32[]{:S(2)}) copy-start(f32[2,192,1536]{2,1,0:T(8,128)} %param.32) | copy-start | bytes 7077892
  425.1 4.6 %copy-start.5 = (f32[2,192,1536]{2,1,0:T(8,128)S(1)}, f32[2,192,1536]{2,1,0:T(8,128)}, u32[]{:S(2)}) copy-start(f32[2,192,1536]{2,1,0:T(8,128)} %param.28) | copy-start | bytes 7077892
  429.7 5.7 %copy-start.1 = (f32[2,384,768]{2,1,0:T(8,128)S(1)}, f32[2,384,768]{2,1,0:T(8,128)}, u32[]{:S(2)}) copy-start(f32[2,384,768]{2,1,0:T(8,128)} %get-tuple-element.130) | copy-start | bytes 7077892
  429.7 5.7 %copy-start.6 = (f32[2,384,768]{2,1,0:T(8,128)S(1)}, f32[2,384,768]{2,1,0:T(8,128)}, u32[]{:S(2)}) copy-start(f32[2,384,768]{2,1,0:T(8,128)} %param.33) | copy-start | bytes 7077892
  429.7 5.7 %copy-start.7 = (f32[2,384,768]{2,1,0:T(8,128)S(1)}, f32[2,384,768]{2,1,0:T(8,128)}, u32[]{:S(2)}) copy-start(f32[2,384,768]{2,1,0:T(8,128)} %param.29) | copy-start | bytes 7077892

commit v4 on v3

--- a/solution.py
+++ b/solution.py
@@ -37,6 +37,7 @@
 
 MESH = pl.DeviceIdType.MESH
 VMEM = pl.BlockSpec(memory_space=pltpu.VMEM)
+ANY = pl.BlockSpec(memory_space=pl.ANY)
 
 
 def remote(src, dst, send, recv, **where):
@@ -57,7 +58,7 @@
     return jnp.where(j <= 2 * reach, alternate, beyond)
 
 
-def greet(n, fused=False):
+def greet(n, fused=False, more=()):
     z, c = lax.axis_index("row"), lax.axis_index("col")
     barrier = pltpu.get_barrier_semaphore()
     pl.semaphore_signal(barrier, inc=1, device_id={"col": 1 - c}, device_id_type=MESH)
@@ -75,7 +76,9 @@
         for other in (b + 1 - 2 * (b % 2), (b + 2) % 4):
             pl.semaphore_signal(barrier, inc=1, device_id={"batch": other}, device_id_type=MESH)
     ends = jnp.where(z > 0, 1, 0) + jnp.where(z < n - 1, 1, 0)
-    pl.semaphore_wait(barrier, ends + (3 if fused else 1))
+    for where in more:
+        pl.semaphore_signal(barrier, inc=1, device_id=where, device_id_type=MESH)
+    pl.semaphore_wait(barrier, ends + (3 if fused else 1) + len(more))
 
 
 class Gather:
@@ -195,12 +198,18 @@
 def sums_of(a, b):
     lane = lax.broadcasted_iota(jnp.int32, (a.shape[0], 128), 1)
     one, two = jnp.sum(a, axis=1, keepdims=True), jnp.sum(b, axis=1, keepdims=True)
-    return jnp.where(lane == 0, one, jnp.where(lane == 1, two, 0.0))
+    return jnp.where(lane == 0, one, jnp.where(lane == 1, two, 0.0)).T[:8]
+
+
+def columns(stat):
+    rows = stat[0]
+    turned = jnp.concatenate([rows, jnp.zeros((120, rows.shape[1]), F32)], 0).T
+    return turned[:, 0:1] / D, turned[:, 1:2] / D
 
 
 def moments(stat):
-    mean = stat[0, :, 0:1] / D
-    return mean, lax.rsqrt(stat[0, :, 1:2] / D - mean * mean + EPSILON)
+    mean, square = columns(stat)
+    return mean, lax.rsqrt(square - mean * mean + EPSILON)
 
 
 def exchange(stat, stat_in, send, recv):
@@ -215,11 +224,11 @@
     return pltpu.SemaphoreType.DMA(shape)
 
 
-def call(kernel, ident, outs, scratch, cost, *operands):
+def call(kernel, ident, outs, scratch, cost, *operands, far=()):
     return pl.pallas_call(
         kernel,
         out_shape=[jax.ShapeDtypeStruct(s, t) for s, t in outs],
-        in_specs=[VMEM] * len(operands),
+        in_specs=[ANY if i in far else VMEM for i in range(len(operands))],
         out_specs=[VMEM] * len(outs),
         scratch_shapes=scratch,
         compiler_params=pltpu.CompilerParams(
@@ -273,12 +282,12 @@
     return call(
         partial(attend_kernel, lay),
         1,
-        [((n, r, d), BF), ((n, r, half), BF), ((1, r, 128), F32)],
+        [((n, r, d), BF), ((n, r, half), BF), ((1, 8, r), F32)],
         [
             pltpu.VMEM((n, r, half), F32),
             pltpu.VMEM((n, r, half), BF),
             pltpu.VMEM((n, r, half), BF),
-            pltpu.VMEM((1, r, 128), F32),
+            pltpu.VMEM((1, 8, r), F32),
             dma(2, n),
             dma(n),
             dma(n),
@@ -420,7 +429,7 @@
             ((n, r, hid), F32),
             ((r, d), F32),
             ((r, d), BF),
-            ((1, r, 128), F32),
+            ((1, 8, r), F32),
         ],
         [
             pltpu.VMEM((heads, n, r, HD), BF),
@@ -433,7 +442,7 @@
             pltpu.VMEM((r, d), F32),
             pltpu.VMEM((n, r, d), BF),
             pltpu.VMEM((n + 1, r, d), BF),
-            pltpu.VMEM((1, r, 128), F32),
+            pltpu.VMEM((1, 8, r), F32),
             dma(2, n),
             dma(n),
             dma(n),
@@ -525,7 +534,7 @@
     grad = acc[...]
     stat_out[0] = sums_of(grad, grad * normed)
     exchange(stat_out, stat_in, t_send, t_recv)
-    back_one, back_two = stat_out[0, :, 0:1] / D, stat_out[0, :, 1:2] / D
+    back_one, back_two = columns(stat_out)
     dmid = cot_ref[...].astype(F32) + inverse * (grad - back_one - normed * back_two)
     dmid_ref[...] = dmid
     dy_ref[...] = dmid.astype(BF)
@@ -557,8 +566,8 @@
             pltpu.VMEM((r, d), F32),
             pltpu.VMEM((n, r, d), BF),
             pltpu.VMEM((n + 1, r, d), BF),
-            pltpu.VMEM((1, r, 128), F32),
-            pltpu.VMEM((1, r, 128), F32),
+            pltpu.VMEM((1, 8, r), F32),
+            pltpu.VMEM((1, 8, r), F32),
             dma(2, n),
             dma(n),
             dma(n),
@@ -647,6 +656,67 @@
     return BatchSum(*scratch[:4], scratch[4:])
 
 
+def squares_of(ref):
+    total = jnp.zeros((1, 1), F32)
+    for m in range(2):
+        lanes = jnp.sum(ref[m] * ref[m], axis=0, keepdims=True)
+        total += jnp.sum(lanes, axis=1, keepdims=True)
+    return jnp.broadcast_to(total, (8, 128))
+
+
+class Norm:
+    def __init__(self, n_batch, n_row, plane, line, p_send, p_recv, b_send, b_recv):
+        self.n_batch, self.plane, self.line = n_batch, plane, line
+        self.p_send, self.p_recv, self.b_send, self.b_recv = p_send, p_recv, b_send, b_recv
+        self.b, z, c = lax.axis_index("batch"), lax.axis_index("row"), lax.axis_index("col")
+        self.me = z * 2 + c
+        self.peers = [((z + i) % n_row, (c + j) % 2) for i in range(n_row) for j in range(2)][1:]
+
+    def where(self):
+        return [{"row": row, "col": col} for row, col in self.peers] + [
+            {"batch": (self.b + i) % self.n_batch} for i in range(1, self.n_batch)
+        ]
+
+    def to_plane(self, i, slot):
+        row, col = self.peers[i]
+        block = self.plane.at[slot]
+        return remote(block, block, self.p_send.at[i], self.p_recv.at[slot], row=row, col=col)
+
+    def to_line(self, i, slot):
+        block = self.line.at[slot]
+        other = (self.b + i) % self.n_batch
+        return remote(block, block, self.b_send.at[i], self.b_recv.at[slot], batch=other)
+
+    def total(self, tile):
+        b, n_batch = self.b, self.n_batch
+        self.plane[self.me] = tile
+        for i in range(len(self.peers)):
+            self.to_plane(i, self.me).start()
+        for i, (row, col) in enumerate(self.peers):
+            self.to_plane(i, row * 2 + col).wait_recv()
+        self.line[b] = jnp.sum(self.plane[...], axis=0)
+        for i in range(1, n_batch):
+            self.to_line(i, b).start()
+        for i in range(1, n_batch):
+            self.to_line(i, (b + i) % n_batch).wait_recv()
+        for i in range(len(self.peers)):
+            self.to_plane(i, self.me).wait_send()
+        for i in range(1, n_batch):
+            self.to_line(i, b).wait_send()
+        return jnp.sum(self.line[...], axis=0)
+
+
+def norm_scratch(n_batch, n_row):
+    return [
+        pltpu.VMEM((2 * n_row, 8, 128), F32),
+        pltpu.VMEM((n_batch, 8, 128), F32),
+        dma(2 * n_row - 1),
+        dma(2 * n_row),
+        dma(n_batch),
+        dma(n_batch),
+    ]
+
+
 def transpose_rows(lay, left, turned):
     n, img, far = lay.n_row, lay.img, lay.n_row * lay.img
     for k in range(n):
@@ -667,12 +737,13 @@
 
 
 def pull_kernel(
-    lay, fused, low_ref, qkv_ref, lse_ref, wo_ref, act_ref, wr_ref, mid_ref, a2_ref, dh_ref, full_ref, dqkv_ref, g_ref, res_ref, exp_ref, *scratch
+    lay, fused, low_ref, qkv_ref, lse_ref, wo_ref, act_ref, wr_any, mid_ref, a2_ref, dh_ref, o_ref,
+    full_ref, dqkv_ref, g_ref, res_ref, exp_ref, out_ref, square_ref, *scratch
 ):
     (
-        q_s, k_s, v_s, do_own, do_out, do_in, do_s, dq_s, dk_s, dv_s, acc, r_out, inbox, turned,
+        q_s, k_s, v_s, do_own, do_out, do_in, do_s, dq_s, dk_s, dv_s, acc, r_out, inbox, turned, wr_ref, a_load, w_load,
         g_send, g_recv, s_send, s_recv, a_send, a_recv, r_send, r_recv,
-    ) = scratch[:22]
+    ) = scratch[:25]
     n, img, txt, far = lay.n_row, lay.img, lay.txt_pad, lay.n_row * lay.img
     z, c = lax.axis_index("row"), lax.axis_index("col")
     heads, half, hid = q_s.shape[0], do_own.shape[2], act_ref.shape[2]
@@ -686,10 +757,10 @@
     gather.push(z)
     swap = Swap(do_out, do_in, s_send, s_recv)
     reduce = Reduce(acc, r_out, inbox, r_send, r_recv, n)
-    local = exp_ref
+    local, local_out = exp_ref, out_ref
     if fused:
-        batch = batch_of(scratch[22:])
-        local = batch.local
+        batch, batch_out = batch_of(scratch[25:33]), batch_of(scratch[33:41])
+        local, local_out = batch.local, batch_out.local
     split_heads(lay, qkv_ref, q_s, k_s, v_s, False)
     bias = text_bias(lay)
     dk_s[...] = jnp.zeros_like(dk_s)
@@ -697,7 +768,18 @@
     lag = jnp.minimum(z, n - 1 - z)
 
     def act_copy(k, where):
-        return remote(act_ref.at[k], g_ref.at[k, :, where], a_send.at[k], a_recv.at[k], col=1 - c)
+        block = g_ref.at[k, :, where]
+        return remote(block, block, a_send.at[k], a_recv.at[k], col=1 - c)
+
+    def load(k):
+        return pltpu.make_async_copy(act_ref.at[k], g_ref.at[k, :, my_act], a_load.at[k])
+
+    def wr_load():
+        return pltpu.make_async_copy(wr_any, wr_ref, w_load.at[0])
+
+    wr_load().start()
+    for k in range(n):
+        load(k).start()
 
     def arrive(k):
         gather.arrive_after_own(k)
@@ -731,7 +813,8 @@
             )
             ds1 = (p1 * (dp1 - row)).astype(BF)
             ds2 = (p2 * (dp2 - row)).astype(BF)
-            dq_s[h, k] = dot(ds1, k_s[h, :far]) + dot(ds2, k_s[h, far:])
+            dq = (dot(ds1, k_s[h, :far]) + dot(ds2, k_s[h, far:])) * HD**-0.5
+            dq_s[h, k] = dq.astype(BF)
             dk_s[h, :, :far] += dot_tn(q, ds1)
             dk_s[h, :, far:] += dot_tn(q, ds2)
             dv_s[h, :, :far] += dot_tn(do, p1.astype(BF))
@@ -739,27 +822,37 @@
 
     def down(k):
         act_copy(k, their_act).wait_recv()
-        g_ref[k, :, my_act] = act_ref[k]
         for part, rows in parts_of(lay):
             acc[rows] = dot(g_ref[k, rows], wr_ref[part])
         reduce.add(k)
 
-    @pl.loop(0, n + 1 + (n - 1) // 2)
+    @pl.loop(0, n + 1)
     def _(j):
         @pl.when(j < n)
         def _():
             arrive(near_first(z, n, j))
+
+        @pl.when(j < 2)
+        def _():
+            load(near_first(z, n, n - 1 - j)).wait()
             act_copy(near_first(z, n, n - 1 - j), my_act).start()
 
+        @pl.when(j == n - 1)
+        def _():
+            for i in range(2, n):
+                load(near_first(z, n, n - 1 - i)).wait()
+                act_copy(near_first(z, n, n - 1 - i), my_act).start()
+
         @pl.when(j == 0)
         def _():
             expand_gradient()
+            wr_load().wait()
             if fused:
                 batch.start()
 
         if fused:
 
-            @pl.when(j == 1)
+            @pl.when(j == 2)
             def _():
                 batch.pass_on()
 
@@ -769,11 +862,16 @@
 
         i = j - 1 - lag
 
-        @pl.when((i >= 0) & (i < n))
+        @pl.when((i >= 0) & (i < 2))
         def _():
             down(near_first(z, n, n - 1 - i))
 
-    res_ref[...] = (mid_ref[...] + acc[...]).astype(BF)
+    turned_o = turned.at[: o_ref.shape[2]]
+    transpose_rows(lay, o_ref, turned_o)
+    for part in range(2):
+        weight_gradient(lay, turned_o, full_ref, local_out, part, slice(0, full_ref.shape[2]))
+    if fused:
+        batch_out.start()
     for k in range(n):
         for h in range(heads):
             at = h * 3 * HD
@@ -781,13 +879,22 @@
                 (slice(0, img), k * img, img),
                 (slice(img, lay.rows), far + k * txt, txt),
             ):
-                dk = dk_s[h, :, first : first + count].T
-                dv = dv_s[h, :, first : first + count].T
-                dq = dq_s[h, k, rows] * HD**-0.5
-                dqkv_ref[k, rows, at : at + 3 * HD] = jnp.concatenate([dq, dk, dv], 1).astype(BF)
+                dk = dk_s[h, :, first : first + count].T.astype(BF)
+                dv = dv_s[h, :, first : first + count].T.astype(BF)
+                dqkv_ref[k, rows, at : at + 3 * HD] = jnp.concatenate(
+                    [dq_s[h, k, rows], dk, dv], 1
+                )
+    if fused:
+        batch_out.pass_on()
+    for i in range(2, n):
+        down(near_first(z, n, n - 1 - i))
+    res_ref[...] = (mid_ref[...] + acc[...]).astype(BF)
     if fused:
         exp_ref[...] = batch.total()
+        out_ref[...] = batch_out.total()
         batch.finish()
+        batch_out.finish()
+        square_ref[...] = squares_of(exp_ref) + squares_of(out_ref)
     gather.finish()
     swap.finish(n)
     reduce.finish()
@@ -797,10 +904,11 @@
         act_copy(k, my_act).wait_send()
 
 
-def pull(lay, fused, low, qkv, lse, wo, act, wr, mid, a2, dh):
+def pull(lay, fused, low, qkv, lse, wo, act, wr, mid, a2, dh, o):
     n, r, d, hid = lay.n_row, lay.rows, low.shape[1], act.shape[2]
     heads = qkv.shape[2] // (3 * HD)
     keys = n * r
+    shapes = [(d, 2 * hid), (o.shape[2], d)]
     return call(
         partial(pull_kernel, lay, fused),
         4,
@@ -809,7 +917,8 @@
             ((n, r, 3 * heads * HD), BF),
             ((n, r, 2 * hid), BF),
             ((r, d), BF),
-            ((2, d // 4, 2 * hid), F32) if fused else ((2, d, 2 * hid), BF),
+            *[((2, s[0] // 4, s[1]), F32) if fused else ((2, *s), BF) for s in shapes],
+            ((8, 128), F32),
         ],
         [
             pltpu.VMEM((heads, n, r, HD), BF),
@@ -819,13 +928,16 @@
             pltpu.VMEM((n, r, heads * HD), BF),
             pltpu.VMEM((n, r, heads * HD), BF),
             pltpu.VMEM((r, heads * HD), BF),
-            pltpu.VMEM((heads, n, r, HD), F32),
+            pltpu.VMEM((heads, n, r, HD), BF),
             pltpu.VMEM((heads, HD, keys), F32),
             pltpu.VMEM((heads, HD, keys), F32),
             pltpu.VMEM((r, d), F32),
             pltpu.VMEM((n, r, d), BF),
             pltpu.VMEM((n + 1, r, d), BF),
             pltpu.VMEM((d, keys), BF),
+            pltpu.VMEM(wr.shape, BF),
+            dma(n),
+            dma(1),
             dma(2, n),
             dma(n),
             dma(n),
@@ -834,7 +946,7 @@
             dma(n),
             dma(n),
             dma(n + 1),
-            *(batch_scratch(d, 2 * hid) if fused else []),
+            *([t for s in shapes for t in batch_scratch(*s)] if fused else []),
         ],
         10**10,
         low,
@@ -846,11 +958,14 @@
         mid,
         a2,
         dh,
+        o,
+        far=(4, 5),
     )
 
 
 def input_kernel(
-    lay, fused, dqkv_ref, x_ref, dmid_ref, stat_ref, wa_ref, a1_ref, o_ref, dy_ref, g_ref, cb_ref, dx_ref, att_ref, out_ref, red_ref, *scratch
+    lay, fused, dqkv_ref, x_ref, dmid_ref, stat_ref, wa_ref, a1_ref, g_ref, cb_ref, square_ref,
+    dx_ref, att_ref, red_ref, norm_ref, *scratch
 ):
     (
         full, into, acc, r_out, inbox, stat_out, stat_in, turned, turned_g,
@@ -859,13 +974,17 @@
     n = lay.n_row
     z, c = lax.axis_index("row"), lax.axis_index("col")
     half, d = dqkv_ref.shape[2], x_ref.shape[1]
-    greet(n, fused)
+    more = ()
+    if fused:
+        norm = Norm(4, n, *scratch[39:])
+        more = norm.where()
+    greet(n, False, more)
     swap = Swap(dqkv_ref, into, s_send, s_recv)
     reduce = Reduce(acc, r_out, inbox, r_send, r_recv, n)
-    own, other, red, out = (scratch[15 + 8 * i : 23 + 8 * i] for i in range(4)) if fused else (
-        scratch[15:16], scratch[16:17], (red_ref,), (out_ref,)
-    )
-    sums = [batch_of(s) for s in (own, other, red, out)] if fused else []
+    own, other, red = (scratch[15 + 8 * i : 23 + 8 * i] for i in range(3)) if fused else (
+        scratch[15:16], scratch[16:17], (red_ref,)
+    )
+    sums = [batch_of(s) for s in (own, other, red)] if fused else []
 
     @pl.loop(0, n)
     def _(j):
@@ -916,51 +1035,45 @@
             def _():
                 sums[2].pass_on()
 
-        @pl.when(j == 2)
-        def _():
-            turned_o = turned_g.at[: o_ref.shape[2]]
-            transpose_rows(lay, o_ref, turned_o)
-            gradient(turned_o, dy_ref, out[0], d)
-            if fused:
-                sums[3].start()
-
     gradient(turned, into, other[0], half)
     if fused:
         sums[1].start()
-        sums[3].pass_on()
     mean, inverse = moments(stat_ref)
     normed = (x_ref[...].astype(F32) - mean) * inverse
     grad = acc[...]
     stat_out[0] = sums_of(grad, grad * normed)
     exchange(stat_out, stat_in, t_send, t_recv)
-    back_one, back_two = stat_out[0, :, 0:1] / D, stat_out[0, :, 1:2] / D
+    back_one, back_two = columns(stat_out)
     dx_ref[...] = dmid_ref[...] + inverse * (grad - back_one - normed * back_two)
     if fused:
         sums[1].pass_on()
         red_ref[...] = sums[2].total()
-        out_ref[...] = sums[3].total()
         mine, theirs = sums[0].total(), sums[1].total()
     else:
         mine, theirs = own[0][...], other[0][...]
     att_ref[...] = jnp.concatenate(
         [jnp.where(c == 0, mine, theirs), jnp.where(c == 0, theirs, mine)], 2
     )
+    if fused:
+        squares = square_ref[...] + squares_of(att_ref) + squares_of(red_ref)
+        norm_ref[...] = jnp.sqrt(norm.total(squares))
     for total in sums:
         total.finish()
     swap.finish(n)
     reduce.finish()
 
 
-def inputs_back(lay, fused, dqkv, x, dmid, stat, wa, a1, o, dy, g, cb):
+def inputs_back(lay, fused, dqkv, x, dmid, stat, wa, a1, g, cb, square):
     n, r, d, half = lay.n_row, lay.rows, x.shape[1], dqkv.shape[2]
     keys = n * r
-    shapes = [(d, 2 * half), (o.shape[2], d), (g.shape[2], d)]
+    shapes = [(d, 2 * half), (g.shape[2], d)]
     return call(
         partial(input_kernel, lay, fused),
         5,
         [
             ((r, d), F32),
             *[((2, s[0] // 4, s[1]), F32) if fused else ((2, *s), BF) for s in shapes],
+            ((8, 128), F32),
         ],
         [
             pltpu.VMEM((r, 2 * half), BF),
@@ -968,8 +1081,8 @@
             pltpu.VMEM((r, d), F32),
             pltpu.VMEM((n, r, d), BF),
             pltpu.VMEM((n + 1, r, d), BF),
-            pltpu.VMEM((1, r, 128), F32),
-            pltpu.VMEM((1, r, 128), F32),
+            pltpu.VMEM((1, 8, r), F32),
+            pltpu.VMEM((1, 8, r), F32),
             pltpu.VMEM((d, keys), BF),
             pltpu.VMEM((g.shape[2], keys), BF),
             dma(n),
@@ -983,7 +1096,7 @@
                     *batch_scratch(d, half),
                     *batch_scratch(d, half),
                     *batch_scratch(g.shape[2], d),
-                    *batch_scratch(o.shape[2], d),
+                    *norm_scratch(4, n),
                 ]
                 if fused
                 else [pltpu.VMEM((2, d, half), BF)] * 2
@@ -996,10 +1109,9 @@
         stat,
         wa,
         a1,
-        o,
-        dy,
         g,
         cb,
+        square,
     )
 
 
@@ -1013,6 +1125,80 @@
         / (jnp.sqrt(square_new / (1.0 - BETA_TWO**STEP)) + 1e-08)
     )
     return (moment_new, square_new, -RATE * (corrected + DECAY * weight))
+
+
+def update_kernel(norm_ref, *refs):
+    grads, moments_in, squares_in, weights = refs[0:4], refs[4:8], refs[8:12], refs[12:16]
+    m_out, v_out, s_out, g_out = refs[16:20], refs[20:24], refs[24:28], refs[28:32]
+    g_s, m_s, v_s, w_s, t_s = (refs[32 + 4 * i : 36 + 4 * i] for i in range(5))
+    load, store = refs[52:]
+    b = lax.axis_index("batch")
+    loads = []
+    for i in range(4):
+        rows = grads[i].shape[1]
+        part = pl.ds(pl.multiple_of(b * rows, 16), rows)
+        for m in range(2):
+            for q, (src, dst) in enumerate(
+                (
+                    (grads[i].at[m], g_s[i]),
+                    (moments_in[i].at[m], m_s[i]),
+                    (squares_in[i].at[m], v_s[i]),
+                    (weights[i].at[m, part, :], w_s[i]),
+                )
+            ):
+                loads.append(pltpu.make_async_copy(src, dst.at[m], load.at[i, m, q]))
+                loads[-1].start()
+    clip = jnp.minimum(1.0, 1.0 / (norm_ref[0:1, 0:1] + 1e-06))
+    stores = []
+    for i in range(4):
+        for m in range(2):
+            for q in range(4):
+                loads[8 * i + 4 * m + q].wait()
+            stores.append(pltpu.make_async_copy(g_s[i].at[m], g_out[i].at[m], store.at[i, m, 3]))
+            stores[-1].start()
+
+            @pl.loop(0, grads[i].shape[1] // TILE)
+            def _(r):
+                part = pl.ds(pl.multiple_of(r * TILE, TILE), TILE)
+                new_m, new_v, step = adamw(
+                    g_s[i][m, part, :],
+                    m_s[i][m, part, :],
+                    v_s[i][m, part, :],
+                    w_s[i][m, part, :].astype(F32),
+                    clip,
+                )
+                m_s[i][m, part, :] = new_m
+                v_s[i][m, part, :] = new_v
+                t_s[i][m, part, :] = step
+
+            for q, (src, dst) in enumerate(
+                ((m_s[i], m_out[i]), (v_s[i], v_out[i]), (t_s[i], s_out[i]))
+            ):
+                stores.append(pltpu.make_async_copy(src.at[m], dst.at[m], store.at[i, m, q]))
+                stores[-1].start()
+    for each in stores:
+        each.wait()
+
+
+TILE = 16
+
+
+def update(norm, grads, ms, vs, ws):
+    shapes = [g.shape for g in grads]
+    outs = pl.pallas_call(
+        update_kernel,
+        out_shape=[jax.ShapeDtypeStruct(s, F32) for _ in range(4) for s in shapes],
+        in_specs=[VMEM] + [ANY] * 16,
+        out_specs=[ANY] * 16,
+        scratch_shapes=[
+            *[pltpu.VMEM(s, t) for t in (F32, F32, F32, BF, F32) for s in shapes],
+            dma(4, 2, 4),
+            dma(4, 2, 4),
+        ],
+        compiler_params=pltpu.CompilerParams(vmem_limit_bytes=60 * 2**20),
+        cost_estimate=pl.CostEstimate(flops=10**8, bytes_accessed=5 * 10**7, transcendentals=0),
+    )(norm, *grads, *ms, *vs, *ws)
+    return outs[0:4], outs[4:8], outs[8:12], outs[12:16]
 
 
 def weight_shard(weight, group_index, shard_rows):
@@ -1070,37 +1256,42 @@
     a2_all, act, dh_all, grad_mid, low_mid = hidden(
         lay, low_two, dg, middle_x, low_cot, stat_two, w_expand
     )
-    dy_all, dqkv, g_all, result, g_exp = pull(
-        lay, fused, low_mid, qkv, lse, w_output, act, w_reduce, middle_x, a2_all, dh_all
-    )
-    grad_in, g_att, g_out, g_red = inputs_back(
-        lay, fused, dqkv, low_x, grad_mid, stat_one, w_attend, a1_all, o_all, dy_all, g_all, cb_all
+    _, dqkv, g_all, result, g_exp, g_out, square = pull(
+        lay, fused, low_mid, qkv, lse, w_output, act, w_reduce, middle_x, a2_all, dh_all, o_all
+    )
+    grad_in, g_att, g_red, norm = inputs_back(
+        lay, fused, dqkv, low_x, grad_mid, stat_one, w_attend, a1_all, g_all, cb_all, square
     )
     sums = [g_att, g_out, g_exp, g_red]
     if not fused:
         sums = [
             lax.psum_scatter(g, "batch", scatter_dimension=1, tiled=True).astype(F32) for g in sums
         ]
-    squares = sum(jnp.sum(g * g) for g in sums)
-    grad_norm = jnp.sqrt(lax.psum(lax.psum(lax.psum(squares, "batch"), "row"), "col"))
-    clip_factor = jnp.minimum(1.0, 1.0 / (grad_norm + 1e-06))
-    news = []
-    for g, m, v, w in zip(
-        sums,
-        (m_attend, m_output, m_expand, m_reduce),
-        (v_attend, v_output, v_expand, v_reduce),
-        (w_attend, w_output, w_expand, w_reduce),
-    ):
-        news.append(adamw(g, m, v, weight_shard(w, group_index, g.shape[1]), clip_factor))
+    ms = (m_attend, m_output, m_expand, m_reduce)
+    vs = (v_attend, v_output, v_expand, v_reduce)
+    ws = (w_attend, w_output, w_expand, w_reduce)
+    if fused:
+        grad_norm = norm[0, 0]
+        new_m, new_v, steps, sums = update(norm, sums, ms, vs, ws)
+    else:
+        squares = sum(jnp.sum(g * g) for g in sums)
+        grad_norm = jnp.sqrt(lax.psum(lax.psum(lax.psum(squares, "batch"), "row"), "col"))
+        clip_factor = jnp.minimum(1.0, 1.0 / (grad_norm + 1e-06))
+        new_m, new_v, steps = zip(
+            *[
+                adamw(g, m, v, weight_shard(w, group_index, g.shape[1]), clip_factor)
+                for g, m, v, w in zip(sums, ms, vs, ws)
+            ]
+        )
     return (
         result[:img][None],
         result[img : lay.real][None],
         grad_in[:img][None],
         grad_in[img : lay.real][None],
         *sums,
-        *[n[0] for n in news],
-        *[n[1] for n in news],
-        *[n[2] for n in news],
+        *new_m,
+        *new_v,
+        *steps,
         grad_norm,
     )
 

time: 456 us -> 409 us (0.90); the launches traced: 447 us -> 409 us
  other arithmetic: 31.4 us -> 3.53 us
  blocking collectives: 21 us -> 0 us
  Pallas kernels: 378 us -> 396 us
  between operations: 6.37 us -> 1.4 us
    psum x3 -> x0, blocking collectives: 21 us -> none  [the longest x1 8.97 us: on_device(): lax.psum(lax.psum(squares, 'batch'), 'row')]
    pallas_call x0 -> x1, Pallas kernels: none -> 20 us  [update(): pl.pallas_call(update_kernel, out_shape=[jax.ShapeDtypeStruct(s, F32) for...]
    mul x4 -> x0, other arithmetic: 18.4 us -> none  [adamw(): return (moment_new, square_new, -RATE * (corrected + DECAY * weight))]
    reduce_sum x4 -> x0, other arithmetic: 7.71 us -> none  [on_device(): squares = sum((jnp.sum(g * g) for g in sums))]
    unnamed x31 -> x7, local copies, waits for them, and re-layouts: 5.66 us -> 0.78 us
where the time goes in v4:
time: 409 us
  Pallas kernels  396 us (97%)
  local copies, waits for them, and re-layouts  8.25 us (2%)
    pallas_call x5, Pallas kernels, call(): pl.pallas_call(kernel, out_shape=[jax.ShapeDtypeStruct(s, t) for s, t in...  376 us
    pallas_call x1, Pallas kernels, update(): pl.pallas_call(update_kernel, out_shape=[jax.ShapeDtypeStruct(s, F32) for...  20 us

profile of v4, /device:TPU:0, one launch (start us, length us, event | category | flops | bytes accessed | tf_op | source)
XLA Modules:
  0.0 408.9 jit_solution(4528965354806264778)
XLA Ops:
  0.7 0.1 pad.5.clone
  0.7 1.9 maximum_maximum_fusion.x_ref
  2.7 0.0 copy-start.2
  2.7 0.0 copy-start
  2.7 0.0 copy-start.1
  2.7 50.5 %shard_map.328 = (bf16[4,304,768]{2,1,0:T(8,128)(2,1)}, bf16[4,304,576]{2,1,0:T(8,128)(2,1)}, f32[1,8,304]{2,1,0:T(8,128)}) custom-call(bf16[304,768]{1,0:T(8,128)(2,1)} %maximum_maximum_fusion.x_ref, bf16[2,768,1152]{2,1,0:T(8,128)(2,1)} %refs_12_.1), custom_call_target="tpu_custom_call" | custom-call | flops 2151677952 | bytes 10000000 | tf_op jit(solution)/shard_map/pallas_call | solution.py:228
  53.2 0.0 copy-done.2
  53.2 0.6 compare_reduce_fusion
  54.5 0.0 copy-done
  54.5 0.0 copy-done.1
  54.5 0.9 multiply_convert_fusion.cot_ref
  55.4 69.9 %shard_map.329 = (bf16[4,304,384]{2,1,0:T(8,128)(2,1)}, f32[4,304,128]{2,1,0:T(8,128)}, bf16[4,304,768]{2,1,0:T(8,128)(2,1)}, f32[4,304,768]{2,1,0:T(8,128)}, f3...) custom-call(bf16[4,304,576]{2,1,0:T(8,128)(2,1)} %get-tuple-element.62.qkv_ref, ...), custom_call_target="tpu_custom_call" | custom-call | flops 10000000000 | bytes 10000000 | tf_op jit(solution)/shard_map/pallas_call | solution.py:228
  125.4 99.5 %shard_map.330 = (bf16[4,304,768]{2,1,0:T(8,128)(2,1)}, bf16[4,304,768]{2,1,0:T(8,128)(2,1)}, bf16[4,304,1536]{2,1,0:T(8,128)(2,1)}, f32[304,768]{1,0:T(8,128)}, bf16[304,768]{1,0:T(8,128)(2,1)}) custom-call(bf16[304,768]{1,0:T(8,128)(2,1)} %get-tuple-element.63.low_ref, f32[4,304,768]{2,1,0:T(8,128)} %get-tuple-element.64.dg_ref, ...), custom_call_target="tpu_custom_call" | custom-call | flops 10000000000 | bytes 10000000 | tf_op jit(solution)/shard_map/pallas_call | solution.py:228
  224.9 73.9 %shard_map.331 = (bf16[4,304,768]{2,1,0:T(8,128)(2,1)}, bf16[4,304,576]{2,1,0:T(8,128)(2,1)}, bf16[4,304,1536]{2,1,0:T(8,128)(2,1)}, bf16[304,768]{1,0:T(8,128)(...) custom-call(bf16[304,768]{1,0:T(8,128)(2,1)} %get-tuple-element.67.low_ref, ...), custom_call_target="tpu_custom_call" | custom-call | flops 10000000000 | bytes 10000000 | tf_op jit(solution)/shard_map/pallas_call | solution.py:228
  298.8 1.8 slice_bitcast_fusion.1
  300.6 1.5 slice_bitcast_fusion.3
  302.1 81.9 %shard_map.332 = (f32[304,768]{1,0:T(8,128)}, f32[2,192,1152]{2,1,0:T(8,128)}, f32[2,384,768]{2,1,0:T(8,128)}, f32[8,128]{1,0:T(8,128)}) custom-call(bf16[4,304,576]{2,1,0:T(8,128)(2,1)} %get-tuple-element.74.dqkv_ref, bf16[304,768]{1,0:T(8,128)(2,1)} %maximum_maximum_fusion.x_ref, f32[304,768]{1,0:T(8,128)} %get-tuple-element.75.dmid_ref, ...), custom_call_target="tpu_custom_call" | custom-call | flops 10000000000 | bytes 10000000 | tf_op jit(solution)/shard_map/pallas_call | solution.py:228
  383.9 2.1 slice_bitcast_fusion
  386.0 0.9 slice_bitcast_fusion.2
  386.9 0.8 copy.38
  387.7 20.0 %shard_map.333 = (f32[2,192,1152]{2,1,0:T(8,128)}, f32[2,96,768]{2,1,0:T(8,128)}, f32[2,192,1536]{2,1,0:T(8,128)}, f32[2,384,768]{2,1,0:T(8,128)}, f32[2,192,115...) custom-call(f32[8,128]{1,0:T(8,128)} %get-tuple-element.82.norm_ref,, ...), custom_call_target="tpu_custom_call" | custom-call | flops 100000000 | bytes 50000000 | tf_op jit(solution)/shard_map/pallas_call | solution.py:1188
  407.7 1.2 slice.19
  (1 shorter events, 0.0 us)
Async XLA Ops:
  2.7 50.5 %copy-start.2 = (s32[3]{0:T(128)S(1)}, s32[3]{0:T(128)}, u32[]{:S(2)}) copy-start(s32[3]{0:T(128)} %param.21) | copy-start | bytes 40
  2.7 51.8 %copy-start = (bf16[1,256,768]{2,1,0:T(8,128)(2,1)S(1)}, bf16[1,256,768]{2,1,0:T(8,128)(2,1)}, u32[]{:S(2)}) copy-start(bf16[1,256,768]{2,1,0:T(8,128)(2,1)} %param.19) | copy-start | bytes 1179652
  2.7 51.8 %copy-start.1 = (bf16[1,38,768]{2,1,0:T(8,128)(2,1)S(1)}, bf16[1,38,768]{2,1,0:T(8,128)(2,1)}, u32[]{:S(2)}) copy-start(bf16[1,38,768]{2,1,0:T(8,128)(2,1)} %param.20) | copy-start | bytes 175108

commit v5 on v4

--- a/solution.py
+++ b/solution.py
@@ -327,7 +327,7 @@
 
 
 def middle_kernel(
-    lay, qkv_ref, x_ref, cot_ref, wo_ref, wr_ref, o_ref, lse_ref, cb_ref, dg_ref, mid_ref, low_ref, stat_ref, *scratch
+    lay, loads, qkv_ref, x_ref, cot_ref, wo_ref, wr_ref, o_ref, lse_ref, cb_ref, dg_ref, mid_ref, low_ref, stat_ref, *scratch
 ):
     (
         q_s, k_s, v_s, o_out, o_in, dg_out, dg_in, acc, r_out, inbox, stat_in,
@@ -379,6 +379,12 @@
         k = near_first(z, n, n - 1 - j)
         attention(k)
         swap_o.start(k)
+
+        @pl.when(j == 0)
+        def _():
+            loads[0].wait()
+            loads[1].wait()
+
         near = near_first(z, n, j)
         gather.arrive_after_own(near)
         for part, rows in parts_of(lay):
@@ -413,54 +419,6 @@
     swap_o.finish(n)
     swap_d.finish(n)
     reduce.finish()
-
-
-def middle(lay, qkv, x, cot, wo, wr):
-    n, r, d = lay.n_row, lay.rows, x.shape[1]
-    heads, hid = qkv.shape[2] // (3 * HD), wr.shape[1] // 2
-    keys = n * r
-    return call(
-        partial(middle_kernel, lay),
-        2,
-        [
-            ((n, r, 2 * heads * HD), BF),
-            ((n, r, 128), F32),
-            ((n, r, d), BF),
-            ((n, r, hid), F32),
-            ((r, d), F32),
-            ((r, d), BF),
-            ((1, 8, r), F32),
-        ],
-        [
-            pltpu.VMEM((heads, n, r, HD), BF),
-            pltpu.VMEM((heads, keys, HD), BF),
-            pltpu.VMEM((heads, keys, 2 * HD), BF),
-            pltpu.VMEM((n, r, heads * HD), BF),
-            pltpu.VMEM((n, r, heads * HD), BF),
-            pltpu.VMEM((n, r, hid), BF),
-            pltpu.VMEM((n, r, hid), BF),
-            pltpu.VMEM((r, d), F32),
-            pltpu.VMEM((n, r, d), BF),
-            pltpu.VMEM((n + 1, r, d), BF),
-            pltpu.VMEM((1, 8, r), F32),
-            dma(2, n),
-            dma(n),
-            dma(n),
-            dma(n),
-            dma(n),
-            dma(n),
-            dma(n),
-            dma(n + 1),
-            dma(1),
-            dma(1),
-        ],
-        10**10,
-        qkv,
-        x,
-        cot,
-        wo,
-        wr,
-    )
 
 
 SLOPE = (2.0 / math.pi) ** 0.5
@@ -487,7 +445,6 @@
     hid = dg_ref.shape[2]
     mine = pl.ds(pl.multiple_of(c * hid, 128), hid)
     theirs = pl.ds(pl.multiple_of((1 - c) * hid, 128), hid)
-    greet(n)
     gather = Gather(full_ref, g_send, g_recv, n)
     full_ref[z] = low_ref[...]
     gather.push(z)
@@ -547,12 +504,37 @@
         dh_copy(k).wait_send()
 
 
-def hidden(lay, low, dg, mid, cot, stat, we):
-    n, r, d, hid = lay.n_row, lay.rows, low.shape[1], dg.shape[2]
+def forward_kernel(
+    lay, qkv_ref, x_ref, cot_ref, wo_ref, wr_any, we_any,
+    o_ref, lse_ref, cb_ref, mid_ref, a2_ref, act_ref, dh_ref, dmid_ref, dy_ref, *scratch
+):
+    dg_ref, low_ref, stat_ref, wr_ref, we_ref, w_load = scratch[:6]
+    loads = [
+        pltpu.make_async_copy(wr_any, wr_ref, w_load.at[0]),
+        pltpu.make_async_copy(we_any, we_ref, w_load.at[1]),
+    ]
+    for each in loads:
+        each.start()
+    middle_kernel(
+        lay, loads, qkv_ref, x_ref, cot_ref, wo_ref, wr_ref, o_ref, lse_ref, cb_ref, dg_ref, mid_ref, low_ref, stat_ref, *scratch[6:27]
+    )
+    hidden_kernel(
+        lay, low_ref, dg_ref, mid_ref, cot_ref, stat_ref, we_ref, a2_ref, act_ref, dh_ref, dmid_ref, dy_ref, *scratch[27:]
+    )
+
+
+def forward(lay, qkv, x, cot, wo, wr, we):
+    n, r, d = lay.n_row, lay.rows, x.shape[1]
+    heads, hid = qkv.shape[2] // (3 * HD), wr.shape[1] // 2
+    keys = n * r
     return call(
-        partial(hidden_kernel, lay),
-        3,
+        partial(forward_kernel, lay),
+        2,
         [
+            ((n, r, 2 * heads * HD), BF),
+            ((n, r, 128), F32),
+            ((n, r, d), BF),
+            ((r, d), F32),
             ((n, r, d), BF),
             ((n, r, hid), BF),
             ((n, r, 2 * hid), BF),
@@ -560,6 +542,33 @@
             ((r, d), BF),
         ],
         [
+            pltpu.VMEM((n, r, hid), F32),
+            pltpu.VMEM((r, d), BF),
+            pltpu.VMEM((1, 8, r), F32),
+            pltpu.VMEM(wr.shape, BF),
+            pltpu.VMEM(we.shape, BF),
+            dma(2),
+            pltpu.VMEM((heads, n, r, HD), BF),
+            pltpu.VMEM((heads, keys, HD), BF),
+            pltpu.VMEM((heads, keys, 2 * HD), BF),
+            pltpu.VMEM((n, r, heads * HD), BF),
+            pltpu.VMEM((n, r, heads * HD), BF),
+            pltpu.VMEM((n, r, hid), BF),
+            pltpu.VMEM((n, r, hid), BF),
+            pltpu.VMEM((r, d), F32),
+            pltpu.VMEM((n, r, d), BF),
+            pltpu.VMEM((n + 1, r, d), BF),
+            pltpu.VMEM((1, 8, r), F32),
+            dma(2, n),
+            dma(n),
+            dma(n),
+            dma(n),
+            dma(n),
+            dma(n),
+            dma(n),
+            dma(n + 1),
+            dma(1),
+            dma(1),
             pltpu.VMEM((n, r, hid), F32),
             pltpu.VMEM((n, r, hid), BF),
             pltpu.VMEM((n, r, hid), BF),
@@ -580,12 +589,13 @@
             dma(1),
         ],
         10**10,
-        low,
-        dg,
-        mid,
+        qkv,
+        x,
         cot,
-        stat,
+        wo,
+        wr,
         we,
+        far=(4, 5),
     )
 
 
@@ -738,12 +748,12 @@
 
 def pull_kernel(
     lay, fused, low_ref, qkv_ref, lse_ref, wo_ref, act_ref, wr_any, mid_ref, a2_ref, dh_ref, o_ref,
-    full_ref, dqkv_ref, g_ref, res_ref, exp_ref, out_ref, square_ref, *scratch
+    dqkv_ref, g_ref, res_ref, exp_ref, out_ref, square_ref, *scratch
 ):
     (
-        q_s, k_s, v_s, do_own, do_out, do_in, do_s, dq_s, dk_s, dv_s, acc, r_out, inbox, turned, wr_ref, a_load, w_load,
+        q_s, k_s, v_s, do_own, do_out, do_in, do_s, dq_s, dk_s, dv_s, acc, r_out, inbox, turned, wr_ref, full_ref, a_load, w_load,
         g_send, g_recv, s_send, s_recv, a_send, a_recv, r_send, r_recv,
-    ) = scratch[:25]
+    ) = scratch[:26]
     n, img, txt, far = lay.n_row, lay.img, lay.txt_pad, lay.n_row * lay.img
     z, c = lax.axis_index("row"), lax.axis_index("col")
     heads, half, hid = q_s.shape[0], do_own.shape[2], act_ref.shape[2]
@@ -759,7 +769,7 @@
     reduce = Reduce(acc, r_out, inbox, r_send, r_recv, n)
     local, local_out = exp_ref, out_ref
     if fused:
-        batch, batch_out = batch_of(scratch[25:33]), batch_of(scratch[33:41])
+        batch, batch_out = batch_of(scratch[26:34]), batch_of(scratch[34:42])
         local, local_out = batch.local, batch_out.local
     split_heads(lay, qkv_ref, q_s, k_s, v_s, False)
     bias = text_bias(lay)
@@ -913,7 +923,6 @@
         partial(pull_kernel, lay, fused),
         4,
         [
-            ((n, r, d), BF),
             ((n, r, 3 * heads * HD), BF),
             ((n, r, 2 * hid), BF),
             ((r, d), BF),
@@ -936,6 +945,7 @@
             pltpu.VMEM((n + 1, r, d), BF),
             pltpu.VMEM((d, keys), BF),
             pltpu.VMEM(wr.shape, BF),
+            pltpu.VMEM((n, r, d), BF),
             dma(n),
             dma(1),
             dma(2, n),
@@ -964,25 +974,27 @@
 
 
 def input_kernel(
-    lay, fused, dqkv_ref, x_ref, dmid_ref, stat_ref, wa_ref, a1_ref, g_ref, cb_ref, square_ref,
+    lay, fused, dqkv_ref, x_ref, dmid_ref, stat_ref, wa_any, a1_ref, g_ref, cb_ref, square_ref,
     dx_ref, att_ref, red_ref, norm_ref, *scratch
 ):
     (
-        full, into, acc, r_out, inbox, stat_out, stat_in, turned, turned_g,
+        full, into, acc, r_out, inbox, stat_out, stat_in, turned, turned_g, wa_ref, w_load,
         s_send, s_recv, r_send, r_recv, t_send, t_recv,
-    ) = scratch[:15]
+    ) = scratch[:17]
     n = lay.n_row
     z, c = lax.axis_index("row"), lax.axis_index("col")
     half, d = dqkv_ref.shape[2], x_ref.shape[1]
     more = ()
     if fused:
-        norm = Norm(4, n, *scratch[39:])
+        norm = Norm(4, n, *scratch[41:])
         more = norm.where()
+    load = pltpu.make_async_copy(wa_any, wa_ref, w_load.at[0])
+    load.start()
     greet(n, False, more)
     swap = Swap(dqkv_ref, into, s_send, s_recv)
     reduce = Reduce(acc, r_out, inbox, r_send, r_recv, n)
-    own, other, red = (scratch[15 + 8 * i : 23 + 8 * i] for i in range(3)) if fused else (
-        scratch[15:16], scratch[16:17], (red_ref,)
+    own, other, red = (scratch[17 + 8 * i : 25 + 8 * i] for i in range(3)) if fused else (
+        scratch[17:18], scratch[18:19], (red_ref,)
     )
     sums = [batch_of(s) for s in (own, other, red)] if fused else []
 
@@ -1007,11 +1019,13 @@
     if fused:
         sums[0].start()
     transpose_rows(lay, g_ref, turned_g)
+    if fused:
+        sums[0].pass_on()
     gradient(turned_g, cb_ref, red[0], STRIPE // 2)
     if fused:
         sums[2].start()
-        sums[0].pass_on()
     lag = jnp.minimum(z, n - 1 - z)
+    load.wait()
 
     @pl.loop(0, n + (n - 1) // 2)
     def _(j):
@@ -1027,6 +1041,14 @@
             )
             for part, rows in parts_of(lay):
                 acc[rows] = dot_nt(full[rows], wa_ref[part])
+
+            @pl.when(i == n - 1)
+            def _():
+                gradient(turned, into, other[0], half)
+                if fused:
+                    sums[1].start()
+                    sums[1].pass_on()
+
             reduce.add(k)
 
         if fused:
@@ -1035,9 +1057,6 @@
             def _():
                 sums[2].pass_on()
 
-    gradient(turned, into, other[0], half)
-    if fused:
-        sums[1].start()
     mean, inverse = moments(stat_ref)
     normed = (x_ref[...].astype(F32) - mean) * inverse
     grad = acc[...]
@@ -1046,7 +1065,6 @@
     back_one, back_two = columns(stat_out)
     dx_ref[...] = dmid_ref[...] + inverse * (grad - back_one - normed * back_two)
     if fused:
-        sums[1].pass_on()
         red_ref[...] = sums[2].total()
         mine, theirs = sums[0].total(), sums[1].total()
     else:
@@ -1085,6 +1103,8 @@
             pltpu.VMEM((1, 8, r), F32),
             pltpu.VMEM((d, keys), BF),
             pltpu.VMEM((g.shape[2], keys), BF),
+            pltpu.VMEM(wa.shape, BF),
+            dma(1),
             dma(n),
             dma(n),
             dma(n),
@@ -1112,6 +1132,7 @@
         g,
         cb,
         square,
+        far=(4,),
     )
 
 
@@ -1250,13 +1271,10 @@
     fused = n_batch == 4
 
     a1_all, qkv, stat_one = attend(lay, low_x, w_attend)
-    o_all, lse, cb_all, dg, middle_x, low_two, stat_two = middle(
-        lay, qkv, low_x, low_cot, w_output, w_reduce
-    )
-    a2_all, act, dh_all, grad_mid, low_mid = hidden(
-        lay, low_two, dg, middle_x, low_cot, stat_two, w_expand
-    )
-    _, dqkv, g_all, result, g_exp, g_out, square = pull(
+    o_all, lse, cb_all, middle_x, a2_all, act, dh_all, grad_mid, low_mid = forward(
+        lay, qkv, low_x, low_cot, w_output, w_reduce, w_expand
+    )
+    dqkv, g_all, result, g_exp, g_out, square = pull(
         lay, fused, low_mid, qkv, lse, w_output, act, w_reduce, middle_x, a2_all, dh_all, o_all
     )
     grad_in, g_att, g_red, norm = inputs_back(

time: 409 us -> 393 us (0.961)
  Pallas kernels: 396 us -> 380 us
    pallas_call x5 -> x4, Pallas kernels: 376 us -> 360 us  [call(): pl.pallas_call(kernel, out_shape=[jax.ShapeDtypeStruct(s, t) for s, t in...]
where the time goes in v5:
time: 393 us
  Pallas kernels  380 us (97%)
  local copies, waits for them, and re-layouts  8.25 us (2%)
    pallas_call x4, Pallas kernels, call(): pl.pallas_call(kernel, out_shape=[jax.ShapeDtypeStruct(s, t) for s, t in...  360 us
    pallas_call x1, Pallas kernels, update(): pl.pallas_call(update_kernel, out_shape=[jax.ShapeDtypeStruct(s, F32) for...  20 us

profile of v5, /device:TPU:0, one launch (start us, length us, event | category | flops | bytes accessed | tf_op | source)
XLA Modules:
  0.0 393.1 jit_solution(9791042905015245462)
XLA Ops:
  0.7 0.1 pad.5.clone
  0.7 1.9 maximum_maximum_fusion.x_ref
  2.7 0.0 copy-start.2
  2.7 0.0 copy-start
  2.7 0.0 copy-start.1
  2.7 50.4 %shard_map.328 = (bf16[4,304,768]{2,1,0:T(8,128)(2,1)}, bf16[4,304,576]{2,1,0:T(8,128)(2,1)}, f32[1,8,304]{2,1,0:T(8,128)}) custom-call(bf16[304,768]{1,0:T(8,128)(2,1)} %maximum_maximum_fusion.x_ref, bf16[2,768,1152]{2,1,0:T(8,128)(2,1)} %refs_12_.1), custom_call_target="tpu_custom_call" | custom-call | flops 2151677952 | bytes 10000000 | tf_op jit(solution)/shard_map/pallas_call | solution.py:228
  53.1 0.0 copy-done.2
  53.2 0.6 compare_reduce_fusion
  54.4 0.0 copy-done
  54.5 0.0 copy-done.1
  54.5 0.9 multiply_convert_fusion.cot_ref
  55.4 164.2 %shard_map.329 = (bf16[4,304,384]{2,1,0:T(8,128)(2,1)}, f32[4,304,128]{2,1,0:T(8,128)}, bf16[4,304,768]{2,1,0:T(8,128)(2,1)}, f32[304,768]{1,0:T(8,128)}, bf16[4...) custom-call(bf16[4,304,576]{2,1,0:T(8,128)(2,1)} %get-tuple-element., ...), custom_call_target="tpu_custom_call" | custom-call | flops 10000000000 | bytes 10000000 | tf_op jit(solution)/shard_map/pallas_call | solution.py:228
  219.6 72.6 %shard_map.330 = (bf16[4,304,576]{2,1,0:T(8,128)(2,1)}, bf16[4,304,1536]{2,1,0:T(8,128)(2,1)}, bf16[304,768]{1,0:T(8,128)(2,1)}, f32[2,192,1536]{2,1,0:T(8,128)}...) custom-call(bf16[304,768]{1,0:T(8,128)(2,1)} %get-tuple-element.60.low_ref, bf16[4,304,576]{2,1,0:T(8,128)(2,1)} %get-tuple-element.59.qkv_ref, ...), custom_call_target="tpu_custom_call" | custom-call | flops 10000000000 | bytes 10000000 | tf_op jit(solution)/shard_map/pallas_call | solution.py:228
  292.2 1.8 slice_bitcast_fusion.1
  294.0 1.5 slice_bitcast_fusion.3
  295.5 72.7 %shard_map.331 = (f32[304,768]{1,0:T(8,128)}, f32[2,192,1152]{2,1,0:T(8,128)}, f32[2,384,768]{2,1,0:T(8,128)}, f32[8,128]{1,0:T(8,128)}) custom-call(bf16[4,304,576]{2,1,0:T(8,128)(2,1)} %get-tuple-element.68.dqkv_ref, bf16[304,768]{1,0:T(8,128)(2,1)} %maximum_maximum_fusion.x_ref, f32[304,768]{1,0:T(8,128)} %get-tuple-element.69.dmid_ref, ...), custom_call_target="tpu_custom_call" | custom-call | flops 10000000000 | bytes 10000000 | tf_op jit(solution)/shard_map/pallas_call | solution.py:228
  368.2 2.1 slice_bitcast_fusion
  370.2 0.9 slice_bitcast_fusion.2
  371.1 0.8 copy.38
  371.9 20.0 %shard_map.332 = (f32[2,192,1152]{2,1,0:T(8,128)}, f32[2,96,768]{2,1,0:T(8,128)}, f32[2,192,1536]{2,1,0:T(8,128)}, f32[2,384,768]{2,1,0:T(8,128)}, f32[2,192,115...) custom-call(f32[8,128]{1,0:T(8,128)} %get-tuple-element.76.norm_ref,, ...), custom_call_target="tpu_custom_call" | custom-call | flops 100000000 | bytes 50000000 | tf_op jit(solution)/shard_map/pallas_call | solution.py:1209
  391.9 1.2 slice.19
  (1 shorter events, 0.0 us)
Async XLA Ops:
  2.7 50.5 %copy-start.2 = (s32[3]{0:T(128)S(1)}, s32[3]{0:T(128)}, u32[]{:S(2)}) copy-start(s32[3]{0:T(128)} %param.21) | copy-start | bytes 40
  2.7 51.8 %copy-start = (bf16[1,256,768]{2,1,0:T(8,128)(2,1)S(1)}, bf16[1,256,768]{2,1,0:T(8,128)(2,1)}, u32[]{:S(2)}) copy-start(bf16[1,256,768]{2,1,0:T(8,128)(2,1)} %param.19) | copy-start | bytes 1179652
  2.7 51.8 %copy-start.1 = (bf16[1,38,768]{2,1,0:T(8,128)(2,1)S(1)}, bf16[1,38,768]{2,1,0:T(8,128)(2,1)}, u32[]{:S(2)}) copy-start(bf16[1,38,768]{2,1,0:T(8,128)(2,1)} %param.20) | copy-start | bytes 175108

commit v6 on v5

--- a/solution.py
+++ b/solution.py
@@ -374,8 +374,7 @@
             acc[rows] = dot(o_ref[k, rows], wo_ref[part])
         reduce.add(k)
 
-    @pl.loop(0, n)
-    def _(j):
+    def step(j):
         k = near_first(z, n, n - 1 - j)
         attention(k)
         swap_o.start(k)
@@ -397,11 +396,20 @@
                 cb_ref[near, rows], wr_ref[part, pl.ds(pl.multiple_of(c * hid, 128), hid), :]
             )
 
-        @pl.when(j > 0)
-        def _():
-            project(near_first(z, n, n - j))
-
-    project(near_first(z, n, 0))
+    lag = 1 + jnp.minimum(z, n - 1 - z)
+
+    @pl.loop(0, n + 1 + (n - 1) // 2)
+    def _(j):
+        @pl.when(j < n)
+        def _():
+            step(j)
+
+        i = j - lag
+
+        @pl.when((i >= 0) & (i < n))
+        def _():
+            project(near_first(z, n, n - 1 - i))
+
     mid = x_ref[...].astype(F32) + acc[...]
     mid_ref[...] = mid
     stat_ref[0] = sums_of(mid, mid * mid)
@@ -409,16 +417,19 @@
     mean, inverse = moments(stat_ref)
     low_ref[...] = ((mid - mean) * inverse).astype(BF)
 
-    @pl.loop(0, n)
-    def _(j):
-        k = near_first(z, n, j)
-        swap_d.arrive(k)
-        dg_ref[k] += dg_in[k].astype(F32)
-
-    gather.finish()
-    swap_o.finish(n)
-    swap_d.finish(n)
-    reduce.finish()
+    def settle():
+        @pl.loop(0, n)
+        def _(j):
+            k = near_first(z, n, j)
+            swap_d.arrive(k)
+            dg_ref[k] += dg_in[k].astype(F32)
+
+        gather.finish()
+        swap_o.finish(n)
+        swap_d.finish(n)
+        reduce.finish()
+
+    return settle
 
 
 SLOPE = (2.0 / math.pi) ** 0.5
@@ -434,7 +445,7 @@
 
 
 def hidden_kernel(
-    lay, low_ref, dg_ref, mid_ref, cot_ref, stat_ref, we_ref, full_ref, act_ref, dh_ref, dmid_ref, dy_ref, *scratch
+    lay, settle, low_ref, dg_ref, mid_ref, cot_ref, stat_ref, we_ref, full_ref, act_ref, dh_ref, dmid_ref, dy_ref, *scratch
 ):
     (
         own, out, into, acc, r_out, inbox, stat_out, stat_in,
@@ -472,20 +483,23 @@
             acc[rows] = dot_nt(dh_ref[k, rows], we_ref[part])
         reduce.add(k)
 
-    @pl.loop(0, n)
+    settle()
+
+    @pl.loop(0, n + 2)
     def _(j):
-        k = near_first(z, n, n - 1 - j)
-        swap.arrive(k)
-        act, slope = gelu_pair(own[k] + into[k].astype(F32))
-        act_ref[k] = act.astype(BF)
-        dh_ref[k, :, mine] = (dg_ref[k] * slope).astype(BF)
-        dh_copy(k).start()
-
-        @pl.when(j > 0)
-        def _():
-            back(near_first(z, n, n - j))
-
-    back(near_first(z, n, 0))
+        @pl.when(j < n)
+        def _():
+            k = near_first(z, n, n - 1 - j)
+            swap.arrive(k)
+            act, slope = gelu_pair(own[k] + into[k].astype(F32))
+            act_ref[k] = act.astype(BF)
+            dh_ref[k, :, mine] = (dg_ref[k] * slope).astype(BF)
+            dh_copy(k).start()
+
+        @pl.when(j > 1)
+        def _():
+            back(near_first(z, n, n + 1 - j))
+
     mean, inverse = moments(stat_ref)
     normed = (mid_ref[...] - mean) * inverse
     grad = acc[...]
@@ -515,11 +529,11 @@
     ]
     for each in loads:
         each.start()
-    middle_kernel(
+    settle = middle_kernel(
         lay, loads, qkv_ref, x_ref, cot_ref, wo_ref, wr_ref, o_ref, lse_ref, cb_ref, dg_ref, mid_ref, low_ref, stat_ref, *scratch[6:27]
     )
     hidden_kernel(
-        lay, low_ref, dg_ref, mid_ref, cot_ref, stat_ref, we_ref, a2_ref, act_ref, dh_ref, dmid_ref, dy_ref, *scratch[27:]
+        lay, settle, low_ref, dg_ref, mid_ref, cot_ref, stat_ref, we_ref, a2_ref, act_ref, dh_ref, dmid_ref, dy_ref, *scratch[27:]
     )
 
 
@@ -1148,11 +1162,12 @@
     return (moment_new, square_new, -RATE * (corrected + DECAY * weight))
 
 
-def update_kernel(norm_ref, *refs):
+def update_kernel(lay, norm_ref, res_ref, dx_ref, *refs):
     grads, moments_in, squares_in, weights = refs[0:4], refs[4:8], refs[8:12], refs[12:16]
     m_out, v_out, s_out, g_out = refs[16:20], refs[20:24], refs[24:28], refs[28:32]
-    g_s, m_s, v_s, w_s, t_s = (refs[32 + 4 * i : 36 + 4 * i] for i in range(5))
-    load, store = refs[52:]
+    image_ref, image_grad_ref, text_grad_ref, one_ref = refs[32:36]
+    g_s, m_s, v_s, w_s, t_s = (refs[36 + 4 * i : 40 + 4 * i] for i in range(5))
+    load, store = refs[56:]
     b = lax.axis_index("batch")
     loads = []
     for i in range(4):
@@ -1170,6 +1185,10 @@
                 loads.append(pltpu.make_async_copy(src, dst.at[m], load.at[i, m, q]))
                 loads[-1].start()
     clip = jnp.minimum(1.0, 1.0 / (norm_ref[0:1, 0:1] + 1e-06))
+    image_ref[...] = res_ref[: lay.img]
+    image_grad_ref[...] = dx_ref[: lay.img]
+    text_grad_ref[...] = dx_ref[lay.img : lay.real]
+    one_ref[...] = norm_ref[0:1, 0:1]
     stores = []
     for i in range(4):
         for m in range(2):
@@ -1204,13 +1223,20 @@
 TILE = 16
 
 
-def update(norm, grads, ms, vs, ws):
+def update(lay, norm, res, dx, grads, ms, vs, ws):
+    d = dx.shape[1]
     shapes = [g.shape for g in grads]
     outs = pl.pallas_call(
-        update_kernel,
-        out_shape=[jax.ShapeDtypeStruct(s, F32) for _ in range(4) for s in shapes],
-        in_specs=[VMEM] + [ANY] * 16,
-        out_specs=[ANY] * 16,
+        partial(update_kernel, lay),
+        out_shape=[jax.ShapeDtypeStruct(s, F32) for _ in range(4) for s in shapes]
+        + [
+            jax.ShapeDtypeStruct((lay.img, d), BF),
+            jax.ShapeDtypeStruct((lay.img, d), F32),
+            jax.ShapeDtypeStruct((lay.txt, d), F32),
+            jax.ShapeDtypeStruct((1, 1), F32),
+        ],
+        in_specs=[VMEM] * 3 + [ANY] * 16,
+        out_specs=[ANY] * 16 + [VMEM] * 4,
         scratch_shapes=[
             *[pltpu.VMEM(s, t) for t in (F32, F32, F32, BF, F32) for s in shapes],
             dma(4, 2, 4),
@@ -1218,8 +1244,8 @@
         ],
         compiler_params=pltpu.CompilerParams(vmem_limit_bytes=60 * 2**20),
         cost_estimate=pl.CostEstimate(flops=10**8, bytes_accessed=5 * 10**7, transcendentals=0),
-    )(norm, *grads, *ms, *vs, *ws)
-    return outs[0:4], outs[4:8], outs[8:12], outs[12:16]
+    )(norm, res, dx, *grads, *ms, *vs, *ws)
+    return outs[0:4], outs[4:8], outs[8:12], outs[12:16], outs[16:]
 
 
 def weight_shard(weight, group_index, shard_rows):
@@ -1289,9 +1315,12 @@
     vs = (v_attend, v_output, v_expand, v_reduce)
     ws = (w_attend, w_output, w_expand, w_reduce)
     if fused:
-        grad_norm = norm[0, 0]
-        new_m, new_v, steps, sums = update(norm, sums, ms, vs, ws)
+        new_m, new_v, steps, sums, (image, image_grad, text_grad, one) = update(
+            lay, norm, result, grad_in, sums, ms, vs, ws
+        )
+        grad_norm = one.reshape(())
     else:
+        image, image_grad, text_grad = result[:img], grad_in[:img], grad_in[img : lay.real]
         squares = sum(jnp.sum(g * g) for g in sums)
         grad_norm = jnp.sqrt(lax.psum(lax.psum(lax.psum(squares, "batch"), "row"), "col"))
         clip_factor = jnp.minimum(1.0, 1.0 / (grad_norm + 1e-06))
@@ -1302,10 +1331,10 @@
             ]
         )
     return (
-        result[:img][None],
+        image[None],
         result[img : lay.real][None],
-        grad_in[:img][None],
-        grad_in[img : lay.real][None],
+        image_grad[None],
+        text_grad[None],
         *sums,
         *new_m,
         *new_v,

time: 393 us -> 385 us (0.980)
  local copies, waits for them, and re-layouts: 8.25 us -> 3.22 us
  Pallas kernels: 380 us -> 376 us
    pallas_call x4, Pallas kernels: 360 us -> 354 us  [call(): pl.pallas_call(kernel, out_shape=[jax.ShapeDtypeStruct(s, t) for s, t in...]
    broadcast_in_dim x3 -> x0, local copies, waits for them, and re-layouts: 4.74 us -> none  [the longest x1 2.06 us: on_device(): grad_in[:img][None]]
where the time goes in v6:
time: 385 us; the launch traced here: 384 us
  Pallas kernels  376 us (98%)
    pallas_call x4, Pallas kernels, call(): pl.pallas_call(kernel, out_shape=[jax.ShapeDtypeStruct(s, t) for s, t in...  354 us
    pallas_call x1, Pallas kernels, update(): pl.pallas_call(partial(update_kernel, lay), out_shape=[jax.ShapeDtypeStru...  22 us

profile of v6, /device:TPU:0, one launch (start us, length us, event | category | flops | bytes accessed | tf_op | source)
XLA Modules:
  0.0 384.3 jit_solution(7268892362850903672)
XLA Ops:
  0.7 0.1 pad.5.clone
  0.7 1.9 maximum_maximum_fusion.x_ref
  2.7 0.0 copy-start.2
  2.7 0.0 copy-start
  2.7 0.0 copy-start.1
  2.7 50.4 %shard_map.328 = (bf16[4,304,768]{2,1,0:T(8,128)(2,1)}, bf16[4,304,576]{2,1,0:T(8,128)(2,1)}, f32[1,8,304]{2,1,0:T(8,128)}) custom-call(bf16[304,768]{1,0:T(8,128)(2,1)} %maximum_maximum_fusion.x_ref, bf16[2,768,1152]{2,1,0:T(8,128)(2,1)} %refs_12_.1), custom_call_target="tpu_custom_call" | custom-call | flops 2151677952 | bytes 10000000 | tf_op jit(solution)/shard_map/pallas_call | solution.py:228
  53.1 0.0 copy-done.2
  53.2 0.6 compare_reduce_fusion
  54.4 0.0 copy-done
  54.5 0.0 copy-done.1
  54.5 0.9 multiply_convert_fusion.cot_ref
  55.4 156.3 %shard_map.329 = (bf16[4,304,384]{2,1,0:T(8,128)(2,1)}, f32[4,304,128]{2,1,0:T(8,128)}, bf16[4,304,768]{2,1,0:T(8,128)(2,1)}, f32[304,768]{1,0:T(8,128)}, bf16[4...) custom-call(bf16[4,304,576]{2,1,0:T(8,128)(2,1)} %get-tuple-element., ...), custom_call_target="tpu_custom_call" | custom-call | flops 10000000000 | bytes 10000000 | tf_op jit(solution)/shard_map/pallas_call | solution.py:228
  211.7 74.8 %shard_map.330 = (bf16[4,304,576]{2,1,0:T(8,128)(2,1)}, bf16[4,304,1536]{2,1,0:T(8,128)(2,1)}, bf16[304,768]{1,0:T(8,128)(2,1)}, f32[2,192,1536]{2,1,0:T(8,128)}...) custom-call(bf16[304,768]{1,0:T(8,128)(2,1)} %get-tuple-element.64.low_ref, bf16[4,304,576]{2,1,0:T(8,128)(2,1)} %get-tuple-element.63.qkv_ref, ...), custom_call_target="tpu_custom_call" | custom-call | flops 10000000000 | bytes 10000000 | tf_op jit(solution)/shard_map/pallas_call | solution.py:228
  286.5 72.7 %shard_map.331 = (f32[304,768]{1,0:T(8,128)}, f32[2,192,1152]{2,1,0:T(8,128)}, f32[2,384,768]{2,1,0:T(8,128)}, f32[8,128]{1,0:T(8,128)}) custom-call(bf16[4,304,576]{2,1,0:T(8,128)(2,1)} %get-tuple-element.71.dqkv_ref, bf16[304,768]{1,0:T(8,128)(2,1)} %maximum_maximum_fusion.x_ref, f32[304,768]{1,0:T(8,128)} %get-tuple-element.72.dmid_ref, ...), custom_call_target="tpu_custom_call" | custom-call | flops 10000000000 | bytes 10000000 | tf_op jit(solution)/shard_map/pallas_call | solution.py:228
  359.2 22.0 %shard_map.332 = (f32[2,192,1152]{2,1,0:T(8,128)}, f32[2,96,768]{2,1,0:T(8,128)}, f32[2,192,1536]{2,1,0:T(8,128)}, f32[2,384,768]{2,1,0:T(8,128)}, f32[2,192,115...) custom-call(f32[8,128]{1,0:T(8,128)} %get-tuple-element.78.norm_ref,, ...), custom_call_target="tpu_custom_call" | custom-call | flops 100000000 | bytes 50000000 | tf_op jit(solution)/shard_map/pallas_call | solution.py:1229
  381.1 1.7 copy.38
  382.8 1.5 slice_bitcast_fusion
  (1 shorter events, 0.0 us)
Async XLA Ops:
  2.7 50.5 %copy-start.2 = (s32[3]{0:T(128)S(1)}, s32[3]{0:T(128)}, u32[]{:S(2)}) copy-start(s32[3]{0:T(128)} %param.21) | copy-start | bytes 40
  2.7 51.8 %copy-start = (bf16[1,256,768]{2,1,0:T(8,128)(2,1)S(1)}, bf16[1,256,768]{2,1,0:T(8,128)(2,1)}, u32[]{:S(2)}) copy-start(bf16[1,256,768]{2,1,0:T(8,128)(2,1)} %param.19) | copy-start | bytes 1179652
  2.7 51.8 %copy-start.1 = (bf16[1,38,768]{2,1,0:T(8,128)(2,1)S(1)}, bf16[1,38,768]{2,1,0:T(8,128)(2,1)}, u32[]{:S(2)}) copy-start(bf16[1,38,768]{2,1,0:T(8,128)(2,1)} %param.20) | copy-start | bytes 175108

commit v7 on v6

--- a/solution.py
+++ b/solution.py
@@ -58,6 +58,10 @@
     return jnp.where(j <= 2 * reach, alternate, beyond)
 
 
+LOADS = []
+STORES = []
+
+
 def greet(n, fused=False, more=()):
     z, c = lax.axis_index("row"), lax.axis_index("col")
     barrier = pltpu.get_barrier_semaphore()
@@ -79,6 +83,8 @@
     for where in more:
         pl.semaphore_signal(barrier, inc=1, device_id=where, device_id_type=MESH)
     pl.semaphore_wait(barrier, ends + (3 if fused else 1) + len(more))
+    for each in LOADS:
+        each.wait()
 
 
 class Gather:
@@ -224,13 +230,40 @@
     return pltpu.SemaphoreType.DMA(shape)
 
 
-def call(kernel, ident, outs, scratch, cost, *operands, far=()):
+def call(kernel, ident, outs, scratch, cost, *operands, far=(), early=0):
+    large = [i for i, o in enumerate(operands) if i not in far and o.size > 2**15]
+    count = len(operands)
+
+    def body(*refs):
+        refs = list(refs)
+        extra = len(large) + early
+        buffers, (load, store) = refs[-extra - 2 : -2], refs[-2:]
+        LOADS.clear()
+        STORES.clear()
+        for q, i in enumerate(large):
+            LOADS.append(pltpu.make_async_copy(refs[i], buffers[q], load.at[q]))
+            LOADS[-1].start()
+            refs[i] = buffers[q]
+        for q in range(early):
+            held = buffers[len(large) + q]
+            STORES.append(pltpu.make_async_copy(held, refs[count + q], store.at[q]))
+            refs[count + q] = held
+        kernel(*refs[: -extra - 2])
+        for each in STORES:
+            each.wait()
+
     return pl.pallas_call(
-        kernel,
+        body,
         out_shape=[jax.ShapeDtypeStruct(s, t) for s, t in outs],
-        in_specs=[ANY if i in far else VMEM for i in range(len(operands))],
-        out_specs=[VMEM] * len(outs),
-        scratch_shapes=scratch,
+        in_specs=[ANY if i in far or i in large else VMEM for i in range(count)],
+        out_specs=[ANY if i < early else VMEM for i in range(len(outs))],
+        scratch_shapes=[
+            *scratch,
+            *[pltpu.VMEM(operands[i].shape, operands[i].dtype) for i in large],
+            *[pltpu.VMEM(*outs[i]) for i in range(early)],
+            dma(len(large)),
+            dma(max(early, 1)),
+        ],
         compiler_params=pltpu.CompilerParams(
             collective_id=ident, has_side_effects=True, vmem_limit_bytes=60 * 2**20
         ),
@@ -484,6 +517,8 @@
         reduce.add(k)
 
     settle()
+    for each in STORES[:5]:
+        each.start()
 
     @pl.loop(0, n + 2)
     def _(j):
@@ -500,6 +535,8 @@
         def _():
             back(near_first(z, n, n + 1 - j))
 
+    for each in STORES[5:]:
+        each.start()
     mean, inverse = moments(stat_ref)
     normed = (mid_ref[...] - mean) * inverse
     grad = acc[...]
@@ -610,6 +647,7 @@
         wr,
         we,
         far=(4, 5),
+        early=7,
     )
 
 

time: 385 us -> 371 us (0.964)
  Pallas kernels: 376 us -> 363 us
    pallas_call x4, Pallas kernels: 354 us -> 341 us  [call(): pl.pallas_call(body, out_shape=[jax.ShapeDtypeStruct(s, t) for s, t in ou...]
where the time goes in v7:
time: 371 us
  Pallas kernels  363 us (98%)
    pallas_call x4, Pallas kernels, call(): pl.pallas_call(body, out_shape=[jax.ShapeDtypeStruct(s, t) for s, t in ou...  341 us
    pallas_call x1, Pallas kernels, update(): pl.pallas_call(partial(update_kernel, lay), out_shape=[jax.ShapeDtypeStru...  22 us

profile of v7, /device:TPU:0, one launch (start us, length us, event | category | flops | bytes accessed | tf_op | source)
XLA Modules:
  0.0 370.8 jit_solution(17663617528172526436)
XLA Ops:
  0.7 0.1 pad.5.clone
  0.7 1.9 maximum_maximum_fusion.refs_0_.refs_1_
  2.7 0.0 copy-start.2
  2.7 0.0 copy-start
  2.7 0.0 copy-start.1
  2.7 49.4 %shard_map.328 = (bf16[4,304,768]{2,1,0:T(8,128)(2,1)}, bf16[4,304,576]{2,1,0:T(8,128)(2,1)}, f32[1,8,304]{2,1,0:T(8,128)}) custom-call(bf16[304,768]{1,0:T(8,128)(2,1)} %maximum_maximum_fusion.refs_0_.refs_1_, bf16[2,768,1152]{2,1,0:T(8,128)(2,1)} %refs_12_.1), custom_call_target="tpu_custom_call" | custom-call | flops 2151677952 | bytes 10000000 | tf_op jit(solution)/shard_map/pallas_call | solution.py:255
  52.1 0.0 copy-done.2
  52.1 0.6 compare_reduce_fusion
  53.4 0.0 copy-done
  53.4 0.0 copy-done.1
  53.4 0.9 multiply_convert_fusion.refs_2_
  54.4 154.5 %shard_map.329 = (bf16[4,304,384]{2,1,0:T(8,128)(2,1)}, f32[4,304,128]{2,1,0:T(8,128)}, bf16[4,304,768]{2,1,0:T(8,128)(2,1)}, f32[304,768]{1,0:T(8,128)}, bf16[4...) custom-call(bf16[4,304,576]{2,1,0:T(8,128)(2,1)} %get-tuple-element., ...), custom_call_target="tpu_custom_call" | custom-call | flops 10000000000 | bytes 10000000 | tf_op jit(solution)/shard_map/pallas_call | solution.py:255
  208.9 68.7 %shard_map.330 = (bf16[4,304,576]{2,1,0:T(8,128)(2,1)}, bf16[4,304,1536]{2,1,0:T(8,128)(2,1)}, bf16[304,768]{1,0:T(8,128)(2,1)}, f32[2,192,1536]{2,1,0:T(8,128)}...) custom-call(bf16[304,768]{1,0:T(8,128)(2,1)} %get-tuple-element.64.refs_0_, ...), custom_call_target="tpu_custom_call" | custom-call | flops 10000000000 | bytes 10000000 | tf_op jit(solution)/shard_map/pallas_call | solution.py:255
  277.6 68.1 %shard_map.331 = (f32[304,768]{1,0:T(8,128)}, f32[2,192,1152]{2,1,0:T(8,128)}, f32[2,384,768]{2,1,0:T(8,128)}, f32[8,128]{1,0:T(8,128)}) custom-call(bf16[4,304,576]{2,1,0:T(8,128)(2,1)} %get-tuple-element.71.refs_0_, bf16[304,768]{1,0:T(8,128)(2,1)} %maximum_maximum_fusion.refs_0_.refs_1_, f32[304,768]{1,0:T(8,128)} %get-tuple-element.72.refs_2_, ...), custom_call_target="tpu_custom_call" | custom-call | flops 10000000000 | bytes 10000000 | tf_op jit(solution)/shard_map/pallas_call | solution.py:255
  345.7 22.0 %shard_map.332 = (f32[2,192,1152]{2,1,0:T(8,128)}, f32[2,96,768]{2,1,0:T(8,128)}, f32[2,192,1536]{2,1,0:T(8,128)}, f32[2,384,768]{2,1,0:T(8,128)}, f32[2,192,115...) custom-call(f32[8,128]{1,0:T(8,128)} %get-tuple-element.78.norm_ref,, ...), custom_call_target="tpu_custom_call" | custom-call | flops 100000000 | bytes 50000000 | tf_op jit(solution)/shard_map/pallas_call | solution.py:1267
  367.7 1.7 copy.38
  369.3 1.5 slice_bitcast_fusion
  (1 shorter events, 0.0 us)
Async XLA Ops:
  2.7 49.4 %copy-start.2 = (s32[3]{0:T(128)S(1)}, s32[3]{0:T(128)}, u32[]{:S(2)}) copy-start(s32[3]{0:T(128)} %param.21) | copy-start | bytes 40
  2.7 50.7 %copy-start = (bf16[1,256,768]{2,1,0:T(8,128)(2,1)S(1)}, bf16[1,256,768]{2,1,0:T(8,128)(2,1)}, u32[]{:S(2)}) copy-start(bf16[1,256,768]{2,1,0:T(8,128)(2,1)} %param.19) | copy-start | bytes 1179652
  2.7 50.7 %copy-start.1 = (bf16[1,38,768]{2,1,0:T(8,128)(2,1)S(1)}, bf16[1,38,768]{2,1,0:T(8,128)(2,1)}, u32[]{:S(2)}) copy-start(bf16[1,38,768]{2,1,0:T(8,128)(2,1)} %param.20) | copy-start | bytes 175108
